TPU v7x, 32 devices: a whole 2x2x4 slice. The times are simulated.
32 devices in a mesh: cuts: 2 (over y), samp: 2 (over core), blk: 4 (over z), tile: 2 (over x).
Axes of the slice: x: 2, y: 2, z: 4, core: 2. Of those that a mesh axis runs over, the one named last changes fastest.
Arguments:
- residual: bfloat16 [2, 4096, 2, 512], P('samp', ('cuts', 'blk', 'tile')), parts along dimension 1, may hold values from -0.25 to 0.25
- uv_offsets: float32 [4096, 2, 512], P(('cuts', 'blk', 'tile')), parts along dimension 0, may hold values from -16 to 16
- counts: int32 [4096], P(('cuts', 'blk', 'tile')), parts along dimension 0, may hold values from 128 to 512
- tile_of_block: int32 [4096, 1], P(('cuts', 'blk', 'tile')), parts along dimension 0, may hold values from 0 to 7; in each aligned block of 256 rows (0 to 255, 256 to 511, ...) at most 64 rows name the same one
- slot_of_block: int32 [4096], P(('cuts', 'blk', 'tile')), parts along dimension 0, may hold values from 0 to 127
- owner_map: int32 [8], replicated, may hold values from 0 to 7, each once
Outputs:
- grid_tiles: float32 [512, 2, 4096], P(('cuts', 'blk', 'tile')), parts along dimension 0
There are 2 independent parts, one for each index of `cuts`. A program takes and returns all parts, laid end to end along the dimension named above; an argument that names none is the same for every part. Nothing has to cross between parts.
Inputs may be any that keep to these rules, and one draw needn't show every extreme that they name: `tile_of_block`: in the rows of one device, no tile is named by more than 64 blocks; some tile is named by exactly 64. `owner_map`: each tile has one owner and each owner one tile.
All inputs are finite; a program needn't handle non-finite values.
Results may differ from a plain program's by a relative error of at most 0.0047.
Values may be sent and summed in bfloat16 or wider, within the bound.
No kernel may reach another device: no remote copies, remote signals or barrier semaphores. Data moves between devices by JAX's collectives and lax.ppermute only.
A program may use at most 64 MiB of HBM per device.

v0:
```python
import jax
import jax.numpy as jnp
from jax import lax
from jax.sharding import PartitionSpec as P

SUB = 32
SLOTS = 128
CAP_MIN = 8


def kernels(resid_piece, uv_piece, count_piece):
    vis_count = resid_piece.shape[-1]
    centre = (jnp.arange(SUB, dtype=jnp.float32) - SUB / 2.0) / SUB
    live_mask = (jnp.arange(vis_count)[None, :] < count_piece[:, None]).astype(jnp.float32)
    phase_rows = 2.0 * jnp.pi * uv_piece[:, 0, :, None] * centre
    phase_cols = 2.0 * jnp.pi * uv_piece[:, 1, :, None] * centre
    real_part = resid_piece[:, 0, :, None].astype(jnp.float32) * live_mask[..., None]
    imag_part = resid_piece[:, 1, :, None].astype(jnp.float32) * live_mask[..., None]
    left_real = real_part * jnp.cos(phase_rows) - imag_part * jnp.sin(phase_rows)
    left_imag = real_part * jnp.sin(phase_rows) + imag_part * jnp.cos(phase_rows)
    left_kernel = jnp.concatenate([left_real, left_imag], -1).astype(jnp.bfloat16)
    right_kernel = jnp.concatenate([jnp.cos(phase_cols), jnp.sin(phase_cols)], -1).astype(
        jnp.bfloat16
    )
    return (left_kernel, right_kernel)


def combine(products):
    sum_real = products[:, :SUB, :SUB] - products[:, SUB:, SUB:]
    sum_imag = products[:, :SUB, SUB:] + products[:, SUB:, :SUB]
    stacked = jnp.stack([sum_real, sum_imag], 2).astype(jnp.bfloat16)
    return stacked.reshape(products.shape[0], 2 * SUB * SUB)


def make_subgrids(pieces):
    resid_piece, uv_piece, count_piece = pieces
    left_kernel, right_kernel = kernels(resid_piece, uv_piece, count_piece)
    products = jnp.einsum(
        "bkp,bkq->bpq", left_kernel, right_kernel, preferred_element_type=jnp.float32
    )
    return combine(products)


def local(residual, uv_offsets, counts, tile_of_block, slot_of_block, owner_map):
    blocks = uv_offsets.shape[0]
    owners = owner_map.shape[0]
    capacity = max(CAP_MIN, 2 * blocks // owners)
    feature = 2 * SUB * SUB
    per_turn = min(blocks, 32)
    turns = blocks // per_turn
    subgrid = lax.map(
        make_subgrids,
        (
            residual[0].reshape((turns, per_turn) + residual.shape[2:]),
            uv_offsets.reshape((turns, per_turn) + uv_offsets.shape[1:]),
            counts.reshape(turns, per_turn),
        ),
    )
    subgrid = subgrid.reshape(blocks, feature)
    tile_ids = tile_of_block[:, 0]
    owner_range = jnp.arange(owners, dtype=jnp.int32)
    owner_ids = jnp.sum(
        jnp.where(tile_ids[:, None] == owner_range[None, :], owner_map[None, :], 0), 1
    )
    same_owner = (owner_ids[:, None] == owner_range[None, :]).astype(jnp.int32)
    earlier = jnp.sum((jnp.cumsum(same_owner, 0) - same_owner) * same_owner, 1)
    target = owner_ids * capacity + earlier
    wanted = jnp.arange(owners * capacity, dtype=jnp.int32)
    matches = target[None, :] == wanted[:, None]
    source = jnp.sum(jnp.where(matches, jnp.arange(blocks, dtype=jnp.int32)[None, :], 0), 1)
    filled = jnp.any(matches, 1)
    outgoing = (subgrid[source] * filled[:, None].astype(jnp.bfloat16)).reshape(
        owners, capacity, feature
    )
    out_slots = jnp.where(filled, slot_of_block[source], SLOTS).reshape(owners, capacity)
    arrived, arrived_slots = (
        lax.all_to_all(outgoing, ("blk", "tile"), split_axis=0, concat_axis=0, tiled=True),
        lax.all_to_all(out_slots, ("blk", "tile"), split_axis=0, concat_axis=0, tiled=True),
    )
    arrived = arrived.reshape(owners * capacity, feature)
    slot_hot = (
        arrived_slots.reshape(-1)[:, None] == jnp.arange(SLOTS, dtype=jnp.int32)[None, :]
    ).astype(jnp.bfloat16)
    tile_sum = lax.dot_general(
        slot_hot, arrived, (((0,), (0,)), ((), ())), preferred_element_type=jnp.float32
    )
    tile_grid = (
        tile_sum.reshape(SLOTS, SUB, 2, SUB).transpose(1, 2, 0, 3).reshape(SUB, 2, SLOTS * SUB)
    )
    summed = lax.psum(tile_grid, "samp")
    return summed


def solution(mesh):
    in_specs = (
        P("samp", ("cuts", "blk", "tile"), None, None),
        P(("cuts", "blk", "tile"), None, None),
        P(("cuts", "blk", "tile")),
        P(("cuts", "blk", "tile"), None),
        P(("cuts", "blk", "tile")),
        P(),
    )
    out_specs = P(("cuts", "blk", "tile"), None, None)
    return jax.shard_map(local, mesh=mesh, in_specs=in_specs, out_specs=out_specs, check_vma=False)
```

profile of v0, /device:TPU:0, one launch (start us, length us, event | category | flops | bytes accessed | tf_op | source)
XLA Modules:
  0.0 278.7 jit_solution(472015044193634381)
XLA Ops:
  6.5 0.8 select_reduce_fusion.1
  8.6 3.5 %gather_fusion = s32[512]{0:T(512)S(1)} fusion(s32[256]{0:T(256)S(1)} %copy-done, s32[1024]{0:T(1024)S(1)} %pad_clamp_fusion), kind=kCustom, calls=%fused_computation | custom fusion | bytes 6144 | tf_op jit(solution)/shard_map/gather | solution.py:75
  12.2 0.7 select_n.38
  12.9 7.3 %all-to-all-start = ((s32[8,1,64]{2,1,0:T(1,128)}), s32[8,1,64]{2,1,0:T(1,128)S(1)}, u32[]{:S(2)}, u32[]{:S(2)}) async-start(s32[8,1,64]{2,1,0:T(1,128)} %select_n.38), calls=%async_computation | async-start | bytes 8192 | tf_op jit(solution)/shard_map/all_to_all | solution.py:78
  20.2 160.1 %while.12 = (s32[]{:T(128)}, bf16[8,32,2048]{2,1,0:T(8,128)(2,1)S(1)}, s32[8,32]{1,0:T(8,128)S(1)}, bf16[8,32,2,512]{3,2,1,0:T(2,128)(2,1)}, f32[8,32,2,512]{3,2,1,0:T(2,128)}, /*index=5*/s32[]{:T(128)}) while((s32[]{:T(128)}, bf16[8,32,2048]{2,1,0:T(8,128)(2,1)S(1)}, s32[8,32]{1,0:T(8,128)S(1)}, bf16[8,32,2,512]{3,2,1,0:T(2,128)(2,1)}, ...), condition=%wide.region_7.8_spmd, body=%wide.region_6.7_spmd.sunk | while | flops 149209152 | bytes 12124893 | solution.py:51
  20.2 0.9 constant_dynamic-slice_fusion.5
  21.2 0.9 constant_dynamic-slice_fusion.6
  22.2 15.5 %fusion.44 = (bf16[32,512,32]{1,2,0:T(8,128)(2,1)S(1)}, bf16[32,512,32]{1,2,0:T(8,128)(2,1)S(1)}, bf16[32,512,32]{1,2,0:T(8,128)(2,1)S(1)}, bf16[32,512,32]{1,2,0:T(8,128)(2,1)S(1)}) fusion(f32[32,512]{1,0:T(8,128)S(1)} %get-tuple-element.144, f32[32]{0:T(128)S(1)} %add_multiply_fusion.2, f32[32,512]{1,0:T(8,128)S(1)} %get-tuple-element.145, ...), kind=kLoop, calls=%fused_computation.14.clone.1 | loop fusion | flops 6291456 | bytes 4456576 | tf_op jit(solution)/shard_map/convert.6
  37.7 0.9 fusion.45
  40.2 0.9 constant_dynamic-slice_fusion.5
  41.2 0.9 constant_dynamic-slice_fusion.6
  42.2 15.5 %fusion.44 = (bf16[32,512,32]{1,2,0:T(8,128)(2,1)S(1)}, bf16[32,512,32]{1,2,0:T(8,128)(2,1)S(1)}, bf16[32,512,32]{1,2,0:T(8,128)(2,1)S(1)}, bf16[32,512,32]{1,2,0:T(8,128)(2,1)S(1)}) fusion(f32[32,512]{1,0:T(8,128)S(1)} %get-tuple-element.144, f32[32]{0:T(128)S(1)} %add_multiply_fusion.2, f32[32,512]{1,0:T(8,128)S(1)} %get-tuple-element.145, ...), kind=kLoop, calls=%fused_computation.14.clone.1 | loop fusion | flops 6291456 | bytes 4456576 | tf_op jit(solution)/shard_map/convert.6
  57.8 0.9 fusion.45
  60.2 0.9 constant_dynamic-slice_fusion.5
  61.2 0.9 constant_dynamic-slice_fusion.6
  62.2 15.5 %fusion.44 = (bf16[32,512,32]{1,2,0:T(8,128)(2,1)S(1)}, bf16[32,512,32]{1,2,0:T(8,128)(2,1)S(1)}, bf16[32,512,32]{1,2,0:T(8,128)(2,1)S(1)}, bf16[32,512,32]{1,2,0:T(8,128)(2,1)S(1)}) fusion(f32[32,512]{1,0:T(8,128)S(1)} %get-tuple-element.144, f32[32]{0:T(128)S(1)} %add_multiply_fusion.2, f32[32,512]{1,0:T(8,128)S(1)} %get-tuple-element.145, ...), kind=kLoop, calls=%fused_computation.14.clone.1 | loop fusion | flops 6291456 | bytes 4456576 | tf_op jit(solution)/shard_map/convert.6
  77.8 0.9 fusion.45
  80.3 0.9 constant_dynamic-slice_fusion.5
  81.2 0.9 constant_dynamic-slice_fusion.6
  82.3 15.5 %fusion.44 = (bf16[32,512,32]{1,2,0:T(8,128)(2,1)S(1)}, bf16[32,512,32]{1,2,0:T(8,128)(2,1)S(1)}, bf16[32,512,32]{1,2,0:T(8,128)(2,1)S(1)}, bf16[32,512,32]{1,2,0:T(8,128)(2,1)S(1)}) fusion(f32[32,512]{1,0:T(8,128)S(1)} %get-tuple-element.144, f32[32]{0:T(128)S(1)} %add_multiply_fusion.2, f32[32,512]{1,0:T(8,128)S(1)} %get-tuple-element.145, ...), kind=kLoop, calls=%fused_computation.14.clone.1 | loop fusion | flops 6291456 | bytes 4456576 | tf_op jit(solution)/shard_map/convert.6
  97.8 0.9 fusion.45
  100.3 0.9 constant_dynamic-slice_fusion.5
  101.3 0.9 constant_dynamic-slice_fusion.6
  102.3 15.5 %fusion.44 = (bf16[32,512,32]{1,2,0:T(8,128)(2,1)S(1)}, bf16[32,512,32]{1,2,0:T(8,128)(2,1)S(1)}, bf16[32,512,32]{1,2,0:T(8,128)(2,1)S(1)}, bf16[32,512,32]{1,2,0:T(8,128)(2,1)S(1)}) fusion(f32[32,512]{1,0:T(8,128)S(1)} %get-tuple-element.144, f32[32]{0:T(128)S(1)} %add_multiply_fusion.2, f32[32,512]{1,0:T(8,128)S(1)} %get-tuple-element.145, ...), kind=kLoop, calls=%fused_computation.14.clone.1 | loop fusion | flops 6291456 | bytes 4456576 | tf_op jit(solution)/shard_map/convert.6
  117.8 0.9 fusion.45
  120.3 0.9 constant_dynamic-slice_fusion.5
  121.3 0.9 constant_dynamic-slice_fusion.6
  122.3 15.5 %fusion.44 = (bf16[32,512,32]{1,2,0:T(8,128)(2,1)S(1)}, bf16[32,512,32]{1,2,0:T(8,128)(2,1)S(1)}, bf16[32,512,32]{1,2,0:T(8,128)(2,1)S(1)}, bf16[32,512,32]{1,2,0:T(8,128)(2,1)S(1)}) fusion(f32[32,512]{1,0:T(8,128)S(1)} %get-tuple-element.144, f32[32]{0:T(128)S(1)} %add_multiply_fusion.2, f32[32,512]{1,0:T(8,128)S(1)} %get-tuple-element.145, ...), kind=kLoop, calls=%fused_computation.14.clone.1 | loop fusion | flops 6291456 | bytes 4456576 | tf_op jit(solution)/shard_map/convert.6
  137.8 0.9 fusion.45
  140.3 0.9 constant_dynamic-slice_fusion.5
  141.3 0.9 constant_dynamic-slice_fusion.6
  142.3 15.5 %fusion.44 = (bf16[32,512,32]{1,2,0:T(8,128)(2,1)S(1)}, bf16[32,512,32]{1,2,0:T(8,128)(2,1)S(1)}, bf16[32,512,32]{1,2,0:T(8,128)(2,1)S(1)}, bf16[32,512,32]{1,2,0:T(8,128)(2,1)S(1)}) fusion(f32[32,512]{1,0:T(8,128)S(1)} %get-tuple-element.144, f32[32]{0:T(128)S(1)} %add_multiply_fusion.2, f32[32,512]{1,0:T(8,128)S(1)} %get-tuple-element.145, ...), kind=kLoop, calls=%fused_computation.14.clone.1 | loop fusion | flops 6291456 | bytes 4456576 | tf_op jit(solution)/shard_map/convert.6
  157.8 0.9 fusion.45
  160.3 0.9 constant_dynamic-slice_fusion.5
  161.3 0.9 constant_dynamic-slice_fusion.6
  162.3 15.5 %fusion.44 = (bf16[32,512,32]{1,2,0:T(8,128)(2,1)S(1)}, bf16[32,512,32]{1,2,0:T(8,128)(2,1)S(1)}, bf16[32,512,32]{1,2,0:T(8,128)(2,1)S(1)}, bf16[32,512,32]{1,2,0:T(8,128)(2,1)S(1)}) fusion(f32[32,512]{1,0:T(8,128)S(1)} %get-tuple-element.144, f32[32]{0:T(128)S(1)} %add_multiply_fusion.2, f32[32,512]{1,0:T(8,128)S(1)} %get-tuple-element.145, ...), kind=kLoop, calls=%fused_computation.14.clone.1 | loop fusion | flops 6291456 | bytes 4456576 | tf_op jit(solution)/shard_map/convert.6
  177.9 0.9 fusion.45
  180.3 2.5 gather_fusion.1
  182.9 1.6 broadcast_multiply_fusion
  184.5 6.0 %all-to-all-start.1 = ((bf16[8,64,2048]{2,1,0:T(8,128)(2,1)}), bf16[8,64,2048]{2,1,0:T(8,128)(2,1)S(1)}, u32[]{:S(2)}, u32[]{:S(2)}) async-start(bf16[8,64,2048]{2,1,0:T(8,128)(2,1)} %broadcast_multiply_fusion), calls=%async_computation.1 | async-start | bytes 4194304 | tf_op jit(solution)/shard_map/all_to_all | solution.py:77
  191.2 0.7 reduce.5
  191.9 46.2 %all-to-all-done.1 = bf16[8,64,2048]{2,1,0:T(8,128)(2,1)S(1)} async-done(((bf16[8,64,2048]{2,1,0:T(8,128)(2,1)}), bf16[8,64,2048]{2,1,0:T(8,128)(2,1)S(1)}, u32[]{:S(2)}, u32[]{:S(2)}) %all-to-all-start.1) | async-done | bytes 2097184 | tf_op jit(solution)/shard_map/all_to_all | solution.py:77
  238.1 2.5 copy.21
  240.6 2.4 convolution_bitcast_fusion
  243.0 2.6 copy.22
  245.6 4.3 %reshape.223 = f32[32,2,4096]{2,0,1:T(8,128)} reshape(f32[32,2,128,32]{3,2,0,1:T(8,128)} %copy.22) | data formatting | bytes 2097152 | tf_op jit(solution)/shard_map/reshape | solution.py:88
  250.0 18.8 %all-reduce.2.cloned.1.call-done = f32[32,2,4096]{2,0,1:T(8,128)} async-done(((f32[32,2,4096]{2,0,1:T(8,128)}), f32[32,2,4096]{2,0,1:T(8,128)}) %all-reduce.2.cloned.1.call-update) | async-done | bytes 1048592 | tf_op jit(solution)/shard_map/psum | solution.py:90
  268.8 3.0 %copy.23 = f32[32,2,4096]{2,1,0:T(2,128)} copy(f32[32,2,4096]{2,0,1:T(8,128)} %all-reduce.2.cloned.1.call-done) | data formatting | bytes 2097152 | tf_op jit(solution)/shard_map/psum | solution.py:90
  (113 shorter events, 15.9 us)
Async XLA Ops:
  6.5 2.1 copy-start
  6.5 13.6 %copy-start.1 = (s32[256]{0:T(256)S(1)}, s32[256]{0:T(256)}, u32[]{:S(2)}) copy-start(s32[256]{0:T(256)} %param.10) | copy-start | bytes 3076
  12.9 171.6 %all-to-all-start = ((s32[8,1,64]{2,1,0:T(1,128)}), s32[8,1,64]{2,1,0:T(1,128)S(1)}, u32[]{:S(2)}, u32[]{:S(2)}) async-start(s32[8,1,64]{2,1,0:T(1,128)} %select_n.38), calls=%async_computation | async-start | bytes 8192 | tf_op jit(solution)/shard_map/all_to_all | solution.py:78
  184.5 53.7 %all-to-all-start.1 = ((bf16[8,64,2048]{2,1,0:T(8,128)(2,1)}), bf16[8,64,2048]{2,1,0:T(8,128)(2,1)S(1)}, u32[]{:S(2)}, u32[]{:S(2)}) async-start(bf16[8,64,2048]{2,1,0:T(8,128)(2,1)} %broadcast_multiply_fusion), calls=%async_computation.1 | async-start | bytes 4194304 | tf_op jit(solution)/shard_map/all_to_all | solution.py:77
  190.4 78.4 %all-reduce.2.cloned.1.call-start = ((), (), s32[]{:S(2)}) async-start(), calls=%async_computation.2 | async-start | bytes 2097152 | tf_op jit(solution)/shard_map/psum | solution.py:90
Sparse Core Ops, SparseCore 0:
  250.1 18.6 all-reduce.1
where the time goes:
time: 279 us
  other arithmetic  133 us (48%)
  waiting for transfers between devices  65 us (23%)
  local copies, waits for them, and re-layouts  43.7 us (16%)
  between operations  13.5 us (5%)
  starting transfers between devices  13.4 us (5%)
  matrix products  9.34 us (3%)
    another operation x10, other arithmetic  125 us
    all_to_all x1, waiting for transfers between devices, local(): lax.all_to_all(outgoing, ('blk', 'tile'), split_axis=0, concat_axis=0, ti...  46.2 us
    psum x1, waiting for transfers between devices, local(): summed = lax.psum(tile_grid, 'samp')  18.8 us
    dynamic_slice x32, local copies, waits for them, and re-layouts, local(): lax.map(make_subgrids, (residual[0].reshape((turns, per_turn) + residual....  14.8 us
    all_to_all x1, starting transfers between devices, local(): lax.all_to_all(out_slots, ('blk', 'tile'), split_axis=0, concat_axis=0, t...  7.25 us
    dot_general x8, matrix products, make_subgrids(): jnp.einsum('bkp,bkq->bpq', left_kernel, right_kernel, preferred_element_t...  6.94 us
    all_to_all x1, starting transfers between devices, local(): lax.all_to_all(outgoing, ('blk', 'tile'), split_axis=0, concat_axis=0, ti...  5.98 us
  transfers between devices with their start and end apart: 3, of which 2 were waited for; matrix products, arithmetic and copies ran while one was open for 59% of the time, Pallas kernels for 0%

commit v1 on v0

v1 whole, which is shorter than its diff:
```python
import itertools

import jax
import jax.numpy as jnp
import numpy as np
from jax import lax
from jax.experimental import pallas as pl
from jax.experimental.pallas import tpu as pltpu
from jax.sharding import PartitionSpec as P

SUB = 32
HALF = SUB // 2
SLOTS = 128
FEATURE = 2 * HALF * SUB
CAP_MIN = 8
GROUP = 8
QUAD = 4
VMEM_LIMIT = 48 * 1024 * 1024


def turn_coefficients():
    knots = np.cos(np.pi * (np.arange(400) + 0.5) / 400)
    cheb = np.polynomial.chebyshev
    even = cheb.cheb2poly(cheb.chebfit(knots, np.cos(np.pi * knots), 12))[0::2]
    odd = cheb.cheb2poly(cheb.chebfit(knots, np.sin(np.pi * knots), 13))[1::2]
    return [float(x) for x in even], [float(x) for x in odd]


COS_COEF, SIN_COEF = turn_coefficients()


def horner(coef, x):
    total = coef[-1] * x + coef[-2]
    for value in coef[-3::-1]:
        total = total * x + value
    return total


def harmonics(offset):
    y = offset * (1.0 / HALF)
    x = y * y
    c1, s1 = horner(COS_COEF, x), horner(SIN_COEF, x) * y
    c2, s2 = 1.0 - 2.0 * s1 * s1, 2.0 * s1 * c1
    c3, s3 = c2 * c1 - s2 * s1, s2 * c1 + c2 * s1
    c4, s4 = 1.0 - 2.0 * s2 * s2, 2.0 * s2 * c2
    c8, s8 = 1.0 - 2.0 * s4 * s4, 2.0 * s4 * c4
    return (c1, c2, c3, c4, c8), (s1, s2, s3, s4, s8)


def fill_table(cos_ref, sin_ref, c, s):
    one = jnp.ones_like(c[0])
    cos_rows = (c[3], c[2], c[1], c[0], one, c[0], c[1], c[2])
    sin_rows = (-s[3], -s[2], -s[1], -s[0], jnp.zeros_like(one), s[0], s[1], s[2])
    for r in range(GROUP):
        for t in range(one.shape[1] // 128):
            at = pl.ds(t * GROUP * GROUP + r, GROUP, stride=GROUP)
            cos_ref[at, :] = cos_rows[r][:, t * 128 : (t + 1) * 128]
            sin_ref[at, :] = sin_rows[r][:, t * 128 : (t + 1) * 128]


def pair(halves):
    return jnp.concatenate(halves, 0).astype(jnp.bfloat16)


def subgrid_kernel(
    row_ref, side_ref, u_ref, v_ref, re_ref, im_ref, out_ref,
    cos_u, sin_u, cos_v, sin_v, dense, lefts, rights, stage,
):
    blocks = u_ref.shape[0]
    vis = u_ref.shape[1]
    rows = out_ref.shape[0]
    side = side_ref[0].astype(jnp.float32)
    lane = lax.broadcasted_iota(jnp.int32, (GROUP, 128), 1) // SUB

    @pl.loop(0, rows // 8)
    def _(i):
        stage[pl.ds(pl.multiple_of(i * 64, 64), 64), :] = jnp.zeros((64, 128), jnp.float32)

    @pl.loop(0, blocks // GROUP)
    def _(g):
        here = pl.ds(pl.multiple_of(g * GROUP, GROUP), GROUP)
        c, s = harmonics(u_ref[here, :])
        fill_table(cos_u, sin_u, c, s)
        s8 = s[4] * side
        re, im = re_ref[here, :], im_ref[here, :]
        vr, vi = re * c[4] - im * s8, re * s8 + im * c[4]
        a, b, e, f = vr * c[3], vi * s[3], vi * c[3], vr * s[3]
        dense[0] = a + b
        dense[1] = e - f
        dense[2] = a - b
        dense[3] = e + f
        c, s = harmonics(v_ref[here, :])
        fill_table(cos_v, sin_v, c, s)
        dense[4] = c[3]
        dense[5] = s[3]
        dense[6] = c[4] * c[3] - s[4] * s[3]
        dense[7] = s[4] * c[3] + c[4] * s[3]
        for quad in range(GROUP // QUAD):
            left, right = lefts.at[quad], rights.at[quad]
            for b, t in itertools.product(range(QUAD), range(vis // 128)):
                i = quad * QUAD + b
                mine = pl.ds((t * GROUP + i) * GROUP, GROUP)
                lanes = pl.ds(t * 128, 128)

                def spread(k):
                    return jnp.broadcast_to(dense[k, pl.ds(i, 1), lanes], (GROUP, 128))

                fc, fs = cos_u[mine, :], sin_u[mine, :]
                real, imag = [], []
                for h in range(2):
                    wr, wi = spread(2 * h), spread(2 * h + 1)
                    real.append(fc * wr - fs * wi)
                    imag.append(fs * wr + fc * wi)
                left[pl.ds(b * SUB, HALF), lanes] = pair(real)
                left[pl.ds(b * SUB + HALF, HALF), lanes] = pair(imag)
                gc, gs = cos_v[mine, :], sin_v[mine, :]
                cos_rows, sin_rows = [None] * 4, [None] * 4
                for h, (low, high) in enumerate(((1, 2), (0, 3))):
                    ch, sh = spread(4 + 2 * h), spread(5 + 2 * h)
                    p, q, r, x = gc * ch, gs * sh, gs * ch, gc * sh
                    cos_rows[low], cos_rows[high] = p + q, p - q
                    sin_rows[low], sin_rows[high] = r - x, r + x
                for h in range(2):
                    at = b * SUB + h * HALF
                    right[pl.ds(at, HALF), lanes] = pair(cos_rows[2 * h : 2 * h + 2])
                    right[pl.ds(QUAD * SUB + at, HALF), lanes] = pair(sin_rows[2 * h : 2 * h + 2])
            product = lax.dot_general(
                left[...], right[...], (((1,), (1,)), ((), ())), preferred_element_type=jnp.float32
            )
            for b in range(QUAD):
                mine = product[b * SUB : (b + 1) * SUB]
                with_cos, with_sin = mine[:, :128], mine[:, 128:]
                real = with_cos[:HALF] - with_sin[HALF:]
                imag = with_cos[HALF:] + with_sin[:HALF]
                parts = (real[:GROUP], real[GROUP:], imag[:GROUP], imag[GROUP:])
                total = None
                for k in range(4):
                    moved = parts[k]
                    if k != b:
                        moved = pltpu.roll(moved, ((k - b) % 4) * SUB, 1)
                    total = moved if total is None else jnp.where(lane == k, moved, total)
                row = row_ref[g * GROUP + quad * QUAD + b]
                stage[pl.ds(pl.multiple_of(row * 8, 8), 8), :] = total

    @pl.loop(0, rows // 16)
    def _(i):
        for k in range(8):
            piece = stage[pl.ds(i * 128 + k, 16, stride=8), :]
            out_ref[pl.ds(pl.multiple_of(i * 16, 16), 16), pl.ds(k * 128, 128)] = piece.astype(
                jnp.bfloat16
            )


def make_subgrids(rows, target, side, u, v, re, im):
    vis = u.shape[1]
    vmem = pl.BlockSpec(memory_space=pltpu.VMEM)
    smem = pl.BlockSpec(memory_space=pltpu.SMEM)
    table = pltpu.VMEM((GROUP * GROUP * (vis // 128), 128), jnp.float32)
    return pl.pallas_call(
        subgrid_kernel,
        out_shape=jax.ShapeDtypeStruct((rows, FEATURE), jnp.bfloat16),
        in_specs=[smem, smem, vmem, vmem, vmem, vmem],
        out_specs=vmem,
        scratch_shapes=[
            table, table, table, table,
            pltpu.VMEM((8, GROUP, vis), jnp.float32),
            pltpu.VMEM((GROUP // QUAD, QUAD * SUB, vis), jnp.bfloat16),
            pltpu.VMEM((GROUP // QUAD, 2 * QUAD * SUB, vis), jnp.bfloat16),
            pltpu.VMEM((rows * 8, 128), jnp.float32),
        ],
        compiler_params=pltpu.CompilerParams(vmem_limit_bytes=VMEM_LIMIT),
        name="subgrids",
    )(target, side, u, v, re, im)


def gather_kernel(slot_ref, x_ref, out_ref, hot, part):
    rows = x_ref.shape[0]
    lane = lax.broadcasted_iota(jnp.int32, (GROUP, 128), 1) // SUB
    wanted = lax.broadcasted_iota(jnp.int32, (SLOTS, rows), 0)
    wanted = (wanted % 32) * 4 + wanted // 32
    hot[...] = jnp.where(slot_ref[...] == wanted, 1.0, 0.0).astype(jnp.bfloat16)
    for k in range(8):
        part[...] = jnp.dot(
            hot[...], x_ref[:, pl.ds(k * 128, 128)], preferred_element_type=jnp.float32
        )
        for grp in range(4):
            given = [part[pl.ds(32 * jl + 8 * grp, 8), :] for jl in range(4)]
            for a in range(4):
                total = None
                for jl in range(4):
                    moved = given[jl]
                    if a != jl:
                        moved = pltpu.roll(moved, ((jl - a) % 4) * SUB, 1)
                    total = moved if total is None else jnp.where(lane == jl, moved, total)
                p = (a % 2) * 8 + k
                out_ref[pl.ds(p * 64 + grp * 16 + a // 2, 8, stride=2), :] = total


def sum_slots(slots, arrived):
    rows = arrived.shape[0]
    vmem = pl.BlockSpec(memory_space=pltpu.VMEM)
    return pl.pallas_call(
        gather_kernel,
        out_shape=jax.ShapeDtypeStruct((HALF * 64, 128), jnp.float32),
        in_specs=[vmem, vmem],
        out_specs=vmem,
        scratch_shapes=[
            pltpu.VMEM((SLOTS, rows), jnp.bfloat16),
            pltpu.VMEM((SLOTS, 128), jnp.float32),
        ],
        compiler_params=pltpu.CompilerParams(vmem_limit_bytes=VMEM_LIMIT),
        name="sum_slots",
    )(slots, arrived)


def local(residual, uv_offsets, counts, tile_of_block, slot_of_block, owner_map):
    blocks, _, vis = uv_offsets.shape
    owners = owner_map.shape[0]
    capacity = max(CAP_MIN, 2 * blocks // owners)
    rows = owners * capacity
    core = lax.axis_index("samp")
    me = lax.axis_index(("blk", "tile"))
    swap = [(0, 1), (1, 0)]
    own = residual[0]
    other = lax.ppermute(own, "samp", swap)

    tile_ids = tile_of_block[:, 0]
    owner_range = jnp.arange(owners, dtype=jnp.int32)
    owner_ids = jnp.sum(
        jnp.where(tile_ids[:, None] == owner_range[None, :], owner_map[None, :], 0), 1
    )
    code = owner_ids * SLOTS + slot_of_block
    codes = lax.all_gather(code, ("blk", "tile"), axis=0, tiled=False)
    same_owner = (owner_ids[:, None] == owner_range[None, :]).astype(jnp.int32)
    earlier = jnp.sum((jnp.cumsum(same_owner, 0) - same_owner) * same_owner, 1)
    target = owner_ids * capacity + earlier

    live = jnp.arange(vis, dtype=jnp.int32)[None, :] < counts[:, None]
    both = own.astype(jnp.float32) + other.astype(jnp.float32)
    both = jnp.where(live[:, None, :], both, 0.0)
    side = (2 * core - 1).astype(jnp.int32).reshape(1)
    outgoing = make_subgrids(
        rows, target, side, uv_offsets[:, 0], uv_offsets[:, 1], both[:, 0], both[:, 1]
    )
    arrived = lax.all_to_all(
        outgoing.reshape(owners, capacity, FEATURE), ("blk", "tile"),
        split_axis=0, concat_axis=0, tiled=True,
    ).reshape(rows, FEATURE)

    mine = (codes // SLOTS == me).astype(jnp.int32)
    order = jnp.cumsum(mine, 1) - mine
    place = jnp.where(mine > 0, order, capacity)
    rank = jnp.arange(capacity, dtype=jnp.int32)
    slots = jnp.sum(
        jnp.where(place[:, None, :] == rank[None, :, None], codes[:, None, :] % SLOTS + 1, 0), 2
    )
    slots = jnp.where(slots > 0, slots - 1, SLOTS).reshape(1, rows)
    half = sum_slots(slots, arrived)
    half = half.reshape(HALF, SLOTS // 4, 2, 128).transpose(0, 2, 1, 3).reshape(HALF, 2, SLOTS * SUB)
    theirs = lax.ppermute(half, "samp", swap)
    return jnp.where(
        core == 0,
        jnp.concatenate([half, theirs], 0),
        jnp.concatenate([theirs, half], 0),
    )


def solution(mesh):
    in_specs = (
        P("samp", ("cuts", "blk", "tile"), None, None),
        P(("cuts", "blk", "tile"), None, None),
        P(("cuts", "blk", "tile")),
        P(("cuts", "blk", "tile"), None),
        P(("cuts", "blk", "tile")),
        P(),
    )
    out_specs = P(("cuts", "blk", "tile"), None, None)
    return jax.shard_map(local, mesh=mesh, in_specs=in_specs, out_specs=out_specs, check_vma=False)
```

time: 279 us -> 73 us (0.26)
  other arithmetic: 133 us -> 3.6 us
  waiting for transfers between devices: 65 us -> 1.9 us
  local copies, waits for them, and re-layouts: 43.7 us -> 4.43 us
  blocking collectives: 0 us -> 32 us
  Pallas kernels: 0 us -> 22 us
  between operations: 13.5 us -> 0.17 us
  matrix products: 9.34 us -> 0 us
  starting transfers between devices: 13.4 us -> 7.84 us
    another operation x26 -> x4, other arithmetic: 128 us -> 1.24 us
    all_to_all x2 -> x1, waiting for transfers between devices: 46.2 us -> 0.01 us  [local(): lax.all_to_all(outgoing.reshape(owners, capacity, FEATURE), ('blk', 'tile...]
    all_gather x0 -> x1, blocking collectives: none -> 32 us  [local(): codes = lax.all_gather(code, ('blk', 'tile'), axis=0, tiled=False)]
    pallas_call x0 -> x2, Pallas kernels: none -> 22 us  [the longest x1 21.3 us: make_subgrids(): pl.pallas_call(subgrid_kernel, out_shape=jax.ShapeDtypeStruct((rows, FEAT...]
    psum x1 -> x0, waiting for transfers between devices: 18.8 us -> none  [local(): summed = lax.psum(tile_grid, 'samp')]
    dynamic_slice x32 -> x0, local copies, waits for them, and re-layouts: 14.8 us -> none  [local(): lax.map(make_subgrids, (residual[0].reshape((turns, per_turn) + residual....]
    dot_general x9 -> x0, matrix products: 9.34 us -> none  [the longest x8 6.94 us: make_subgrids(): jnp.einsum('bkp,bkq->bpq', left_kernel, right_kernel, preferred_element_t...]
    gather x2 -> x0, local copies, waits for them, and re-layouts: 5.98 us -> none  [the longest x1 3.52 us: local(): slot_of_block[source]]
  transfers between devices with their start and end apart: 3 -> 3, of which waited for: 2 -> 1; matrix products, arithmetic and copies ran while one was open for 59% -> 5% of each run, Pallas kernels for 0% -> 0%
where the time goes in v1:
time: 73 us; the launch traced here: 71.9 us
  blocking collectives  32 us (44%)
  Pallas kernels  22 us (30%)
  starting transfers between devices  7.84 us (11%)
  local copies, waits for them, and re-layouts  4.43 us (6%)
  other arithmetic  3.6 us (5%)
  waiting for transfers between devices  1.9 us (3%)
    all_gather x1, blocking collectives, local(): codes = lax.all_gather(code, ('blk', 'tile'), axis=0, tiled=False)  32 us
    pallas_call x1, Pallas kernels, make_subgrids(): pl.pallas_call(subgrid_kernel, out_shape=jax.ShapeDtypeStruct((rows, FEAT...  21.3 us
    all_to_all x1, starting transfers between devices, local(): lax.all_to_all(outgoing.reshape(owners, capacity, FEATURE), ('blk', 'tile...  7.25 us
    unnamed x13, local copies, waits for them, and re-layouts  2.96 us
    ppermute x1, waiting for transfers between devices, local(): theirs = lax.ppermute(half, 'samp', swap)  1.89 us
    select_n x1, other arithmetic, local(): jnp.where(core == 0, jnp.concatenate([half, theirs], 0), jnp.concatenate(...  1.55 us
  transfers between devices with their start and end apart: 3, of which 1 were waited for; matrix products, arithmetic and copies ran while one was open for 5% of the time, Pallas kernels for 0%

profile of v1, /device:TPU:0, one launch (start us, length us, event | category | flops | bytes accessed | tf_op | source)
XLA Modules:
  0.0 71.9 jit_solution(3102554504360715105)
XLA Ops:
  0.0 0.0 copy-start.1
  0.0 1.2 %copy.51 = bf16[1,256,2,512]{3,1,2,0:T(8,128)(2,1)S(1)} copy(bf16[1,256,2,512]{3,2,1,0:T(2,128)(2,1)} %param.6) | data formatting | bytes 1048576 | tf_op args[0]
  1.2 0.0 copy-start.4
  1.2 0.0 copy-start.5
  1.2 0.5 collective-permute-start
  1.7 0.1 copy-done.4
  1.9 0.0 copy-done.5
  1.9 0.1 select_reduce_fusion.1
  2.0 0.6 reduce-window.16
  2.5 0.2 slice_reduce_fusion
  2.8 0.1 fusion.5
  2.9 0.0 copy-done.1
  2.9 0.0 copy-start.3
  2.9 0.8 %fusion.10 = (f32[256,1,512]{2,1,0:T(1,128)S(1)}, f32[256,1,512]{2,1,0:T(1,128)S(1)}) fusion(f32[256,2,512]{2,1,0:T(2,128)S(1)} %copy-done.1), kind=kLoop, calls=%fused_computation.39 | loop fusion | bytes 2097152 | tf_op jit(solution)/shard_map/slice | solution.py:243
  3.7 0.0 copy-done.3
  3.8 0.0 copy-start.2
  3.8 0.7 copy-done.2
  4.4 0.1 iota_compare_fusion
  4.6 0.0 copy-start
  4.6 0.1 copy_bitcast_fusion
  4.7 0.0 collective-permute-done
  4.7 0.9 %copy-done = bf16[1,256,2,512]{3,2,1,0:T(2,128)(2,1)S(1)} copy-done((bf16[1,256,2,512]{3,2,1,0:T(2,128)(2,1)S(1)}, bf16[1,256,2,512]{3,2,1,0:T(2,128)(2,1)}, u32[]{:S(2)}) %copy-start) | copy-done | bytes 524312
  5.6 0.2 add_select_fusion
  5.8 0.1 slice_bitcast_fusion
  5.9 21.3 %subgrids.1 = bf16[512,1024]{1,0:T(8,128)(2,1)} custom-call(s32[256]{0:T(256)S(1)} %get-tuple-element.11.row_ref, s32[1]{0:T(128)} %bitcast.7.side_ref, f32[256,512]{1,0:T(8,128)S(1)} %get-tuple-element.16.u_ref, f32[256,512]{1,0:T(8,128)S(1)} %get-tuple-element.15.v_ref, f32[256,512]{1,0:T(8,128)S(1)} %get-tuple-element.8.re_ref, ...), custom_call_target="tpu_custom_call" | custom-call | tf_op jit(solution)/shard_map/subgrids/pallas_call | solution.py:159
  27.2 7.2 %all-to-all-start = ((bf16[8,64,1024]{2,1,0:T(8,128)(2,1)}), bf16[8,64,1024]{2,1,0:T(8,128)(2,1)S(1)}, u32[]{:S(2)}, u32[]{:S(2)}) async-start(bf16[8,64,1024]{2,1,0:T(8,128)(2,1)} %bitcast.13), calls=%async_computation | async-start | bytes 2097152 | tf_op jit(solution)/shard_map/all_to_all | solution.py:245
  34.5 32.0 %all-gather.1 = s32[8,1,256]{2,1,0:T(1,128)S(1)} all-gather(s32[1,1,256]{2,1,0:T(1,128)S(1)} %bitcast.68), channel_id=2, replica_groups=mesh['cuts'=2,'samp'=2,'blk'=4,'tile'=2] {'blk','tile'}, dimensions={0}, use_global_device_ids=true | all-gather | bytes 9216 | tf_op jit(solution)/shard_map/all_gather | solution.py:233
  66.4 0.6 reduce-window.14
  67.0 0.2 slice_reduce_fusion.1
  67.3 0.1 fusion.1
  67.4 0.2 select_reduce_fusion
  67.6 0.1 select_n.58.slot_ref
  67.7 0.0 all-to-all-done
  67.7 0.7 sum_slots.1
  68.4 0.1 collective-permute-start.1
  68.5 1.9 %collective-permute-done.1 = f32[16,2,4096]{2,1,0:T(2,128)S(1)} collective-permute-done((f32[16,2,4096]{2,1,0:T(2,128)S(1)}, f32[16,2,4096]{2,1,0:T(2,128)S(1)}, u32[]{:S(2)}, u32[]{:S(2)}) %collective-permute-start.1) | collective-permute-done | bytes 524320 | tf_op jit(solution)/shard_map/ppermute | solution.py:260
  70.4 1.5 %maximum_select_fusion = f32[32,2,4096]{2,1,0:T(2,128)} fusion(f32[16,2,4096]{2,1,0:T(2,128)S(1)} %collective-permute-done.1, f32[16,2,4096]{2,1,0:T(2,128)S(1)} %bitcast.65, pred[]{:T(512)S(6)} %eq.62), kind=kLoop, calls=%fused_computation | loop fusion | flops 786432 | bytes 2097153 | tf_op jit(solution)/shard_map/jit(_where)/select_n | solution.py:261
  (8 shorter events, 0.1 us)
Async XLA Ops:
  0.0 2.9 %copy-start.1 = (f32[256,2,512]{2,1,0:T(2,128)S(1)}, f32[256,2,512]{2,1,0:T(2,128)}, u32[]{:S(2)}) copy-start(f32[256,2,512]{2,1,0:T(2,128)} %param.7) | copy-start | bytes 3145732
  1.2 0.7 copy-start.4
  1.2 0.7 copy-start.5
  1.2 3.5 %collective-permute-start = (bf16[256,2,512]{2,0,1:T(8,128)(2,1)S(1)}, bf16[256,2,512]{2,0,1:T(8,128)(2,1)S(1)}, u32[]{:S(2)}, u32[]{:S(2)}) collective-permute-start(bf16[256,2,512]{2,0,1:T(8,128)(2,1)S(1)} %bitcast.66), channel_id=1, source_target_pairs={{0,8},{8,0},{1,9},{9,1},{2,10},{10,2},{3,11},{11,3},{4,12},{12,4},... | collective-permute-start | bytes 1572872 | tf_op jit(solution)/shard_map/ppermute | solution.py:225
  2.9 0.8 %copy-start.3 = (s32[256]{0:T(256)S(1)}, s32[256]{0:T(256)}, u32[]{:S(2)}) copy-start(s32[256]{0:T(256)} %param.10) | copy-start | bytes 3076
  3.8 0.7 copy-start.2
  4.6 1.0 %copy-start = (bf16[1,256,2,512]{3,2,1,0:T(2,128)(2,1)S(1)}, bf16[1,256,2,512]{3,2,1,0:T(2,128)(2,1)}, u32[]{:S(2)}) copy-start(bf16[1,256,2,512]{3,2,1,0:T(2,128)(2,1)} %param.6) | copy-start | bytes 1572868
  27.2 40.5 %all-to-all-start = ((bf16[8,64,1024]{2,1,0:T(8,128)(2,1)}), bf16[8,64,1024]{2,1,0:T(8,128)(2,1)S(1)}, u32[]{:S(2)}, u32[]{:S(2)}) async-start(bf16[8,64,1024]{2,1,0:T(8,128)(2,1)} %bitcast.13), calls=%async_computation | async-start | bytes 2097152 | tf_op jit(solution)/shard_map/all_to_all | solution.py:245
  68.4 2.0 %collective-permute-start.1 = (f32[16,2,4096]{2,1,0:T(2,128)S(1)}, f32[16,2,4096]{2,1,0:T(2,128)S(1)}, u32[]{:S(2)}, u32[]{:S(2)}) collective-permute-start(f32[16,2,4096]{2,1,0:T(2,128)S(1)} %bitcast.64), channel_id=1, source_target_pairs={{0,8},{8,0},{1,9},{9,1},{2,10},{10,2},{3,11},{11,3},{4,12},{12,4},... | collective-permute-start | bytes 1572872 | tf_op jit(solution)/shard_map/ppermute | solution.py:260

commit v2 on v1

v2 whole, which is shorter than its diff:
```python
import functools

import jax
import jax.numpy as jnp
import numpy as np
from jax import lax
from jax.experimental import pallas as pl
from jax.experimental.pallas import tpu as pltpu
from jax.sharding import PartitionSpec as P

SUB = 32
HALF = SUB // 2
SLOTS = 128
FEATURE = 2 * HALF * SUB
CAP_MIN = 8
GROUP = 8
QUAD = 4
PAIRED_MAX = 16
VMEM_LIMIT = 48 * 1024 * 1024


def turn_coefficients():
    knots = np.cos(np.pi * (np.arange(400) + 0.5) / 400)
    cheb = np.polynomial.chebyshev
    even = cheb.cheb2poly(cheb.chebfit(knots, np.cos(np.pi * knots), 12))[0::2]
    odd = cheb.cheb2poly(cheb.chebfit(knots, np.sin(np.pi * knots), 13))[1::2]
    return [float(x) for x in even], [float(x) for x in odd]


COS_COEF, SIN_COEF = turn_coefficients()


def horner(coef, x):
    total = coef[-1] * x + coef[-2]
    for value in coef[-3::-1]:
        total = total * x + value
    return total


def harmonics(offset):
    y = offset * (1.0 / HALF)
    x = y * y
    c1, s1 = horner(COS_COEF, x), horner(SIN_COEF, x) * y
    c2, s2 = 1.0 - 2.0 * s1 * s1, 2.0 * s1 * c1
    c3, s3 = c2 * c1 - s2 * s1, s2 * c1 + c2 * s1
    c4, s4 = 1.0 - 2.0 * s2 * s2, 2.0 * s2 * c2
    c8, s8 = 1.0 - 2.0 * s4 * s4, 2.0 * s4 * c4
    return (c1, c2, c3, c4, c8), (s1, s2, s3, s4, s8)


def fill_table(cos_ref, sin_ref, c, s):
    one = jnp.ones_like(c[0])
    cos_rows = (c[3], c[2], c[1], c[0], one, c[0], c[1], c[2])
    sin_rows = (-s[3], -s[2], -s[1], -s[0], jnp.zeros_like(one), s[0], s[1], s[2])
    for r in range(GROUP):
        for t in range(one.shape[1] // 128):
            at = pl.ds(t * GROUP * GROUP + r, GROUP, stride=GROUP)
            cos_ref[at, :] = cos_rows[r][:, t * 128 : (t + 1) * 128]
            sin_ref[at, :] = sin_rows[r][:, t * 128 : (t + 1) * 128]


def pair(halves):
    return jnp.concatenate(halves, 0).astype(jnp.bfloat16)


def subgrid_kernel(
    first, capacity, order_ref, start_ref, side_ref, uv_ref, res_ref, out_ref,
    gathered, cos_u, sin_u, cos_v, sin_v, dense, lefts, rights, stage,
):
    tiles = gathered.shape[0] // (4 * GROUP)
    vis = tiles * 128
    side = side_ref[0].astype(jnp.float32)
    lane = lax.broadcasted_iota(jnp.int32, (GROUP, 128), 1) // SUB

    def wide(ref, row, stride=1, step=GROUP):
        return jnp.concatenate(
            [ref[pl.ds(row + t * step, GROUP, stride=stride), :] for t in range(tiles)], 1
        )

    def serve(index):
        start = start_ref[first + index]
        count = start_ref[first + index + 1] - start
        turns = (count + GROUP - 1) // GROUP

        @pl.loop(turns, capacity // GROUP)
        def _(g):
            at = pl.ds(pl.multiple_of(g * GROUP * 8, GROUP * 8), GROUP * 8)
            stage[at, :] = jnp.zeros((GROUP * 8, 128), jnp.float32)

        @pl.loop(0, turns)
        def _(g):
            for i in range(GROUP):
                block = order_ref[start + g * GROUP + i]
                at = pl.ds(pl.multiple_of(block * 2 * tiles, 2 * tiles), 2 * tiles)
                gathered[pl.ds(i, 2 * tiles, stride=GROUP), :] = uv_ref[at, :]
                gathered[pl.ds(2 * tiles * GROUP + i, 2 * tiles, stride=GROUP), :] = res_ref[at, :]
            u, v, re, im = [
                wide(gathered, (k // 2) * 2 * tiles * GROUP + (k % 2) * GROUP, step=2 * GROUP)
                for k in range(4)
            ]

            def keep(k, value):
                for t in range(tiles):
                    dense[pl.ds((k * tiles + t) * GROUP, GROUP), :] = value[:, t * 128 : (t + 1) * 128]

            c, s = harmonics(u)
            fill_table(cos_u, sin_u, c, s)
            s8 = s[4] * side
            vr, vi = re * c[4] - im * s8, re * s8 + im * c[4]
            a, b, e, f = vr * c[3], vi * s[3], vi * c[3], vr * s[3]
            keep(0, a + b)
            keep(1, e - f)
            keep(2, a - b)
            keep(3, e + f)
            c, s = harmonics(v)
            fill_table(cos_v, sin_v, c, s)
            keep(4, c[3])
            keep(5, s[3])
            keep(6, c[4] * c[3] - s[4] * s[3])
            keep(7, s[4] * c[3] + c[4] * s[3])
            for quad in range(GROUP // QUAD):
                left, right = lefts.at[quad], rights.at[quad]
                for b in range(QUAD):
                    i = quad * QUAD + b

                    def spread(k):
                        return wide(dense, k * tiles * GROUP + i, stride=0)

                    def table(ref):
                        return wide(ref, i * GROUP, step=GROUP * GROUP)

                    fc, fs = table(cos_u), table(sin_u)
                    real, imag = [], []
                    for h in range(2):
                        wr, wi = spread(2 * h), spread(2 * h + 1)
                        real.append(fc * wr - fs * wi)
                        imag.append(fs * wr + fc * wi)
                    left[pl.ds(b * SUB, HALF), :] = pair(real)
                    left[pl.ds(b * SUB + HALF, HALF), :] = pair(imag)
                    gc, gs = table(cos_v), table(sin_v)
                    cos_rows, sin_rows = [None] * 4, [None] * 4
                    for h, (low, high) in enumerate(((1, 2), (0, 3))):
                        ch, sh = spread(4 + 2 * h), spread(5 + 2 * h)
                        p, q, r, x = gc * ch, gs * sh, gs * ch, gc * sh
                        cos_rows[low], cos_rows[high] = p + q, p - q
                        sin_rows[low], sin_rows[high] = r - x, r + x
                    for h in range(2):
                        at = b * SUB + h * HALF
                        right[pl.ds(at, HALF), :] = pair(cos_rows[2 * h : 2 * h + 2])
                        right[pl.ds(QUAD * SUB + at, HALF), :] = pair(sin_rows[2 * h : 2 * h + 2])
                product = lax.dot_general(
                    left[...], right[...], (((1,), (1,)), ((), ())), preferred_element_type=jnp.float32
                )
                for b in range(QUAD):
                    mine = product[b * SUB : (b + 1) * SUB]
                    with_cos, with_sin = mine[:, :128], mine[:, 128:]
                    real = with_cos[:HALF] - with_sin[HALF:]
                    imag = with_cos[HALF:] + with_sin[:HALF]
                    parts = (real[:GROUP], real[GROUP:], imag[:GROUP], imag[GROUP:])
                    total = None
                    for k in range(4):
                        moved = parts[k]
                        if k != b:
                            moved = pltpu.roll(moved, ((k - b) % 4) * SUB, 1)
                        total = moved if total is None else jnp.where(lane == k, moved, total)
                    row = g * GROUP + quad * QUAD + b
                    stage[pl.ds(pl.multiple_of(row * 8, 8), 8), :] = total

        for i in range(capacity // 16):
            for k in range(8):
                piece = stage[pl.ds(i * 128 + k, 16, stride=8), :]
                at = pl.ds(pl.multiple_of(index * capacity + i * 16, 16), 16)
                out_ref[at, pl.ds(k * 128, 128)] = piece.astype(jnp.bfloat16)

    destinations = out_ref.shape[0] // capacity
    if destinations == 1:
        serve(0)
    else:
        pl.loop(0, destinations)(serve)


def make_subgrids(first, destinations, capacity, order, start, side, uv, res, vis):
    rows = destinations * capacity
    tiles = vis // 128
    vmem = pl.BlockSpec(memory_space=pltpu.VMEM)
    smem = pl.BlockSpec(memory_space=pltpu.SMEM)
    table = pltpu.VMEM((GROUP * GROUP * tiles, 128), jnp.float32)
    return pl.pallas_call(
        functools.partial(subgrid_kernel, first, capacity),
        out_shape=jax.ShapeDtypeStruct((rows, FEATURE), jnp.bfloat16),
        in_specs=[smem, smem, smem, vmem, vmem],
        out_specs=vmem,
        scratch_shapes=[
            pltpu.VMEM((4 * tiles * GROUP, 128), jnp.float32),
            table, table, table, table,
            pltpu.VMEM((8 * tiles * GROUP, 128), jnp.float32),
            pltpu.VMEM((GROUP // QUAD, QUAD * SUB, vis), jnp.bfloat16),
            pltpu.VMEM((GROUP // QUAD, 2 * QUAD * SUB, vis), jnp.bfloat16),
            pltpu.VMEM((capacity * 8, 128), jnp.float32),
        ],
        compiler_params=pltpu.CompilerParams(vmem_limit_bytes=VMEM_LIMIT),
        cost_estimate=pl.CostEstimate(
            flops=rows * 4 * SUB * SUB * vis, bytes_accessed=8 * rows * FEATURE, transcendentals=0
        ),
        name="subgrids",
    )(order, start, side, uv, res)


def gather_kernel(slot_ref, *refs):
    x_refs, (out_ref, hot, part) = refs[:-3], refs[-3:]
    lane = lax.broadcasted_iota(jnp.int32, (GROUP, 128), 1) // SUB
    wanted = lax.broadcasted_iota(jnp.int32, hot.shape, 0)
    wanted = (wanted % 32) * 4 + wanted // 32
    hot[...] = jnp.where(slot_ref[...] == wanted, 1.0, 0.0).astype(jnp.bfloat16)
    for k in range(8):
        total, at = None, 0
        for x_ref in x_refs:
            term = jnp.dot(
                hot[:, pl.ds(at, x_ref.shape[0])], x_ref[:, pl.ds(k * 128, 128)],
                preferred_element_type=jnp.float32,
            )
            total = term if total is None else total + term
            at += x_ref.shape[0]
        part[...] = total
        for grp in range(4):
            given = [part[pl.ds(32 * jl + 8 * grp, 8), :] for jl in range(4)]
            for a in range(4):
                total = None
                for jl in range(4):
                    moved = given[jl]
                    if a != jl:
                        moved = pltpu.roll(moved, ((jl - a) % 4) * SUB, 1)
                    total = moved if total is None else jnp.where(lane == jl, moved, total)
                p = (a % 2) * 8 + k
                out_ref[pl.ds(p * 64 + grp * 16 + a // 2, 8, stride=2), :] = total


def sum_slots(slots, arrived):
    vmem = pl.BlockSpec(memory_space=pltpu.VMEM)
    return pl.pallas_call(
        gather_kernel,
        out_shape=jax.ShapeDtypeStruct((HALF * 64, 128), jnp.float32),
        in_specs=[vmem] * (1 + len(arrived)),
        out_specs=vmem,
        scratch_shapes=[
            pltpu.VMEM((SLOTS, slots.shape[1]), jnp.bfloat16),
            pltpu.VMEM((SLOTS, 128), jnp.float32),
        ],
        compiler_params=pltpu.CompilerParams(vmem_limit_bytes=VMEM_LIMIT),
        name="sum_slots",
    )(slots, *arrived)


def rows_of(array):
    blocks, parts, vis = array.shape
    tiles = vis // 128
    split = array.reshape(blocks, parts, tiles, 128)
    return split.transpose(0, 2, 1, 3).reshape(blocks * tiles * parts, 128)


def local(residual, uv_offsets, counts, tile_of_block, slot_of_block, owner_map):
    blocks, _, vis = uv_offsets.shape
    owners = owner_map.shape[0]
    capacity = -(-max(CAP_MIN, 2 * blocks // owners) // 16) * 16
    core = lax.axis_index("samp")
    me = lax.axis_index(("blk", "tile"))
    swap = [(0, 1), (1, 0)]
    own = residual[0]
    other = lax.ppermute(own, "samp", swap)

    tile_ids = tile_of_block[:, 0]
    owner_range = jnp.arange(owners, dtype=jnp.int32)
    owner_ids = jnp.sum(
        jnp.where(tile_ids[:, None] == owner_range[None, :], owner_map[None, :], 0), 1
    )
    paired = owners <= PAIRED_MAX and owners & (owners - 1) == 0
    offset = (owners - 1) - jnp.bitwise_xor(owner_ids, me) if paired else owner_ids
    index = jnp.arange(blocks, dtype=jnp.int32)
    same = offset[None, :] == offset[:, None]
    rank = jnp.sum((same & (index[None, :] < index[:, None])).astype(jnp.int32), 1)
    start = jnp.sum(
        (offset[None, :] < jnp.arange(owners + 1, dtype=jnp.int32)[:, None]).astype(jnp.int32), 1
    )
    before = jnp.sum((offset[None, :] < offset[:, None]).astype(jnp.int32), 1)
    place = before + rank
    wanted = jnp.arange(blocks + GROUP, dtype=jnp.int32)
    order = jnp.sum(jnp.where(place[None, :] == wanted[:, None], index[None, :], 0), 1)
    target = offset * capacity + rank
    wanted = jnp.arange(owners * capacity, dtype=jnp.int32)
    slots = jnp.sum(
        jnp.where(target[None, :] == wanted[:, None], slot_of_block[None, :] + 1, 0), 1
    )
    slots = jnp.where(slots > 0, slots - 1, SLOTS).reshape(owners, 1, capacity)

    live = jnp.arange(vis, dtype=jnp.int32)[None, None, :] < counts[:, None, None]
    both = own.astype(jnp.float32) + other.astype(jnp.float32)
    both = rows_of(jnp.where(live, both, 0.0))
    uv = rows_of(uv_offsets)
    side = (2 * core - 1).astype(jnp.int32).reshape(1)
    subgrids = functools.partial(
        make_subgrids, capacity=capacity, order=order, start=start, side=side, uv=uv, res=both, vis=vis
    )
    if paired:
        arrived, arrived_slots = [], []
        for turn in range(owners):
            distance = owners - 1 - turn
            rows = subgrids(turn, 1)
            row_slots = slots[turn]
            if distance:
                pairs = [(k, k ^ distance) for k in range(owners)]
                rows = lax.ppermute(rows, ("blk", "tile"), pairs)
                row_slots = lax.ppermute(row_slots, ("blk", "tile"), pairs)
            arrived.append(rows)
            arrived_slots.append(row_slots)
        arrived_slots = jnp.concatenate(arrived_slots, 1)
    else:
        move = functools.partial(
            lax.all_to_all, axis_name=("blk", "tile"), split_axis=0, concat_axis=0, tiled=True
        )
        rows = subgrids(0, owners).reshape(owners, capacity, FEATURE)
        arrived = [move(rows).reshape(owners * capacity, FEATURE)]
        arrived_slots = move(slots).reshape(1, owners * capacity)
    half = sum_slots(arrived_slots, arrived)
    half = half.reshape(HALF, SLOTS // 4, 2, 128).transpose(0, 2, 1, 3).reshape(HALF, 2, SLOTS * SUB)
    theirs = lax.ppermute(half, "samp", swap)
    return jnp.where(
        core == 0,
        jnp.concatenate([half, theirs], 0),
        jnp.concatenate([theirs, half], 0),
    )


def solution(mesh):
    in_specs = (
        P("samp", ("cuts", "blk", "tile"), None, None),
        P(("cuts", "blk", "tile"), None, None),
        P(("cuts", "blk", "tile")),
        P(("cuts", "blk", "tile"), None),
        P(("cuts", "blk", "tile")),
        P(),
    )
    out_specs = P(("cuts", "blk", "tile"), None, None)
    return jax.shard_map(local, mesh=mesh, in_specs=in_specs, out_specs=out_specs, check_vma=False)
```

time: 73 us -> 68.9 us (0.944)
  blocking collectives: 32 us -> 0 us
  starting transfers between devices: 7.84 us -> 26.5 us
  Pallas kernels: 22 us -> 26.6 us
  waiting for transfers between devices: 1.9 us -> 5.03 us
  other arithmetic: 3.6 us -> 4.48 us
    all_gather x1 -> x0, blocking collectives: 32 us -> none  [local(): codes = lax.all_gather(code, ('blk', 'tile'), axis=0, tiled=False)]
    ppermute x0 -> x14, starting transfers between devices: none -> 25.9 us  [the longest x7 14.8 us: local(): rows = lax.ppermute(rows, ('blk', 'tile'), pairs)]
    all_to_all x1 -> x0, starting transfers between devices: 7.25 us -> none  [local(): lax.all_to_all(outgoing.reshape(owners, capacity, FEATURE), ('blk', 'tile...]
    pallas_call x1 -> x8, Pallas kernels: 21.3 us -> 24.7 us  [make_subgrids(): pl.pallas_call(functools.partial(subgrid_kernel, first, capacity), out_sh...]
    ppermute x0 -> x14, waiting for transfers between devices: none -> 3.13 us  [the longest x7 3.12 us: local(): rows = lax.ppermute(rows, ('blk', 'tile'), pairs)]
    select_n x2, other arithmetic: 0.18 us -> 2.06 us  [the longest x1 2.05 us: local(): both = rows_of(jnp.where(live, both, 0.0))]
    unnamed x13 -> x24, local copies, waits for them, and re-layouts: 2.96 us -> 4.23 us
    another operation x4 -> x0, other arithmetic: 1.24 us -> none
  transfers between devices with their start and end apart: 3 -> 16, of which waited for: 1 -> 3; matrix products, arithmetic and copies ran while one was open for 5% -> 3% of each run, Pallas kernels for 0% -> 26%
where the time goes in v2:
time: 68.9 us; the launch traced here: 67.9 us
  Pallas kernels  26.6 us (39%)
  starting transfers between devices  26.5 us (38%)
  local copies, waits for them, and re-layouts  5.11 us (7%)
  waiting for transfers between devices  5.03 us (7%)
  other arithmetic  4.48 us (7%)
    pallas_call x8, Pallas kernels, make_subgrids(): pl.pallas_call(functools.partial(subgrid_kernel, first, capacity), out_sh...  24.7 us
    ppermute x7, starting transfers between devices, local(): rows = lax.ppermute(rows, ('blk', 'tile'), pairs)  14.8 us
    ppermute x7, starting transfers between devices, local(): row_slots = lax.ppermute(row_slots, ('blk', 'tile'), pairs)  11.1 us
    unnamed x24, local copies, waits for them, and re-layouts  4.23 us
    ppermute x7, waiting for transfers between devices, local(): rows = lax.ppermute(rows, ('blk', 'tile'), pairs)  3.12 us
    select_n x1, other arithmetic, local(): both = rows_of(jnp.where(live, both, 0.0))  2.05 us
    ppermute x1, waiting for transfers between devices, local(): theirs = lax.ppermute(half, 'samp', swap)  1.89 us
    pallas_call x1, Pallas kernels, sum_slots(): pl.pallas_call(gather_kernel, out_shape=jax.ShapeDtypeStruct((HALF * 64,...  1.84 us
  transfers between devices with their start and end apart: 16, of which 3 were waited for; matrix products, arithmetic and copies ran while one was open for 3% of the time, Pallas kernels for 26%

profile of v2, /device:TPU:0, one launch (start us, length us, event | category | flops | bytes accessed | tf_op | source)
XLA Modules:
  0.0 67.9 jit_solution(16057979452929486482)
XLA Ops:
  0.0 0.5 collective-permute-start.7
  0.5 0.7 copy-done.3
  1.1 0.1 select_reduce_fusion.2
  1.2 0.2 convert_reduce_fusion
  1.5 0.0 copy-start.2
  1.5 0.7 copy-done.2
  2.1 0.1 select_reduce_fusion.1.order_ref
  2.3 0.2 select_reduce_fusion
  2.4 0.1 convert_reduce_fusion.2.start_ref
  2.6 0.7 copy-done.1
  3.2 0.1 iota_compare_fusion
  3.4 0.0 copy-start
  3.4 2.1 %add_select_fusion = f32[256,2,512]{2,1,0:T(2,128)S(1)} fusion(bf16[256,2,512]{2,1,0:T(2,128)(2,1)S(1)} %collective-permute-done.7, pred[256,512]{1,0:T(8,128)(4,1)S(1)} %iota_compare_fusion, bf16[1,256,2,512]{3,2,1,0:T(2,128)(2,1)} %param.6), kind=kLoop, calls=%fused_computation.1 | loop fusion | flops 1048576 | bytes 2228224 | tf_op jit(solution)/shard_map/jit(_where)/select_n | solution.py:297
  5.5 5.0 %subgrids.9 = bf16[64,1024]{1,0:T(8,128)(2,1)S(1)} custom-call(s32[264]{0:T(512)S(1)} %select_reduce_fusion.1.order_ref, s32[9]{0:T(128)S(1)} %convert_reduce_fusion.2.start_ref, s32[1]{0:T(128)} %bitcast.9.side_ref, f32[2048,128]{1,0:T(8,128)S(1)} %bitcast.43, f32[2048,128]{1,0:T(8,128)S(1)} %bitcast.35), custom_call_target="tpu_custom_call" | custom-call | flops 134217728 | bytes 524288 | tf_op jit(solution)/shard_map/subgrids/pallas_call | solution.py:188
  10.5 2.3 %subgrids.8 = bf16[64,1024]{1,0:T(8,128)(2,1)S(1)} custom-call(s32[264]{0:T(512)S(1)} %select_reduce_fusion.1.order_ref, s32[9]{0:T(128)S(1)} %convert_reduce_fusion.2.start_ref, s32[1]{0:T(128)} %bitcast.9.side_ref, f32[2048,128]{1,0:T(8,128)S(1)} %bitcast.44, f32[2048,128]{1,0:T(8,128)S(1)} %bitcast.36), custom_call_target="tpu_custom_call" | custom-call | flops 134217728 | bytes 524288 | tf_op jit(solution)/shard_map/subgrids/pallas_call | solution.py:188
  12.8 4.0 %collective-permute-start.8 = (bf16[64,1024]{1,0:T(8,128)(2,1)S(1)}, bf16[64,1024]{1,0:T(8,128)(2,1)S(1)}, u32[]{:S(2)}, u32[]{:S(2)}) collective-permute-start(bf16[64,1024]{1,0:T(8,128)(2,1)S(1)} %subgrids.8), channel_id=1, source_target_pairs={{0,7},{1,6},{2,5},{3,4},{4,3},{5,2},{6,1},{7,0},{8,15},{9,14},{10,... | collective-permute-start | bytes 393224 | tf_op jit(solution)/shard_map/ppermute | solution.py:311
  16.7 1.8 %collective-permute-start.9 = (bf16[64,1024]{1,0:T(8,128)(2,1)S(1)}, bf16[64,1024]{1,0:T(8,128)(2,1)S(1)}, u32[]{:S(2)}, u32[]{:S(2)}) collective-permute-start(bf16[64,1024]{1,0:T(8,128)(2,1)S(1)} %subgrids.9), channel_id=1, source_target_pairs={{0,6},{1,7},{2,4},{3,5},{4,2},{5,3},{6,0},{7,1},{8,14},{9,15},{10,... | collective-permute-start | bytes 393224 | tf_op jit(solution)/shard_map/ppermute | solution.py:311
  18.6 0.1 slice_bitcast_fusion
  18.6 0.0 collective-permute-start.6
  18.7 0.1 collective-permute-start.5
  18.7 3.4 %collective-permute-start.4 = (s32[1,64]{1,0:T(1,128)S(1)}, s32[1,64]{1,0:T(1,128)S(1)}, u32[]{:S(2)}, u32[]{:S(2)}) collective-permute-start(s32[1,64]{1,0:T(1,128)S(1)} %get-tuple-element.10), channel_id=1, source_target_pairs={{0,3},{1,2},{2,1},{3,0},{4,7},{5,6},{6,5},{7,4},{8,11},{9,10},{10,... | collective-permute-start | bytes 776 | tf_op jit(solution)/shard_map/ppermute | solution.py:312
  22.1 2.3 %subgrids.14 = bf16[64,1024]{1,0:T(8,128)(2,1)S(1)} custom-call(s32[264]{0:T(512)S(1)} %select_reduce_fusion.1.order_ref, s32[9]{0:T(128)S(1)} %convert_reduce_fusion.2.start_ref, s32[1]{0:T(128)} %bitcast.9.side_ref, f32[2048,128]{1,0:T(8,128)S(1)} %bitcast.45, f32[2048,128]{1,0:T(8,128)S(1)} %bitcast.37), custom_call_target="tpu_custom_call" | custom-call | flops 134217728 | bytes 524288 | tf_op jit(solution)/shard_map/subgrids/pallas_call | solution.py:188
  24.4 2.8 %subgrids.13 = bf16[64,1024]{1,0:T(8,128)(2,1)S(1)} custom-call(s32[264]{0:T(512)S(1)} %select_reduce_fusion.1.order_ref, s32[9]{0:T(128)S(1)} %convert_reduce_fusion.2.start_ref, s32[1]{0:T(128)} %bitcast.9.side_ref, f32[2048,128]{1,0:T(8,128)S(1)} %bitcast.46, f32[2048,128]{1,0:T(8,128)S(1)} %bitcast.38), custom_call_target="tpu_custom_call" | custom-call | flops 134217728 | bytes 524288 | tf_op jit(solution)/shard_map/subgrids/pallas_call | solution.py:188
  27.2 2.3 %subgrids.12 = bf16[64,1024]{1,0:T(8,128)(2,1)S(1)} custom-call(s32[264]{0:T(512)S(1)} %select_reduce_fusion.1.order_ref, s32[9]{0:T(128)S(1)} %convert_reduce_fusion.2.start_ref, s32[1]{0:T(128)} %bitcast.9.side_ref, f32[2048,128]{1,0:T(8,128)S(1)} %bitcast.47, f32[2048,128]{1,0:T(8,128)S(1)} %bitcast.39), custom_call_target="tpu_custom_call" | custom-call | flops 134217728 | bytes 524288 | tf_op jit(solution)/shard_map/subgrids/pallas_call | solution.py:188
  29.5 5.0 %subgrids.11 = bf16[64,1024]{1,0:T(8,128)(2,1)S(1)} custom-call(s32[264]{0:T(512)S(1)} %select_reduce_fusion.1.order_ref, s32[9]{0:T(128)S(1)} %convert_reduce_fusion.2.start_ref, s32[1]{0:T(128)} %bitcast.9.side_ref, f32[2048,128]{1,0:T(8,128)S(1)} %bitcast.48, f32[2048,128]{1,0:T(8,128)S(1)} %bitcast.40), custom_call_target="tpu_custom_call" | custom-call | flops 134217728 | bytes 524288 | tf_op jit(solution)/shard_map/subgrids/pallas_call | solution.py:188
  34.5 0.0 collective-permute-done.6
  34.5 0.6 copy-done.5
  35.1 1.1 %collective-permute-start.3 = (s32[1,64]{1,0:T(1,128)S(1)}, s32[1,64]{1,0:T(1,128)S(1)}, u32[]{:S(2)}, u32[]{:S(2)}) collective-permute-start(s32[1,64]{1,0:T(1,128)S(1)} %get-tuple-element.11), channel_id=1, source_target_pairs={{0,4},{1,5},{2,6},{3,7},{4,0},{5,1},{6,2},{7,3},{8,12},{9,13},{10,... | collective-permute-start | bytes 776 | tf_op jit(solution)/shard_map/ppermute | solution.py:312
  36.2 0.0 collective-permute-done.5
  36.2 0.5 copy-done.6
  36.7 1.1 %collective-permute-start.2 = (s32[1,64]{1,0:T(1,128)S(1)}, s32[1,64]{1,0:T(1,128)S(1)}, u32[]{:S(2)}, u32[]{:S(2)}) collective-permute-start(s32[1,64]{1,0:T(1,128)S(1)} %get-tuple-element.12), channel_id=1, source_target_pairs={{0,5},{1,4},{2,7},{3,6},{4,1},{5,0},{6,3},{7,2},{8,13},{9,12},{10,... | collective-permute-start | bytes 776 | tf_op jit(solution)/shard_map/ppermute | solution.py:312
  37.8 0.6 copy-done.7
  38.4 3.9 %collective-permute-start.1 = (s32[1,64]{1,0:T(1,128)S(1)}, s32[1,64]{1,0:T(1,128)S(1)}, u32[]{:S(2)}, u32[]{:S(2)}) collective-permute-start(s32[1,64]{1,0:T(1,128)S(1)} %get-tuple-element.13), channel_id=1, source_target_pairs={{0,6},{1,7},{2,4},{3,5},{4,2},{5,3},{6,0},{7,1},{8,14},{9,15},{10,... | collective-permute-start | bytes 776 | tf_op jit(solution)/shard_map/ppermute | solution.py:312
  42.3 0.5 copy-done.8
  42.8 1.6 %collective-permute-start = (s32[1,64]{1,0:T(1,128)S(1)}, s32[1,64]{1,0:T(1,128)S(1)}, u32[]{:S(2)}, u32[]{:S(2)}) collective-permute-start(s32[1,64]{1,0:T(1,128)S(1)} %get-tuple-element.14), channel_id=1, source_target_pairs={{0,7},{1,6},{2,5},{3,4},{4,3},{5,2},{6,1},{7,0},{8,15},{9,14},{10,... | collective-permute-start | bytes 776 | tf_op jit(solution)/shard_map/ppermute | solution.py:312
  44.4 1.7 %subgrids.10 = bf16[64,1024]{1,0:T(8,128)(2,1)S(1)} custom-call(s32[264]{0:T(512)S(1)} %select_reduce_fusion.1.order_ref, s32[9]{0:T(128)S(1)} %convert_reduce_fusion.2.start_ref, s32[1]{0:T(128)} %bitcast.9.side_ref, f32[2048,128]{1,0:T(8,128)S(1)} %bitcast.49, f32[2048,128]{1,0:T(8,128)S(1)} %bitcast.41), custom_call_target="tpu_custom_call" | custom-call | flops 134217728 | bytes 524288 | tf_op jit(solution)/shard_map/subgrids/pallas_call | solution.py:188
  46.2 2.0 %collective-permute-start.10 = (bf16[64,1024]{1,0:T(8,128)(2,1)S(1)}, bf16[64,1024]{1,0:T(8,128)(2,1)S(1)}, u32[]{:S(2)}, u32[]{:S(2)}) collective-permute-start(bf16[64,1024]{1,0:T(8,128)(2,1)S(1)} %subgrids.10), channel_id=1, source_target_pairs={{0,5},{1,4},{2,7},{3,6},{4,1},{5,0},{6,3},{7,2},{8,13},{9,12},{10,... | collective-permute-start | bytes 393224 | tf_op jit(solution)/shard_map/ppermute | solution.py:311
  48.2 3.5 %collective-permute-start.11 = (bf16[64,1024]{1,0:T(8,128)(2,1)S(1)}, bf16[64,1024]{1,0:T(8,128)(2,1)S(1)}, u32[]{:S(2)}, u32[]{:S(2)}) collective-permute-start(bf16[64,1024]{1,0:T(8,128)(2,1)S(1)} %subgrids.11), channel_id=1, source_target_pairs={{0,4},{1,5},{2,6},{3,7},{4,0},{5,1},{6,2},{7,3},{8,12},{9,13},{10,... | collective-permute-start | bytes 393224 | tf_op jit(solution)/shard_map/ppermute | solution.py:311
  51.7 0.4 collective-permute-start.13
  52.1 3.1 %collective-permute-start.14 = (bf16[64,1024]{1,0:T(8,128)(2,1)S(1)}, bf16[64,1024]{1,0:T(8,128)(2,1)}, u32[]{:S(2)}, u32[]{:S(2)}) collective-permute-start(bf16[64,1024]{1,0:T(8,128)(2,1)S(1)} %subgrids.14), channel_id=1, source_target_pairs={{0,1},{1,0},{2,3},{3,2},{4,5},{5,4},{6,7},{7,6},{8,9},{9,8},{10,11... | collective-permute-start | bytes 393224 | tf_op jit(solution)/shard_map/ppermute | solution.py:311
  55.2 0.8 %concatenate.9.slot_ref = s32[1,512]{1,0:T(1,128)S(1)} concatenate(s32[1,64]{1,0:T(1,128)} %copy-done.11, s32[1,64]{1,0:T(1,128)} %copy-done.10, s32[1,64]{1,0:T(1,128)} %copy-done.9, s32[1,64]{1,0:T(1,128)} %copy-done.8, s32[1,64]{1,0:T(1,128)} %copy-done.7, s32[1,64]{1,0:T(1,128)} %copy-done.6, s32[1,64]{1,0:T(1,128)} %copy-done.5, s32[1,64]{1,0:T(1,128)S(1)} %get-tuple-element.7), dimensions={1} | concatenate | bytes 4096 | tf_op jit(solution)/shard_map/concatenate | solution.py:315
  56.0 3.4 %subgrids.15.refs_7_ = bf16[64,1024]{1,0:T(8,128)(2,1)S(1)} custom-call(s32[264]{0:T(512)S(1)} %select_reduce_fusion.1.order_ref, s32[9]{0:T(128)S(1)} %convert_reduce_fusion.2.start_ref, s32[1]{0:T(128)} %bitcast.9.side_ref, f32[2048,128]{1,0:T(8,128)S(1)} %bitcast.50, f32[2048,128]{1,0:T(8,128)S(1)} %bitcast.42), custom_call_target="tpu_custom_call" | custom-call | flops 134217728 | bytes 524288 | tf_op jit(solution)/shard_map/subgrids/pallas_call | solution.py:188
  59.4 1.9 %collective-permute-done.11.refs_3_ = bf16[64,1024]{1,0:T(8,128)(2,1)S(1)} collective-permute-done((bf16[64,1024]{1,0:T(8,128)(2,1)S(1)}, bf16[64,1024]{1,0:T(8,128)(2,1)S(1)}, u32[]{:S(2)}, u32[]{:S(2)}) %collective-permute-start.11) | collective-permute-done | bytes 131104 | tf_op jit(solution)/shard_map/ppermute | solution.py:311
  61.2 1.2 %collective-permute-done.12.refs_4_ = bf16[64,1024]{1,0:T(8,128)(2,1)S(1)} collective-permute-done((bf16[64,1024]{1,0:T(8,128)(2,1)S(1)}, bf16[64,1024]{1,0:T(8,128)(2,1)S(1)}, u32[]{:S(2)}, u32[]{:S(2)}) %collective-permute-start.12) | collective-permute-done | bytes 131104 | tf_op jit(solution)/shard_map/ppermute | solution.py:311
  62.5 1.8 %sum_slots.1 = f32[1024,128]{1,0:T(8,128)S(1)} custom-call(s32[1,512]{1,0:T(1,128)S(1)} %concatenate.9.slot_ref, bf16[64,1024]{1,0:T(8,128)(2,1)S(1)} %collective-permute-done.8.refs_0_, bf16[64,1024]{1,0:T(8,128)(2,1)S(1)} %collective-permute-done.9.refs_1_, bf16[64,1024]{1,0:T(8,128)(2,1)S(1)} %collective-permute-done.10.refs_2_, ...), custom_call_target="tpu_custom_call" | custom-call | tf_op jit(solution)/shard_map/sum_slots/pallas_call | solution.py:240
  64.3 0.1 collective-permute-start.15
  64.4 1.9 %collective-permute-done.15 = f32[16,2,4096]{2,1,0:T(2,128)S(1)} collective-permute-done((f32[16,2,4096]{2,1,0:T(2,128)S(1)}, f32[16,2,4096]{2,1,0:T(2,128)S(1)}, u32[]{:S(2)}, u32[]{:S(2)}) %collective-permute-start.15) | collective-permute-done | bytes 524320 | tf_op jit(solution)/shard_map/ppermute | solution.py:325
  66.3 1.5 %maximum_select_fusion = f32[32,2,4096]{2,1,0:T(2,128)} fusion(f32[16,2,4096]{2,1,0:T(2,128)S(1)} %collective-permute-done.15, f32[16,2,4096]{2,1,0:T(2,128)S(1)} %bitcast.52, pred[]{:T(512)S(6)} %eq.28), kind=kLoop, calls=%fused_computation | loop fusion | flops 786432 | bytes 2097153 | tf_op jit(solution)/shard_map/jit(_where)/select_n | solution.py:326
  (30 shorter events, 0.1 us)
Async XLA Ops:
  0.0 3.4 %collective-permute-start.7 = (bf16[256,2,512]{2,1,0:T(2,128)(2,1)}, bf16[256,2,512]{2,1,0:T(2,128)(2,1)S(1)}, u32[]{:S(2)}, u32[]{:S(2)}) collective-permute-start(bf16[256,2,512]{2,1,0:T(2,128)(2,1)} %bitcast.53), channel_id=1, source_target_pairs={{0,8},{8,0},{1,9},{9,1},{2,10},{10,2},{3,11},{11,3},{4,12},{12,4},... | collective-permute-start | bytes 1572872 | tf_op jit(solution)/shard_map/ppermute | solution.py:269
  0.5 0.7 %copy-start.3 = (s32[256,1]{0,1:T(1,128)S(1)}, s32[256,1]{0,1:T(1,128)}, u32[]{:S(2)}) copy-start(s32[256,1]{0,1:T(1,128)} %param.9) | copy-start | bytes 3076
  0.5 0.7 %copy-start.4 = (s32[8]{0:T(128)S(1)}, s32[8]{0:T(128)}, u32[]{:S(2)}) copy-start(s32[8]{0:T(128)} %param.11) | copy-start | bytes 100
  1.5 0.7 %copy-start.2 = (s32[256]{0:T(256)S(1)}, s32[256]{0:T(256)}, u32[]{:S(2)}) copy-start(s32[256]{0:T(256)} %param.10) | copy-start | bytes 3076
  2.6 0.7 %copy-start.1 = (s32[256]{0:T(256)S(1)}, s32[256]{0:T(256)}, u32[]{:S(2)}) copy-start(s32[256]{0:T(256)} %param.8) | copy-start | bytes 3076
  3.4 2.1 %copy-start = (f32[256,2,512]{2,1,0:T(2,128)S(1)}, f32[256,2,512]{2,1,0:T(2,128)}, u32[]{:S(2)}) copy-start(f32[256,2,512]{2,1,0:T(2,128)} %param.7) | copy-start | bytes 3145732
  12.8 38.9 %collective-permute-start.8 = (bf16[64,1024]{1,0:T(8,128)(2,1)S(1)}, bf16[64,1024]{1,0:T(8,128)(2,1)S(1)}, u32[]{:S(2)}, u32[]{:S(2)}) collective-permute-start(bf16[64,1024]{1,0:T(8,128)(2,1)S(1)} %subgrids.8), channel_id=1, source_target_pairs={{0,7},{1,6},{2,5},{3,4},{4,3},{5,2},{6,1},{7,0},{8,15},{9,14},{10,... | collective-permute-start | bytes 393224 | tf_op jit(solution)/shard_map/ppermute | solution.py:311
  16.7 35.4 %collective-permute-start.9 = (bf16[64,1024]{1,0:T(8,128)(2,1)S(1)}, bf16[64,1024]{1,0:T(8,128)(2,1)S(1)}, u32[]{:S(2)}, u32[]{:S(2)}) collective-permute-start(bf16[64,1024]{1,0:T(8,128)(2,1)S(1)} %subgrids.9), channel_id=1, source_target_pairs={{0,6},{1,7},{2,4},{3,5},{4,2},{5,3},{6,0},{7,1},{8,14},{9,15},{10,... | collective-permute-start | bytes 393224 | tf_op jit(solution)/shard_map/ppermute | solution.py:311
  18.6 15.9 %collective-permute-start.6 = (s32[1,64]{1,0:T(1,128)S(1)}, s32[1,64]{1,0:T(1,128)S(1)}, u32[]{:S(2)}, u32[]{:S(2)}) collective-permute-start(s32[1,64]{1,0:T(1,128)S(1)} %get-tuple-element.8), channel_id=1, source_target_pairs={{0,1},{1,0},{2,3},{3,2},{4,5},{5,4},{6,7},{7,6},{8,9},{9,8},{10,11... | collective-permute-start | bytes 776 | tf_op jit(solution)/shard_map/ppermute | solution.py:312
  18.7 17.5 %collective-permute-start.5 = (s32[1,64]{1,0:T(1,128)S(1)}, s32[1,64]{1,0:T(1,128)S(1)}, u32[]{:S(2)}, u32[]{:S(2)}) collective-permute-start(s32[1,64]{1,0:T(1,128)S(1)} %get-tuple-element.9), channel_id=1, source_target_pairs={{0,2},{1,3},{2,0},{3,1},{4,6},{5,7},{6,4},{7,5},{8,10},{9,11},{10,... | collective-permute-start | bytes 776 | tf_op jit(solution)/shard_map/ppermute | solution.py:312
  18.7 19.0 %collective-permute-start.4 = (s32[1,64]{1,0:T(1,128)S(1)}, s32[1,64]{1,0:T(1,128)S(1)}, u32[]{:S(2)}, u32[]{:S(2)}) collective-permute-start(s32[1,64]{1,0:T(1,128)S(1)} %get-tuple-element.10), channel_id=1, source_target_pairs={{0,3},{1,2},{2,1},{3,0},{4,7},{5,6},{6,5},{7,4},{8,11},{9,10},{10,... | collective-permute-start | bytes 776 | tf_op jit(solution)/shard_map/ppermute | solution.py:312
  34.5 0.6 copy-start.5
  35.1 7.2 %collective-permute-start.3 = (s32[1,64]{1,0:T(1,128)S(1)}, s32[1,64]{1,0:T(1,128)S(1)}, u32[]{:S(2)}, u32[]{:S(2)}) collective-permute-start(s32[1,64]{1,0:T(1,128)S(1)} %get-tuple-element.11), channel_id=1, source_target_pairs={{0,4},{1,5},{2,6},{3,7},{4,0},{5,1},{6,2},{7,3},{8,12},{9,13},{10,... | collective-permute-start | bytes 776 | tf_op jit(solution)/shard_map/ppermute | solution.py:312
  36.2 0.5 copy-start.6
  36.7 9.5 %collective-permute-start.2 = (s32[1,64]{1,0:T(1,128)S(1)}, s32[1,64]{1,0:T(1,128)S(1)}, u32[]{:S(2)}, u32[]{:S(2)}) collective-permute-start(s32[1,64]{1,0:T(1,128)S(1)} %get-tuple-element.12), channel_id=1, source_target_pairs={{0,5},{1,4},{2,7},{3,6},{4,1},{5,0},{6,3},{7,2},{8,13},{9,12},{10,... | collective-permute-start | bytes 776 | tf_op jit(solution)/shard_map/ppermute | solution.py:312
  37.8 0.6 copy-start.7
  38.4 9.8 %collective-permute-start.1 = (s32[1,64]{1,0:T(1,128)S(1)}, s32[1,64]{1,0:T(1,128)S(1)}, u32[]{:S(2)}, u32[]{:S(2)}) collective-permute-start(s32[1,64]{1,0:T(1,128)S(1)} %get-tuple-element.13), channel_id=1, source_target_pairs={{0,6},{1,7},{2,4},{3,5},{4,2},{5,3},{6,0},{7,1},{8,14},{9,15},{10,... | collective-permute-start | bytes 776 | tf_op jit(solution)/shard_map/ppermute | solution.py:312
  42.3 0.5 copy-start.8
  42.8 8.9 %collective-permute-start = (s32[1,64]{1,0:T(1,128)S(1)}, s32[1,64]{1,0:T(1,128)S(1)}, u32[]{:S(2)}, u32[]{:S(2)}) collective-permute-start(s32[1,64]{1,0:T(1,128)S(1)} %get-tuple-element.14), channel_id=1, source_target_pairs={{0,7},{1,6},{2,5},{3,4},{4,3},{5,2},{6,1},{7,0},{8,15},{9,14},{10,... | collective-permute-start | bytes 776 | tf_op jit(solution)/shard_map/ppermute | solution.py:312
  46.2 9.0 %copy-start.9 = (s32[1,64]{1,0:T(1,128)}, s32[1,64]{1,0:T(1,128)S(1)}, u32[]{:S(2)}) copy-start(s32[1,64]{1,0:T(1,128)S(1)} %collective-permute-done.2) | copy-start | bytes 772
  46.2 13.2 %collective-permute-start.10 = (bf16[64,1024]{1,0:T(8,128)(2,1)S(1)}, bf16[64,1024]{1,0:T(8,128)(2,1)S(1)}, u32[]{:S(2)}, u32[]{:S(2)}) collective-permute-start(bf16[64,1024]{1,0:T(8,128)(2,1)S(1)} %subgrids.10), channel_id=1, source_target_pairs={{0,5},{1,4},{2,7},{3,6},{4,1},{5,0},{6,3},{7,2},{8,13},{9,12},{10,... | collective-permute-start | bytes 393224 | tf_op jit(solution)/shard_map/ppermute | solution.py:311
  48.2 7.0 %copy-start.10 = (s32[1,64]{1,0:T(1,128)}, s32[1,64]{1,0:T(1,128)S(1)}, u32[]{:S(2)}) copy-start(s32[1,64]{1,0:T(1,128)S(1)} %collective-permute-done.1) | copy-start | bytes 772
  48.2 13.0 %collective-permute-start.11 = (bf16[64,1024]{1,0:T(8,128)(2,1)S(1)}, bf16[64,1024]{1,0:T(8,128)(2,1)S(1)}, u32[]{:S(2)}, u32[]{:S(2)}) collective-permute-start(bf16[64,1024]{1,0:T(8,128)(2,1)S(1)} %subgrids.11), channel_id=1, source_target_pairs={{0,4},{1,5},{2,6},{3,7},{4,0},{5,1},{6,2},{7,3},{8,12},{9,13},{10,... | collective-permute-start | bytes 393224 | tf_op jit(solution)/shard_map/ppermute | solution.py:311
  51.7 3.5 %copy-start.11 = (s32[1,64]{1,0:T(1,128)}, s32[1,64]{1,0:T(1,128)S(1)}, u32[]{:S(2)}) copy-start(s32[1,64]{1,0:T(1,128)S(1)} %collective-permute-done) | copy-start | bytes 772
  51.7 10.8 %collective-permute-start.12 = (bf16[64,1024]{1,0:T(8,128)(2,1)S(1)}, bf16[64,1024]{1,0:T(8,128)(2,1)S(1)}, u32[]{:S(2)}, u32[]{:S(2)}) collective-permute-start(bf16[64,1024]{1,0:T(8,128)(2,1)S(1)} %subgrids.12), channel_id=1, source_target_pairs={{0,3},{1,2},{2,1},{3,0},{4,7},{5,6},{6,5},{7,4},{8,11},{9,10},{10,... | collective-permute-start | bytes 393224 | tf_op jit(solution)/shard_map/ppermute | solution.py:311
  51.7 10.8 %collective-permute-start.13 = (bf16[64,1024]{1,0:T(8,128)(2,1)S(1)}, bf16[64,1024]{1,0:T(8,128)(2,1)S(1)}, u32[]{:S(2)}, u32[]{:S(2)}) collective-permute-start(bf16[64,1024]{1,0:T(8,128)(2,1)S(1)} %subgrids.13), channel_id=1, source_target_pairs={{0,2},{1,3},{2,0},{3,1},{4,6},{5,7},{6,4},{7,5},{8,10},{9,11},{10,... | collective-permute-start | bytes 393224 | tf_op jit(solution)/shard_map/ppermute | solution.py:311
  52.1 10.4 %collective-permute-start.14 = (bf16[64,1024]{1,0:T(8,128)(2,1)S(1)}, bf16[64,1024]{1,0:T(8,128)(2,1)}, u32[]{:S(2)}, u32[]{:S(2)}) collective-permute-start(bf16[64,1024]{1,0:T(8,128)(2,1)S(1)} %subgrids.14), channel_id=1, source_target_pairs={{0,1},{1,0},{2,3},{3,2},{4,5},{5,4},{6,7},{7,6},{8,9},{9,8},{10,11... | collective-permute-start | bytes 393224 | tf_op jit(solution)/shard_map/ppermute | solution.py:311
  64.3 2.0 %collective-permute-start.15 = (f32[16,2,4096]{2,1,0:T(2,128)S(1)}, f32[16,2,4096]{2,1,0:T(2,128)S(1)}, u32[]{:S(2)}, u32[]{:S(2)}) collective-permute-start(f32[16,2,4096]{2,1,0:T(2,128)S(1)} %bitcast.51), channel_id=1, source_target_pairs={{0,8},{8,0},{1,9},{9,1},{2,10},{10,2},{3,11},{11,3},{4,12},{12,4},... | collective-permute-start | bytes 1572872 | tf_op jit(solution)/shard_map/ppermute | solution.py:325

commit v3 on v1

v3 whole, which is shorter than its diff:
```python
import functools

import jax
import jax.numpy as jnp
import numpy as np
from jax import lax
from jax.experimental import pallas as pl
from jax.experimental.pallas import tpu as pltpu
from jax.sharding import PartitionSpec as P

SUB = 32
HALF = SUB // 2
SLOTS = 128
LANES = 128
FEATURE = 2 * SUB * SUB
PIECES = FEATURE // LANES
WIDTH = FEATURE + LANES
CAP_MIN = 8
GROUP = 8
QUAD = 4
TABLES = 12
PAIRED_MAX = 16
VMEM_LIMIT = 48 * 1024 * 1024


def turn_coefficients():
    knots = np.cos(np.pi * (np.arange(400) + 0.5) / 400)
    cheb = np.polynomial.chebyshev
    even = cheb.cheb2poly(cheb.chebfit(knots, np.cos(np.pi * knots), 12))[0::2]
    odd = cheb.cheb2poly(cheb.chebfit(knots, np.sin(np.pi * knots), 13))[1::2]
    return [float(x) for x in even], [float(x) for x in odd]


COS_COEF, SIN_COEF = turn_coefficients()


def horner(coef, x):
    total = coef[-1] * x + coef[-2]
    for value in coef[-3::-1]:
        total = total * x + value
    return total


def harmonics(offset):
    y = offset * (1.0 / HALF)
    x = y * y
    c1, s1 = horner(COS_COEF, x), horner(SIN_COEF, x) * y
    c2, s2 = 1.0 - 2.0 * s1 * s1, 2.0 * s1 * c1
    c3, s3 = c2 * c1 - s2 * s1, s2 * c1 + c2 * s1
    c4, s4 = 1.0 - 2.0 * s2 * s2, 2.0 * s2 * c2
    c8, s8 = 1.0 - 2.0 * s4 * s4, 2.0 * s4 * c4
    c12, s12 = c8 * c4 - s8 * s4, s8 * c4 + c8 * s4
    return (c1, c2, c3, c4, c12), (s1, s2, s3, s4, s12)


def tile_of(value, t):
    return value[:, t * LANES : (t + 1) * LANES]


def fill_table(cos_ref, sin_ref, base, c, s):
    one = jnp.ones_like(c[0])
    cos_rows = (c[3], c[2], c[1], c[0], one, c[0], c[1], c[2])
    sin_rows = (-s[3], -s[2], -s[1], -s[0], jnp.zeros_like(one), s[0], s[1], s[2])
    for r in range(GROUP):
        for t in range(one.shape[1] // LANES):
            at = pl.ds(base + (t * GROUP * GROUP + r), GROUP, stride=GROUP)
            cos_ref[at, :] = tile_of(cos_rows[r], t)
            sin_ref[at, :] = tile_of(sin_rows[r], t)


def pair(halves):
    return jnp.concatenate(halves, 0).astype(jnp.bfloat16)


def subgrid_kernel(
    first, destinations, capacity, order_ref, row_ref, slot_ref, start_ref, uv_ref, res_ref, *refs
):
    out_refs, scratch = refs[:-12], refs[-12:]
    gathered, cos_u, sin_u, cos_v, sin_v, dense, left_a, right_a, left_b, right_b, stage, tags = scratch
    tiles = gathered.shape[0] // (4 * GROUP)
    rows = destinations * capacity
    lane = lax.broadcasted_iota(jnp.int32, (GROUP, LANES), 1) // SUB
    low, high = start_ref[first], start_ref[first + destinations]
    turns = (high - low + GROUP - 1) // GROUP
    last = order_ref.shape[0] - 1

    def wide(ref, row, stride=1, step=GROUP):
        return jnp.concatenate(
            [ref[pl.ds(row + t * step, GROUP, stride=stride), :] for t in range(tiles)], 1
        )

    def tabulate(g):
        for i in range(GROUP):
            block = order_ref[jnp.minimum(low + g * GROUP + i, last)]
            at = pl.ds(pl.multiple_of(block * 2 * tiles, 2 * tiles), 2 * tiles)
            gathered[pl.ds(i, 2 * tiles, stride=GROUP), :] = uv_ref[at, :]
            gathered[pl.ds(2 * tiles * GROUP + i, 2 * tiles, stride=GROUP), :] = res_ref[at, :]
        u, v, re, im = [
            wide(gathered, (k // 2) * 2 * tiles * GROUP + (k % 2) * GROUP, step=2 * GROUP)
            for k in range(4)
        ]
        table_at = pl.multiple_of(g * (tiles * GROUP * GROUP), tiles * GROUP * GROUP)

        def keep(k, value):
            base = pl.multiple_of(g * (TABLES * tiles * GROUP), TABLES * tiles * GROUP)
            for t in range(tiles):
                dense[pl.ds(base + (k * tiles + t) * GROUP, GROUP), :] = tile_of(value, t)

        c, s = harmonics(u)
        fill_table(cos_u, sin_u, table_at, c, s)
        for h in range(2):
            ch, sh = c[3 + h], s[3 + h]
            a, b, e, f = re * ch, im * sh, im * ch, re * sh
            keep(4 * h, a + b)
            keep(4 * h + 1, e - f)
            keep(4 * h + 2, a - b)
            keep(4 * h + 3, e + f)
        c, s = harmonics(v)
        fill_table(cos_v, sin_v, table_at, c, s)
        for h in range(2):
            keep(8 + 2 * h, c[3 + h])
            keep(9 + 2 * h, s[3 + h])

    def expand(g, quad, left, right):
        for b in range(QUAD):
            i = quad * QUAD + b

            def spread(k):
                base = pl.multiple_of(g * (TABLES * tiles * GROUP), TABLES * tiles * GROUP)
                return wide(dense, base + (k * tiles * GROUP + i), stride=0)

            def table(ref):
                base = pl.multiple_of(g * (tiles * GROUP * GROUP), tiles * GROUP * GROUP)
                return wide(ref, base + i * GROUP, step=GROUP * GROUP)

            fc, fs = table(cos_u), table(sin_u)
            real, imag = [None] * 4, [None] * 4
            for k, at in enumerate((1, 2, 0, 3)):
                wr, wi = spread(2 * k), spread(2 * k + 1)
                real[at] = fc * wr - fs * wi
                imag[at] = fs * wr + fc * wi
            gc, gs = table(cos_v), table(sin_v)
            cos_rows, sin_rows = [None] * 4, [None] * 4
            for h, (down, up) in enumerate(((1, 2), (0, 3))):
                ch, sh = spread(8 + 2 * h), spread(9 + 2 * h)
                p, q, r, x = gc * ch, gs * sh, gs * ch, gc * sh
                cos_rows[down], cos_rows[up] = p + q, p - q
                sin_rows[down], sin_rows[up] = r - x, r + x
            for h in range(2):
                two = slice(2 * h, 2 * h + 2)
                left[pl.ds(2 * b * SUB + h * HALF, HALF), :] = pair(real[two])
                left[pl.ds(2 * b * SUB + SUB + h * HALF, HALF), :] = pair(imag[two])
                right[pl.ds(b * SUB + h * HALF, HALF), :] = pair(cos_rows[two])
                right[pl.ds(QUAD * SUB + b * SUB + h * HALF, HALF), :] = pair(sin_rows[two])

    def multiply(left, right):
        return lax.dot_general(
            left[...], right[...], (((1,), (1,)), ((), ())), preferred_element_type=jnp.float32
        )

    def finish(product, turn):
        for b in range(QUAD):
            mine = product[2 * b * SUB : 2 * (b + 1) * SUB]
            with_cos, with_sin = mine[:, :LANES], mine[:, LANES:]
            index = low + turn * QUAD + b
            known = (index >= low) & (index < high)
            index = jnp.clip(index, 0, last)
            row = jnp.where(known, row_ref[index] - first * capacity, rows)
            for part in range(2):
                if part == 0:
                    whole = with_cos[:SUB] - with_sin[SUB:]
                else:
                    whole = with_cos[SUB:] + with_sin[:SUB]
                total = None
                for k in range(4):
                    moved = whole[k * GROUP : (k + 1) * GROUP]
                    if k != b:
                        moved = pltpu.roll(moved, ((k - b) % 4) * SUB, 1)
                    total = moved if total is None else jnp.where(lane == k, moved, total)
                stage[pl.ds(pl.multiple_of(row * PIECES, PIECES) + part * GROUP, GROUP), :] = total
            tag = (slot_ref[index] + 1).astype(jnp.float32)
            tags[pl.ds(row, 1), :] = jnp.full((1, LANES), tag, jnp.float32)

    @pl.loop(0, rows // GROUP)
    def _(i):
        at = pl.multiple_of(i * GROUP, GROUP)
        stage[pl.ds(at * PIECES, GROUP * PIECES), :] = jnp.zeros((GROUP * PIECES, LANES), jnp.float32)
        tags[pl.ds(at, GROUP), :] = jnp.zeros((GROUP, LANES), jnp.float32)

    pl.loop(0, turns)(tabulate)

    @pl.loop(0, turns)
    def _(g):
        product = multiply(left_b, right_b)
        expand(g, 0, left_a, right_a)
        finish(product, 2 * g - 1)
        product = multiply(left_a, right_a)
        expand(g, 1, left_b, right_b)
        finish(product, 2 * g)

    finish(multiply(left_b, right_b), 2 * turns - 1)

    at = 0
    for out_ref in out_refs:

        @pl.loop(0, out_ref.shape[0] // 16)
        def _(i):
            here = pl.multiple_of(i * 16, 16)
            for k in range(PIECES):
                piece = stage[pl.ds((at + here) * PIECES + k, 16, stride=PIECES), :]
                out_ref[pl.ds(here, 16), pl.ds(k * LANES, LANES)] = piece.astype(jnp.bfloat16)
            out_ref[pl.ds(here, 16), pl.ds(FEATURE, LANES)] = tags[pl.ds(at + here, 16), :].astype(
                jnp.bfloat16
            )

        at += out_ref.shape[0]


def make_subgrids(first, outs, capacity, order, row, slot, start, uv, res, vis):
    tiles = vis // LANES
    destinations = sum(outs)
    rows = destinations * capacity
    groups = min(rows, order.shape[0]) // GROUP + 1
    vmem = pl.BlockSpec(memory_space=pltpu.VMEM)
    smem = pl.BlockSpec(memory_space=pltpu.SMEM)
    table = pltpu.VMEM((groups * GROUP * GROUP * tiles, LANES), jnp.float32)
    quad = pltpu.VMEM((2 * QUAD * SUB, vis), jnp.bfloat16)
    return pl.pallas_call(
        functools.partial(subgrid_kernel, first, destinations, capacity),
        out_shape=[jax.ShapeDtypeStruct((n * capacity, WIDTH), jnp.bfloat16) for n in outs],
        in_specs=[smem, smem, smem, smem, vmem, vmem],
        out_specs=[vmem] * len(outs),
        scratch_shapes=[
            pltpu.VMEM((4 * tiles * GROUP, LANES), jnp.float32),
            table, table, table, table,
            pltpu.VMEM((groups * TABLES * tiles * GROUP, LANES), jnp.float32),
            quad, quad, quad, quad,
            pltpu.VMEM(((rows + 1) * PIECES, LANES), jnp.float32),
            pltpu.VMEM((rows + GROUP, LANES), jnp.float32),
        ],
        compiler_params=pltpu.CompilerParams(vmem_limit_bytes=VMEM_LIMIT),
        cost_estimate=pl.CostEstimate(
            flops=rows * 8 * SUB * SUB * vis, bytes_accessed=8 * rows * FEATURE, transcendentals=0
        ),
        name="subgrids",
    )(order, row, slot, start, uv, res)


def gather_kernel(*refs):
    x_refs, (out_ref, xs, hot, part) = refs[:-4], refs[-4:]
    lane = lax.broadcasted_iota(jnp.int32, (GROUP, LANES), 1) // SUB
    at = 0
    for x_ref in x_refs:
        xs[pl.ds(at, x_ref.shape[0]), :] = x_ref[...]
        at += x_ref.shape[0]
    tags = xs[:, pl.ds(FEATURE, LANES)].astype(jnp.float32)
    wanted = lax.broadcasted_iota(jnp.int32, tags.shape, 1)
    wanted = (wanted % 32) * 4 + wanted // 32 + 1
    hot[...] = jnp.where(tags == wanted.astype(jnp.float32), 1.0, 0.0).T.astype(jnp.bfloat16)
    for k in range(PIECES):
        part[...] = jnp.dot(
            hot[...], xs[:, pl.ds(k * LANES, LANES)], preferred_element_type=jnp.float32
        )
        for grp in range(4):
            given = [part[pl.ds(32 * jl + 8 * grp, 8), :] for jl in range(4)]
            for a in range(4):
                total = None
                for jl in range(4):
                    moved = given[jl]
                    if a != jl:
                        moved = pltpu.roll(moved, ((jl - a) % 4) * SUB, 1)
                    total = moved if total is None else jnp.where(lane == jl, moved, total)
                p = a * GROUP + k % GROUP
                out_ref[pl.ds(p * 64 + grp * 16 + k // GROUP, 8, stride=2), :] = total


def sum_slots(arrived):
    rows = sum(x.shape[0] for x in arrived)
    vmem = pl.BlockSpec(memory_space=pltpu.VMEM)
    return pl.pallas_call(
        gather_kernel,
        out_shape=jax.ShapeDtypeStruct((SUB * 64, LANES), jnp.float32),
        in_specs=[vmem] * len(arrived),
        out_specs=vmem,
        scratch_shapes=[
            pltpu.VMEM((rows, WIDTH), jnp.bfloat16),
            pltpu.VMEM((SLOTS, rows), jnp.bfloat16),
            pltpu.VMEM((SLOTS, LANES), jnp.float32),
        ],
        compiler_params=pltpu.CompilerParams(vmem_limit_bytes=VMEM_LIMIT),
        name="sum_slots",
    )(*arrived)


def rows_of(array):
    blocks, parts, vis = array.shape
    tiles = vis // LANES
    split = array.reshape(blocks, parts, tiles, LANES)
    return split.transpose(0, 2, 1, 3).reshape(blocks * tiles * parts, LANES)


def local(residual, uv_offsets, counts, tile_of_block, slot_of_block, owner_map):
    blocks, _, vis = uv_offsets.shape
    owners = owner_map.shape[0]
    capacity = -(-max(CAP_MIN, 2 * blocks // owners) // 32) * 16
    core = lax.axis_index("samp")
    me = lax.axis_index(("blk", "tile"))
    swap = [(0, 1), (1, 0)]
    own = residual[0]
    other = lax.ppermute(own, "samp", swap)

    tile_ids = tile_of_block[:, 0]
    owner_range = jnp.arange(owners, dtype=jnp.int32)
    owner_ids = jnp.sum(
        jnp.where(tile_ids[:, None] == owner_range[None, :], owner_map[None, :], 0), 1
    )
    paired = owners <= PAIRED_MAX and owners & (owners - 1) == 0
    offset = (owners - 1) - jnp.bitwise_xor(owner_ids, me) if paired else owner_ids
    index = jnp.arange(blocks, dtype=jnp.int32)
    same = (offset[None, :] == offset[:, None]) & (index[None, :] < index[:, None])
    rank = jnp.sum(same.astype(jnp.int32), 1)
    mine = (rank & 1) == core
    edges = jnp.arange(owners + 1, dtype=jnp.int32)
    start = jnp.sum((mine[None, :] & (offset[None, :] < edges[:, None])).astype(jnp.int32), 1)
    before = jnp.sum((mine[None, :] & (offset[None, :] < offset[:, None])).astype(jnp.int32), 1)
    place = jnp.where(mine, before + rank // 2, -1)
    wanted = jnp.arange((blocks + owners) // 2 + GROUP, dtype=jnp.int32)
    chosen = place[None, :] == wanted[:, None]
    order = jnp.sum(jnp.where(chosen, index[None, :], 0), 1)
    row = jnp.sum(jnp.where(chosen, (offset * capacity + rank // 2)[None, :], 0), 1)
    slot = jnp.sum(jnp.where(chosen, slot_of_block[None, :], 0), 1)

    live = jnp.arange(vis, dtype=jnp.int32)[None, None, :] < counts[:, None, None]
    both = own.astype(jnp.float32) + other.astype(jnp.float32)
    both = rows_of(jnp.where(live, both, 0.0))
    uv = rows_of(uv_offsets)
    subgrids = functools.partial(
        make_subgrids, capacity=capacity, order=order, row=row, slot=slot, start=start,
        uv=uv, res=both, vis=vis,
    )
    if paired:
        far = owners // 2
        rows = subgrids(0, (1,) * far) + subgrids(far, (1,) * (owners - far))
        arrived = []
        for turn in range(owners):
            distance = owners - 1 - turn
            piece = rows[turn]
            if distance:
                pairs = [(k, k ^ distance) for k in range(owners)]
                piece = lax.ppermute(piece, ("blk", "tile"), pairs)
            arrived.append(piece)
    else:
        each = max(d for d in range(1, 17) if owners % d == 0)
        rows = [subgrids(k, (each,))[0] for k in range(0, owners, each)]
        rows = jnp.concatenate(rows, 0).reshape(owners, capacity, WIDTH)
        rows = lax.all_to_all(rows, ("blk", "tile"), split_axis=0, concat_axis=0, tiled=True)
        arrived = [rows.reshape(owners * capacity, WIDTH)]
    part = sum_slots(arrived)
    part = part.reshape(SUB, SLOTS // 4, 2, LANES).transpose(0, 2, 1, 3).reshape(SUB, 2, SLOTS * SUB)
    return part + lax.ppermute(part, "samp", swap)


def solution(mesh):
    in_specs = (
        P("samp", ("cuts", "blk", "tile"), None, None),
        P(("cuts", "blk", "tile"), None, None),
        P(("cuts", "blk", "tile")),
        P(("cuts", "blk", "tile"), None),
        P(("cuts", "blk", "tile")),
        P(),
    )
    out_specs = P(("cuts", "blk", "tile"), None, None)
    return jax.shard_map(local, mesh=mesh, in_specs=in_specs, out_specs=out_specs, check_vma=False)
```

time: 73 us -> 56.3 us (0.77); the launches traced: 71.9 us -> 56.4 us
  blocking collectives: 32 us -> 0 us
  waiting for transfers between devices: 1.9 us -> 23.2 us
  Pallas kernels: 22 us -> 14 us
  starting transfers between devices: 7.84 us -> 12.7 us
  local copies, waits for them, and re-layouts: 4.43 us -> 1.85 us
  other arithmetic: 3.6 us -> 4.53 us
    all_gather x1 -> x0, blocking collectives: 32 us -> none  [local(): codes = lax.all_gather(code, ('blk', 'tile'), axis=0, tiled=False)]
    ppermute x1 -> x8, waiting for transfers between devices: 1.89 us -> 23.2 us  [the longest x7 20.5 us: local(): piece = lax.ppermute(piece, ('blk', 'tile'), pairs)]
    ppermute x1 -> x8, starting transfers between devices: 0.07 us -> 12.2 us  [the longest x7 12.1 us: local(): piece = lax.ppermute(piece, ('blk', 'tile'), pairs)]
    pallas_call x2 -> x3, Pallas kernels: 22 us -> 14 us  [the longest x2 12.9 us: make_subgrids(): pl.pallas_call(functools.partial(subgrid_kernel, first, destinations, cap...]
    all_to_all x1 -> x0, starting transfers between devices: 7.25 us -> none  [local(): lax.all_to_all(outgoing.reshape(owners, capacity, FEATURE), ('blk', 'tile...]
    add x2, other arithmetic: 0.09 us -> 1.54 us  [the longest x1 1.53 us: local(): return part + lax.ppermute(part, 'samp', swap)]
    another operation x4 -> x0, other arithmetic: 1.24 us -> none
    unnamed x13 -> x10, local copies, waits for them, and re-layouts: 2.96 us -> 1.85 us
  transfers between devices with their start and end apart: 3 -> 9, of which waited for: 1 -> 5; matrix products, arithmetic and copies ran while one was open for 5% -> 2% of each run, Pallas kernels for 0% -> 13%
where the time goes in v3:
time: 56.3 us; the launch traced here: 56.4 us
  waiting for transfers between devices  23.2 us (41%)
  Pallas kernels  14 us (25%)
  starting transfers between devices  12.7 us (23%)
  other arithmetic  4.53 us (8%)
  local copies, waits for them, and re-layouts  1.85 us (3%)
    ppermute x7, waiting for transfers between devices, local(): piece = lax.ppermute(piece, ('blk', 'tile'), pairs)  20.5 us
    pallas_call x2, Pallas kernels, make_subgrids(): pl.pallas_call(functools.partial(subgrid_kernel, first, destinations, cap...  12.9 us
    ppermute x7, starting transfers between devices, local(): piece = lax.ppermute(piece, ('blk', 'tile'), pairs)  12.1 us
    ppermute x1, waiting for transfers between devices, local(): return part + lax.ppermute(part, 'samp', swap)  2.65 us
    select_n x1, other arithmetic, local(): both = rows_of(jnp.where(live, both, 0.0))  2.07 us
    unnamed x10, local copies, waits for them, and re-layouts  1.85 us
    add x1, other arithmetic, local(): return part + lax.ppermute(part, 'samp', swap)  1.53 us
    pallas_call x1, Pallas kernels, sum_slots(): pl.pallas_call(gather_kernel, out_shape=jax.ShapeDtypeStruct((SUB * 64, L...  1.13 us
  transfers between devices with their start and end apart: 9, of which 5 were waited for; matrix products, arithmetic and copies ran while one was open for 2% of the time, Pallas kernels for 13%

profile of v3, /device:TPU:0, one launch (start us, length us, event | category | flops | bytes accessed | tf_op | source)
XLA Modules:
  0.0 56.4 jit_solution(21390967931501481)
XLA Ops:
  0.0 0.5 collective-permute-start
  0.5 0.0 copy-start.2
  0.5 0.0 copy-start.4
  0.5 0.7 %copy-done.2 = s32[256,1]{0,1:T(1,128)S(1)} copy-done((s32[256,1]{0,1:T(1,128)S(1)}, s32[256,1]{0,1:T(1,128)}, u32[]{:S(2)}) %copy-start.2) | copy-done | bytes 1048
  1.1 0.0 copy-done.4
  1.1 0.1 select_reduce_fusion.3
  1.2 0.2 convert_reduce_fusion.1
  1.4 0.1 convert_reduce_fusion.2.start_ref
  1.5 0.2 convert_reduce_fusion
  1.8 0.0 copy-start.3
  1.8 0.7 %copy-done.3 = s32[256]{0:T(256)S(1)} copy-done((s32[256]{0:T(256)S(1)}, s32[256]{0:T(256)}, u32[]{:S(2)}) %copy-start.3) | copy-done | bytes 1048
  2.4 0.0 copy-start.1
  2.4 0.2 select_reduce_fusion
  2.6 0.5 copy-done.1
  3.1 0.1 iota_compare_fusion
  3.3 0.0 copy-start
  3.3 0.0 collective-permute-done
  3.3 2.1 %add_select_fusion = f32[256,2,512]{2,1,0:T(2,128)S(1)} fusion(bf16[256,2,512]{2,1,0:T(2,128)(2,1)S(1)} %collective-permute-done, pred[256,512]{1,0:T(8,128)(4,1)S(1)} %iota_compare_fusion, bf16[1,256,2,512]{3,2,1,0:T(2,128)(2,1)} %param.6), kind=kLoop, calls=%fused_computation | loop fusion | flops 1048576 | bytes 2228224 | tf_op jit(solution)/shard_map/jit(_where)/select_n | solution.py:335
  5.4 0.0 copy-done
  5.4 5.6 %subgrids.3 = (bf16[32,2176]{1,0:T(8,128)(2,1)S(1)}, bf16[32,2176]{1,0:T(8,128)(2,1)S(1)}, bf16[32,2176]{1,0:T(8,128)(2,1)S(1)}, bf16[32,2176]{1,0:T(8,128)(2,1)S(1)}) custom-call(s32[140]{0:T(256)S(1)} %get-tuple-element.23.order_ref, s32[140]{0:T(256)S(1)} %get-tuple-element.22.row_ref, s32[140]{0:T(256)S(1)} %get-tuple-element.21.slot_ref, ...), custom_call_target="tpu_custom_call" | custom-call | flops 536870912 | bytes 2097152 | tf_op jit(solution)/shard_map/subgrids/pallas_call | solution.py:228
  11.0 3.6 %collective-permute-start.5 = (bf16[32,2176]{1,0:T(8,128)(2,1)S(1)}, bf16[32,2176]{1,0:T(8,128)(2,1)S(1)}, u32[]{:S(2)}, u32[]{:S(2)}) collective-permute-start(bf16[32,2176]{1,0:T(8,128)(2,1)S(1)} %get-tuple-element.17), channel_id=1, source_target_pairs={{0,3},{1,2},{2,1},{3,0},{4,7},{5,6},{6,5},{7,4},{8,11},{9,10},{10,... | collective-permute-start | bytes 417800 | tf_op jit(solution)/shard_map/ppermute | solution.py:350
  14.5 0.4 collective-permute-start.6
  15.0 0.2 collective-permute-start.7
  15.2 7.3 %subgrids.2 = (bf16[32,2176]{1,0:T(8,128)(2,1)S(1)}, bf16[32,2176]{1,0:T(8,128)(2,1)S(1)}, bf16[32,2176]{1,0:T(8,128)(2,1)S(1)}, bf16[32,2176]{1,0:T(8,128)(2,1)S(1)}) custom-call(s32[140]{0:T(256)S(1)} %get-tuple-element.23.order_ref, s32[140]{0:T(256)S(1)} %get-tuple-element.22.row_ref, s32[140]{0:T(256)S(1)} %get-tuple-element.21.slot_ref, ...), custom_call_target="tpu_custom_call" | custom-call | flops 536870912 | bytes 2097152 | tf_op jit(solution)/shard_map/subgrids/pallas_call | solution.py:228
  22.5 4.9 %collective-permute-start.1 = (bf16[32,2176]{1,0:T(8,128)(2,1)S(1)}, bf16[32,2176]{1,0:T(8,128)(2,1)S(1)}, u32[]{:S(2)}, u32[]{:S(2)}) collective-permute-start(bf16[32,2176]{1,0:T(8,128)(2,1)S(1)} %get-tuple-element.13), channel_id=1, source_target_pairs={{0,7},{1,6},{2,5},{3,4},{4,3},{5,2},{6,1},{7,0},{8,15},{9,14},{10,... | collective-permute-start | bytes 417800 | tf_op jit(solution)/shard_map/ppermute | solution.py:350
  27.4 0.2 collective-permute-start.2
  27.7 0.0 collective-permute-done.5.refs_4_
  27.7 1.4 %collective-permute-start.3 = (bf16[32,2176]{1,0:T(8,128)(2,1)S(1)}, bf16[32,2176]{1,0:T(8,128)(2,1)S(1)}, u32[]{:S(2)}, u32[]{:S(2)}) collective-permute-start(bf16[32,2176]{1,0:T(8,128)(2,1)S(1)} %get-tuple-element.15), channel_id=1, source_target_pairs={{0,5},{1,4},{2,7},{3,6},{4,1},{5,0},{6,3},{7,2},{8,13},{9,12},{10,... | collective-permute-start | bytes 417800 | tf_op jit(solution)/shard_map/ppermute | solution.py:350
  29.0 0.0 collective-permute-done.6.refs_5_
  29.0 1.4 %collective-permute-start.4 = (bf16[32,2176]{1,0:T(8,128)(2,1)S(1)}, bf16[32,2176]{1,0:T(8,128)(2,1)S(1)}, u32[]{:S(2)}, u32[]{:S(2)}) collective-permute-start(bf16[32,2176]{1,0:T(8,128)(2,1)S(1)} %get-tuple-element.16), channel_id=1, source_target_pairs={{0,4},{1,5},{2,6},{3,7},{4,0},{5,1},{6,2},{7,3},{8,12},{9,13},{10,... | collective-permute-start | bytes 417800 | tf_op jit(solution)/shard_map/ppermute | solution.py:350
  30.4 0.0 collective-permute-done.7.refs_6_
  30.4 1.1 %collective-permute-done.1.refs_0_ = bf16[32,2176]{1,0:T(8,128)(2,1)S(1)} collective-permute-done((bf16[32,2176]{1,0:T(8,128)(2,1)S(1)}, bf16[32,2176]{1,0:T(8,128)(2,1)S(1)}, u32[]{:S(2)}, u32[]{:S(2)}) %collective-permute-start.1) | collective-permute-done | bytes 139296 | tf_op jit(solution)/shard_map/ppermute | solution.py:350
  31.5 4.3 %collective-permute-done.2.refs_1_ = bf16[32,2176]{1,0:T(8,128)(2,1)S(1)} collective-permute-done((bf16[32,2176]{1,0:T(8,128)(2,1)S(1)}, bf16[32,2176]{1,0:T(8,128)(2,1)S(1)}, u32[]{:S(2)}, u32[]{:S(2)}) %collective-permute-start.2) | collective-permute-done | bytes 139296 | tf_op jit(solution)/shard_map/ppermute | solution.py:350
  35.8 13.1 %collective-permute-done.3.refs_2_ = bf16[32,2176]{1,0:T(8,128)(2,1)S(1)} collective-permute-done((bf16[32,2176]{1,0:T(8,128)(2,1)S(1)}, bf16[32,2176]{1,0:T(8,128)(2,1)S(1)}, u32[]{:S(2)}, u32[]{:S(2)}) %collective-permute-start.3) | collective-permute-done | bytes 139296 | tf_op jit(solution)/shard_map/ppermute | solution.py:350
  48.9 2.0 %collective-permute-done.4.refs_3_ = bf16[32,2176]{1,0:T(8,128)(2,1)S(1)} collective-permute-done((bf16[32,2176]{1,0:T(8,128)(2,1)S(1)}, bf16[32,2176]{1,0:T(8,128)(2,1)S(1)}, u32[]{:S(2)}, u32[]{:S(2)}) %collective-permute-start.4) | collective-permute-done | bytes 139296 | tf_op jit(solution)/shard_map/ppermute | solution.py:350
  51.0 1.1 %sum_slots.1 = f32[2048,128]{1,0:T(8,128)S(1)} custom-call(bf16[32,2176]{1,0:T(8,128)(2,1)S(1)} %collective-permute-done.1.refs_0_, bf16[32,2176]{1,0:T(8,128)(2,1)S(1)} %collective-permute-done.2.refs_1_, bf16[32,2176]{1,0:T(8,128)(2,1)S(1)} %collective-permute-done.3.refs_2_, bf16[32,2176]{1,0:T(8,128)(2,1)S(1)} %collective-permute-done.4.refs_3_, ...), custom_call_target="tpu_custom_call" | custom-call | tf_op jit(solution)/shard_map/sum_slots/pallas_call | solution.py:280
  52.1 0.1 collective-permute-start.8
  52.2 2.6 %collective-permute-done.8 = f32[32,2,4096]{2,1,0:T(2,128)S(1)} collective-permute-done((f32[32,2,4096]{2,1,0:T(2,128)S(1)}, f32[32,2,4096]{2,1,0:T(2,128)S(1)}, u32[]{:S(2)}, u32[]{:S(2)}) %collective-permute-start.8) | collective-permute-done | bytes 1048608 | tf_op jit(solution)/shard_map/ppermute | solution.py:360
  54.9 1.5 %add.35 = f32[32,2,4096]{2,1,0:T(2,128)} add(f32[32,2,4096]{2,1,0:T(2,128)S(1)} %bitcast.23, f32[32,2,4096]{2,1,0:T(2,128)S(1)} %collective-permute-done.8) | non-fusion elementwise | flops 262144 | bytes 3145728 | tf_op jit(solution)/shard_map/add | solution.py:360
  (4 shorter events, 0.0 us)
Async XLA Ops:
  0.0 3.3 %collective-permute-start = (bf16[256,2,512]{2,1,0:T(2,128)(2,1)}, bf16[256,2,512]{2,1,0:T(2,128)(2,1)S(1)}, u32[]{:S(2)}, u32[]{:S(2)}) collective-permute-start(bf16[256,2,512]{2,1,0:T(2,128)(2,1)} %bitcast.24), channel_id=1, source_target_pairs={{0,8},{8,0},{1,9},{9,1},{2,10},{10,2},{3,11},{11,3},{4,12},{12,4},... | collective-permute-start | bytes 1572872 | tf_op jit(solution)/shard_map/ppermute | solution.py:310
  0.5 0.7 %copy-start.2 = (s32[256,1]{0,1:T(1,128)S(1)}, s32[256,1]{0,1:T(1,128)}, u32[]{:S(2)}) copy-start(s32[256,1]{0,1:T(1,128)} %param.9) | copy-start | bytes 3076
  0.5 0.7 %copy-start.4 = (s32[8]{0:T(128)S(1)}, s32[8]{0:T(128)}, u32[]{:S(2)}) copy-start(s32[8]{0:T(128)} %param.11) | copy-start | bytes 100
  1.8 0.7 %copy-start.3 = (s32[256]{0:T(256)S(1)}, s32[256]{0:T(256)}, u32[]{:S(2)}) copy-start(s32[256]{0:T(256)} %param.10) | copy-start | bytes 3076
  2.4 0.7 %copy-start.1 = (s32[256]{0:T(256)S(1)}, s32[256]{0:T(256)}, u32[]{:S(2)}) copy-start(s32[256]{0:T(256)} %param.8) | copy-start | bytes 3076
  3.3 2.1 %copy-start = (f32[256,2,512]{2,1,0:T(2,128)S(1)}, f32[256,2,512]{2,1,0:T(2,128)}, u32[]{:S(2)}) copy-start(f32[256,2,512]{2,1,0:T(2,128)} %param.7) | copy-start | bytes 3145732
  11.0 16.7 %collective-permute-start.5 = (bf16[32,2176]{1,0:T(8,128)(2,1)S(1)}, bf16[32,2176]{1,0:T(8,128)(2,1)S(1)}, u32[]{:S(2)}, u32[]{:S(2)}) collective-permute-start(bf16[32,2176]{1,0:T(8,128)(2,1)S(1)} %get-tuple-element.17), channel_id=1, source_target_pairs={{0,3},{1,2},{2,1},{3,0},{4,7},{5,6},{6,5},{7,4},{8,11},{9,10},{10,... | collective-permute-start | bytes 417800 | tf_op jit(solution)/shard_map/ppermute | solution.py:350
  14.5 14.5 %collective-permute-start.6 = (bf16[32,2176]{1,0:T(8,128)(2,1)S(1)}, bf16[32,2176]{1,0:T(8,128)(2,1)S(1)}, u32[]{:S(2)}, u32[]{:S(2)}) collective-permute-start(bf16[32,2176]{1,0:T(8,128)(2,1)S(1)} %get-tuple-element.18), channel_id=1, source_target_pairs={{0,2},{1,3},{2,0},{3,1},{4,6},{5,7},{6,4},{7,5},{8,10},{9,11},{10,... | collective-permute-start | bytes 417800 | tf_op jit(solution)/shard_map/ppermute | solution.py:350
  15.0 15.5 %collective-permute-start.7 = (bf16[32,2176]{1,0:T(8,128)(2,1)S(1)}, bf16[32,2176]{1,0:T(8,128)(2,1)S(1)}, u32[]{:S(2)}, u32[]{:S(2)}) collective-permute-start(bf16[32,2176]{1,0:T(8,128)(2,1)S(1)} %get-tuple-element.19), channel_id=1, source_target_pairs={{0,1},{1,0},{2,3},{3,2},{4,5},{5,4},{6,7},{7,6},{8,9},{9,8},{10,11... | collective-permute-start | bytes 417800 | tf_op jit(solution)/shard_map/ppermute | solution.py:350
  22.5 9.0 %collective-permute-start.1 = (bf16[32,2176]{1,0:T(8,128)(2,1)S(1)}, bf16[32,2176]{1,0:T(8,128)(2,1)S(1)}, u32[]{:S(2)}, u32[]{:S(2)}) collective-permute-start(bf16[32,2176]{1,0:T(8,128)(2,1)S(1)} %get-tuple-element.13), channel_id=1, source_target_pairs={{0,7},{1,6},{2,5},{3,4},{4,3},{5,2},{6,1},{7,0},{8,15},{9,14},{10,... | collective-permute-start | bytes 417800 | tf_op jit(solution)/shard_map/ppermute | solution.py:350
  27.4 8.4 %collective-permute-start.2 = (bf16[32,2176]{1,0:T(8,128)(2,1)S(1)}, bf16[32,2176]{1,0:T(8,128)(2,1)S(1)}, u32[]{:S(2)}, u32[]{:S(2)}) collective-permute-start(bf16[32,2176]{1,0:T(8,128)(2,1)S(1)} %get-tuple-element.14), channel_id=1, source_target_pairs={{0,6},{1,7},{2,4},{3,5},{4,2},{5,3},{6,0},{7,1},{8,14},{9,15},{10,... | collective-permute-start | bytes 417800 | tf_op jit(solution)/shard_map/ppermute | solution.py:350
  27.7 21.3 %collective-permute-start.3 = (bf16[32,2176]{1,0:T(8,128)(2,1)S(1)}, bf16[32,2176]{1,0:T(8,128)(2,1)S(1)}, u32[]{:S(2)}, u32[]{:S(2)}) collective-permute-start(bf16[32,2176]{1,0:T(8,128)(2,1)S(1)} %get-tuple-element.15), channel_id=1, source_target_pairs={{0,5},{1,4},{2,7},{3,6},{4,1},{5,0},{6,3},{7,2},{8,13},{9,12},{10,... | collective-permute-start | bytes 417800 | tf_op jit(solution)/shard_map/ppermute | solution.py:350
  29.0 22.0 %collective-permute-start.4 = (bf16[32,2176]{1,0:T(8,128)(2,1)S(1)}, bf16[32,2176]{1,0:T(8,128)(2,1)S(1)}, u32[]{:S(2)}, u32[]{:S(2)}) collective-permute-start(bf16[32,2176]{1,0:T(8,128)(2,1)S(1)} %get-tuple-element.16), channel_id=1, source_target_pairs={{0,4},{1,5},{2,6},{3,7},{4,0},{5,1},{6,2},{7,3},{8,12},{9,13},{10,... | collective-permute-start | bytes 417800 | tf_op jit(solution)/shard_map/ppermute | solution.py:350
  52.1 2.7 %collective-permute-start.8 = (f32[32,2,4096]{2,1,0:T(2,128)S(1)}, f32[32,2,4096]{2,1,0:T(2,128)S(1)}, u32[]{:S(2)}, u32[]{:S(2)}) collective-permute-start(f32[32,2,4096]{2,1,0:T(2,128)S(1)} %bitcast.22), channel_id=1, source_target_pairs={{0,8},{8,0},{1,9},{9,1},{2,10},{10,2},{3,11},{11,3},{4,12},{12,4},... | collective-permute-start | bytes 3145736 | tf_op jit(solution)/shard_map/ppermute | solution.py:360

commit v4 on v3

--- a/solution.py
+++ b/solution.py
@@ -20,6 +20,7 @@
 QUAD = 4
 TABLES = 12
 PAIRED_MAX = 16
+CALLS = (0, 2, 4, 8)
 VMEM_LIMIT = 48 * 1024 * 1024
 
 
@@ -73,13 +74,18 @@
 
 
 def subgrid_kernel(
-    first, destinations, capacity, order_ref, row_ref, slot_ref, start_ref, uv_ref, res_ref, *refs
+    first, destinations, capacity, order_ref, row_ref, slot_ref, start_ref, count_ref, token_ref,
+    uv_ref, own_ref, other_ref, *refs
 ):
-    out_refs, scratch = refs[:-12], refs[-12:]
+    out_refs, next_ref, scratch = refs[:-13], refs[-13], refs[-12:]
+    next_ref[...] = jnp.zeros_like(next_ref)
     gathered, cos_u, sin_u, cos_v, sin_v, dense, left_a, right_a, left_b, right_b, stage, tags = scratch
     tiles = gathered.shape[0] // (4 * GROUP)
     rows = destinations * capacity
     lane = lax.broadcasted_iota(jnp.int32, (GROUP, LANES), 1) // SUB
+    vis_at = lax.broadcasted_iota(jnp.int32, (2 * tiles, LANES), 1) + LANES * (
+        lax.broadcasted_iota(jnp.int32, (2 * tiles, LANES), 0) // 2
+    )
     low, high = start_ref[first], start_ref[first + destinations]
     turns = (high - low + GROUP - 1) // GROUP
     last = order_ref.shape[0] - 1
@@ -94,7 +100,11 @@
             block = order_ref[jnp.minimum(low + g * GROUP + i, last)]
             at = pl.ds(pl.multiple_of(block * 2 * tiles, 2 * tiles), 2 * tiles)
             gathered[pl.ds(i, 2 * tiles, stride=GROUP), :] = uv_ref[at, :]
-            gathered[pl.ds(2 * tiles * GROUP + i, 2 * tiles, stride=GROUP), :] = res_ref[at, :]
+            two = pl.ds(pl.multiple_of((block // 2) * 4 * tiles, 4 * tiles), 4 * tiles)
+            both = own_ref[two, :].astype(jnp.float32) + other_ref[two, :].astype(jnp.float32)
+            both = jnp.where(block % 2 == 1, both[2 * tiles :], both[: 2 * tiles])
+            both = jnp.where(vis_at < count_ref[block], both, 0.0)
+            gathered[pl.ds(2 * tiles * GROUP + i, 2 * tiles, stride=GROUP), :] = both
         u, v, re, im = [
             wide(gathered, (k // 2) * 2 * tiles * GROUP + (k % 2) * GROUP, step=2 * GROUP)
             for k in range(4)
@@ -216,7 +226,7 @@
         at += out_ref.shape[0]
 
 
-def make_subgrids(first, outs, capacity, order, row, slot, start, uv, res, vis):
+def make_subgrids(first, outs, token, capacity, order, row, slot, start, counts, uv, own, other, vis):
     tiles = vis // LANES
     destinations = sum(outs)
     rows = destinations * capacity
@@ -227,9 +237,10 @@
     quad = pltpu.VMEM((2 * QUAD * SUB, vis), jnp.bfloat16)
     return pl.pallas_call(
         functools.partial(subgrid_kernel, first, destinations, capacity),
-        out_shape=[jax.ShapeDtypeStruct((n * capacity, WIDTH), jnp.bfloat16) for n in outs],
-        in_specs=[smem, smem, smem, smem, vmem, vmem],
-        out_specs=[vmem] * len(outs),
+        out_shape=[jax.ShapeDtypeStruct((n * capacity, WIDTH), jnp.bfloat16) for n in outs]
+        + [jax.ShapeDtypeStruct(token.shape, token.dtype)],
+        in_specs=[smem] * 5 + [vmem] * 4,
+        out_specs=[vmem] * (len(outs) + 1),
         scratch_shapes=[
             pltpu.VMEM((4 * tiles * GROUP, LANES), jnp.float32),
             table, table, table, table,
@@ -243,7 +254,7 @@
             flops=rows * 8 * SUB * SUB * vis, bytes_accessed=8 * rows * FEATURE, transcendentals=0
         ),
         name="subgrids",
-    )(order, row, slot, start, uv, res)
+    )(order, row, slot, start, counts, token, uv, own, other)
 
 
 def gather_kernel(*refs):
@@ -330,17 +341,18 @@
     row = jnp.sum(jnp.where(chosen, (offset * capacity + rank // 2)[None, :], 0), 1)
     slot = jnp.sum(jnp.where(chosen, slot_of_block[None, :], 0), 1)
 
-    live = jnp.arange(vis, dtype=jnp.int32)[None, None, :] < counts[:, None, None]
-    both = own.astype(jnp.float32) + other.astype(jnp.float32)
-    both = rows_of(jnp.where(live, both, 0.0))
-    uv = rows_of(uv_offsets)
     subgrids = functools.partial(
         make_subgrids, capacity=capacity, order=order, row=row, slot=slot, start=start,
-        uv=uv, res=both, vis=vis,
+        counts=counts, uv=rows_of(uv_offsets), own=rows_of(own), other=rows_of(other), vis=vis,
     )
+    token = jnp.zeros((GROUP, LANES), jnp.int32)
     if paired:
-        far = owners // 2
-        rows = subgrids(0, (1,) * far) + subgrids(far, (1,) * (owners - far))
+        rows = []
+        for first, last in zip(CALLS[:-1], CALLS[1:]):
+            first, last = owners * first // CALLS[-1], owners * last // CALLS[-1]
+            if first < last:
+                *more, token = subgrids(first, (1,) * (last - first), token)
+                rows += more
         arrived = []
         for turn in range(owners):
             distance = owners - 1 - turn
@@ -351,13 +363,14 @@
             arrived.append(piece)
     else:
         each = max(d for d in range(1, 17) if owners % d == 0)
-        rows = [subgrids(k, (each,))[0] for k in range(0, owners, each)]
+        rows = [subgrids(k, (each,), token)[0] for k in range(0, owners, each)]
         rows = jnp.concatenate(rows, 0).reshape(owners, capacity, WIDTH)
         rows = lax.all_to_all(rows, ("blk", "tile"), split_axis=0, concat_axis=0, tiled=True)
         arrived = [rows.reshape(owners * capacity, WIDTH)]
     part = sum_slots(arrived)
-    part = part.reshape(SUB, SLOTS // 4, 2, LANES).transpose(0, 2, 1, 3).reshape(SUB, 2, SLOTS * SUB)
-    return part + lax.ppermute(part, "samp", swap)
+    whole = part + lax.ppermute(part, "samp", swap)
+    whole = whole.reshape(SUB, SLOTS // 4, 2, LANES).transpose(0, 2, 1, 3)
+    return whole.reshape(SUB, 2, SLOTS * SUB)
 
 
 def solution(mesh):

time: 56.3 us -> 51 us (0.906)
  waiting for transfers between devices: 23.2 us -> 13.9 us
  other arithmetic: 4.53 us -> 1.87 us
  Pallas kernels: 14 us -> 16.5 us
  local copies, waits for them, and re-layouts: 1.85 us -> 4.29 us
  starting transfers between devices: 12.7 us -> 14.5 us
    ppermute x7, waiting for transfers between devices: 20.5 us -> 11.3 us  [local(): piece = lax.ppermute(piece, ('blk', 'tile'), pairs)]
    pallas_call x2 -> x3, Pallas kernels: 12.9 us -> 15.4 us  [make_subgrids(): pl.pallas_call(functools.partial(subgrid_kernel, first, destinations, cap...]
    unnamed x10 -> x16, local copies, waits for them, and re-layouts: 1.85 us -> 4.29 us
    select_n x1 -> x0, other arithmetic: 2.07 us -> none  [local(): both = rows_of(jnp.where(live, both, 0.0))]
    ppermute x7, starting transfers between devices: 12.1 us -> 14 us  [local(): piece = lax.ppermute(piece, ('blk', 'tile'), pairs)]
  transfers between devices with their start and end apart: 9 -> 9, of which waited for: 5 -> 5; matrix products, arithmetic and copies ran while one was open for 2% -> 2% of each run, Pallas kernels for 13% -> 24%
where the time goes in v4:
time: 51 us; the launch traced here: 51.3 us
  Pallas kernels  16.5 us (32%)
  starting transfers between devices  14.5 us (28%)
  waiting for transfers between devices  13.9 us (27%)
  local copies, waits for them, and re-layouts  4.29 us (8%)
  other arithmetic  1.87 us (4%)
    pallas_call x3, Pallas kernels, make_subgrids(): pl.pallas_call(functools.partial(subgrid_kernel, first, destinations, cap...  15.4 us
    ppermute x7, starting transfers between devices, local(): piece = lax.ppermute(piece, ('blk', 'tile'), pairs)  14 us
    ppermute x7, waiting for transfers between devices, local(): piece = lax.ppermute(piece, ('blk', 'tile'), pairs)  11.3 us
    unnamed x16, local copies, waits for them, and re-layouts  4.29 us
    ppermute x1, waiting for transfers between devices, local(): whole = part + lax.ppermute(part, 'samp', swap)  2.65 us
    pallas_call x1, Pallas kernels, sum_slots(): pl.pallas_call(gather_kernel, out_shape=jax.ShapeDtypeStruct((SUB * 64, L...  1.14 us
    add x1, other arithmetic, local(): whole = part + lax.ppermute(part, 'samp', swap)  1.08 us
  transfers between devices with their start and end apart: 9, of which 5 were waited for; matrix products, arithmetic and copies ran while one was open for 2% of the time, Pallas kernels for 24%

profile of v4, /device:TPU:0, one launch (start us, length us, event | category | flops | bytes accessed | tf_op | source)
XLA Modules:
  0.0 51.3 jit_solution(223403252851819516)
XLA Ops:
  0.0 0.5 collective-permute-start
  0.5 0.0 copy-start.5
  0.5 0.0 copy-start.7
  0.5 0.7 %copy-done.5 = s32[256,1]{0,1:T(1,128)S(1)} copy-done((s32[256,1]{0,1:T(1,128)S(1)}, s32[256,1]{0,1:T(1,128)}, u32[]{:S(2)}) %copy-start.5) | copy-done | bytes 1048
  1.1 0.0 copy-done.7
  1.1 0.1 select_reduce_fusion.3
  1.2 0.2 convert_reduce_fusion.1
  1.4 0.1 convert_reduce_fusion.2.start_ref
  1.5 0.2 convert_reduce_fusion
  1.8 0.0 copy-start.6
  1.8 0.7 %copy-done.6 = s32[256]{0:T(256)S(1)} copy-done((s32[256]{0:T(256)S(1)}, s32[256]{0:T(256)}, u32[]{:S(2)}) %copy-start.6) | copy-done | bytes 1048
  2.4 0.2 select_reduce_fusion
  2.6 0.0 collective-permute-done
  2.6 0.0 copy-start.4
  2.7 0.7 %copy-done.4 = s32[256]{0:T(256)S(1)} copy-done((s32[256]{0:T(256)S(1)}, s32[256]{0:T(256)}, u32[]{:S(2)}) %copy-start.4) | copy-done | bytes 1048
  3.3 0.0 copy-start
  3.3 1.2 %copy-done = f32[256,2,512]{2,1,0:T(2,128)S(1)} copy-done((f32[256,2,512]{2,1,0:T(2,128)S(1)}, f32[256,2,512]{2,1,0:T(2,128)}, u32[]{:S(2)}) %copy-start) | copy-done | bytes 1048600
  4.6 0.0 copy-start.2
  4.6 1.0 %copy-done.2 = bf16[1,256,2,512]{3,2,1,0:T(2,128)(2,1)S(1)} copy-done((bf16[1,256,2,512]{3,2,1,0:T(2,128)(2,1)S(1)}, bf16[1,256,2,512]{3,2,1,0:T(2,128)(2,1)}, u32[]{:S(2)}) %copy-start.2) | copy-done | bytes 524312
  5.6 0.0 copy-start.1
  5.6 0.0 copy-start.3
  5.6 3.1 %subgrids.3 = (bf16[32,2176]{1,0:T(8,128)(2,1)S(1)}, bf16[32,2176]{1,0:T(8,128)(2,1)S(1)}, s32[8,128]{1,0:T(8,128)S(1)}) custom-call(s32[140]{0:T(256)S(1)} %get-tuple-element.27.order_ref, s32[140]{0:T(256)S(1)} %get-tuple-element.26.row_ref, s32[140]{0:T(256)S(1)} %get-tuple-element.25.slot_ref, s32[9]{0:T(128)S(1)} %convert_reduce_fusion.2.start_ref, ...), custom_call_target="tpu_custom_call" | custom-call | flops 268435456 | bytes 1048576 | tf_op jit(solution)/shard_map/subgrids/pallas_call | solution.py:238
  8.7 6.9 %collective-permute-start.1 = (bf16[32,2176]{1,0:T(8,128)(2,1)S(1)}, bf16[32,2176]{1,0:T(8,128)(2,1)S(1)}, u32[]{:S(2)}, u32[]{:S(2)}) collective-permute-start(bf16[32,2176]{1,0:T(8,128)(2,1)S(1)} %get-tuple-element.15), channel_id=1, source_target_pairs={{0,7},{1,6},{2,5},{3,4},{4,3},{5,2},{6,1},{7,0},{8,15},{9,14},{10,... | collective-permute-start | bytes 417800 | tf_op jit(solution)/shard_map/ppermute | solution.py:362
  15.6 0.0 collective-permute-start.2
  15.6 0.0 copy-done.1
  15.6 0.0 copy-done.3
  15.6 3.1 %subgrids.4 = (bf16[32,2176]{1,0:T(8,128)(2,1)S(1)}, bf16[32,2176]{1,0:T(8,128)(2,1)S(1)}, s32[8,128]{1,0:T(8,128)S(1)}) custom-call(s32[140]{0:T(256)S(1)} %get-tuple-element.27.order_ref, s32[140]{0:T(256)S(1)} %get-tuple-element.26.row_ref, s32[140]{0:T(256)S(1)} %get-tuple-element.25.slot_ref, s32[9]{0:T(128)S(1)} %convert_reduce_fusion.2.start_ref, ...), custom_call_target="tpu_custom_call" | custom-call | flops 268435456 | bytes 1048576 | tf_op jit(solution)/shard_map/subgrids/pallas_call | solution.py:238
  18.8 9.1 %subgrids.5 = (bf16[32,2176]{1,0:T(8,128)(2,1)S(1)}, bf16[32,2176]{1,0:T(8,128)(2,1)S(1)}, bf16[32,2176]{1,0:T(8,128)(2,1)S(1)}, bf16[32,2176]{1,0:T(8,128)(2,1)S(1)}, s32[8,128]{1,0:T(8,128)}) custom-call(s32[140]{0:T(256)S(1)} %get-tuple-element.27.order_ref, s32[140]{0:T(256)S(1)} %get-tuple-element.26.row_ref, s32[140]{0:T(256)S(1)} %get-tuple-element.25.slot_ref, ...), custom_call_target="tpu_custom_call" | custom-call | flops 536870912 | bytes 2097152 | tf_op jit(solution)/shard_map/subgrids/pallas_call | solution.py:238
  27.9 0.9 %collective-permute-start.5 = (bf16[32,2176]{1,0:T(8,128)(2,1)S(1)}, bf16[32,2176]{1,0:T(8,128)(2,1)S(1)}, u32[]{:S(2)}, u32[]{:S(2)}) collective-permute-start(bf16[32,2176]{1,0:T(8,128)(2,1)S(1)} %get-tuple-element.21), channel_id=1, source_target_pairs={{0,3},{1,2},{2,1},{3,0},{4,7},{5,6},{6,5},{7,4},{8,11},{9,10},{10,... | collective-permute-start | bytes 417800 | tf_op jit(solution)/shard_map/ppermute | solution.py:362
  28.8 1.8 %collective-permute-start.6 = (bf16[32,2176]{1,0:T(8,128)(2,1)S(1)}, bf16[32,2176]{1,0:T(8,128)(2,1)S(1)}, u32[]{:S(2)}, u32[]{:S(2)}) collective-permute-start(bf16[32,2176]{1,0:T(8,128)(2,1)S(1)} %get-tuple-element.22), channel_id=1, source_target_pairs={{0,2},{1,3},{2,0},{3,1},{4,6},{5,7},{6,4},{7,5},{8,10},{9,11},{10,... | collective-permute-start | bytes 417800 | tf_op jit(solution)/shard_map/ppermute | solution.py:362
  30.6 0.7 %collective-permute-start.7 = (bf16[32,2176]{1,0:T(8,128)(2,1)S(1)}, bf16[32,2176]{1,0:T(8,128)(2,1)S(1)}, u32[]{:S(2)}, u32[]{:S(2)}) collective-permute-start(bf16[32,2176]{1,0:T(8,128)(2,1)S(1)} %get-tuple-element.23), channel_id=1, source_target_pairs={{0,1},{1,0},{2,3},{3,2},{4,5},{5,4},{6,7},{7,6},{8,9},{9,8},{10,11... | collective-permute-start | bytes 417800 | tf_op jit(solution)/shard_map/ppermute | solution.py:362
  31.4 0.0 collective-permute-done.1.refs_0_
  31.4 1.7 %collective-permute-start.3 = (bf16[32,2176]{1,0:T(8,128)(2,1)S(1)}, bf16[32,2176]{1,0:T(8,128)(2,1)S(1)}, u32[]{:S(2)}, u32[]{:S(2)}) collective-permute-start(bf16[32,2176]{1,0:T(8,128)(2,1)S(1)} %get-tuple-element.18), channel_id=1, source_target_pairs={{0,5},{1,4},{2,7},{3,6},{4,1},{5,0},{6,3},{7,2},{8,13},{9,12},{10,... | collective-permute-start | bytes 417800 | tf_op jit(solution)/shard_map/ppermute | solution.py:362
  33.1 0.0 collective-permute-done.2.refs_1_
  33.1 1.9 %collective-permute-start.4 = (bf16[32,2176]{1,0:T(8,128)(2,1)S(1)}, bf16[32,2176]{1,0:T(8,128)(2,1)S(1)}, u32[]{:S(2)}, u32[]{:S(2)}) collective-permute-start(bf16[32,2176]{1,0:T(8,128)(2,1)S(1)} %get-tuple-element.19), channel_id=1, source_target_pairs={{0,4},{1,5},{2,6},{3,7},{4,0},{5,1},{6,2},{7,3},{8,12},{9,13},{10,... | collective-permute-start | bytes 417800 | tf_op jit(solution)/shard_map/ppermute | solution.py:362
  35.0 1.0 %collective-permute-done.5.refs_4_ = bf16[32,2176]{1,0:T(8,128)(2,1)S(1)} collective-permute-done((bf16[32,2176]{1,0:T(8,128)(2,1)S(1)}, bf16[32,2176]{1,0:T(8,128)(2,1)S(1)}, u32[]{:S(2)}, u32[]{:S(2)}) %collective-permute-start.5) | collective-permute-done | bytes 139296 | tf_op jit(solution)/shard_map/ppermute | solution.py:362
  36.0 3.6 %collective-permute-done.6.refs_5_ = bf16[32,2176]{1,0:T(8,128)(2,1)S(1)} collective-permute-done((bf16[32,2176]{1,0:T(8,128)(2,1)S(1)}, bf16[32,2176]{1,0:T(8,128)(2,1)S(1)}, u32[]{:S(2)}, u32[]{:S(2)}) %collective-permute-start.6) | collective-permute-done | bytes 139296 | tf_op jit(solution)/shard_map/ppermute | solution.py:362
  39.6 0.0 collective-permute-done.7.refs_6_
  39.6 5.6 %collective-permute-done.3.refs_2_ = bf16[32,2176]{1,0:T(8,128)(2,1)S(1)} collective-permute-done((bf16[32,2176]{1,0:T(8,128)(2,1)S(1)}, bf16[32,2176]{1,0:T(8,128)(2,1)S(1)}, u32[]{:S(2)}, u32[]{:S(2)}) %collective-permute-start.3) | collective-permute-done | bytes 139296 | tf_op jit(solution)/shard_map/ppermute | solution.py:362
  45.2 1.1 %collective-permute-done.4.refs_3_ = bf16[32,2176]{1,0:T(8,128)(2,1)S(1)} collective-permute-done((bf16[32,2176]{1,0:T(8,128)(2,1)S(1)}, bf16[32,2176]{1,0:T(8,128)(2,1)S(1)}, u32[]{:S(2)}, u32[]{:S(2)}) %collective-permute-start.4) | collective-permute-done | bytes 139296 | tf_op jit(solution)/shard_map/ppermute | solution.py:362
  46.3 1.1 %sum_slots.1 = f32[2048,128]{1,0:T(8,128)S(1)} custom-call(bf16[32,2176]{1,0:T(8,128)(2,1)S(1)} %collective-permute-done.1.refs_0_, bf16[32,2176]{1,0:T(8,128)(2,1)S(1)} %collective-permute-done.2.refs_1_, bf16[32,2176]{1,0:T(8,128)(2,1)S(1)} %collective-permute-done.3.refs_2_, bf16[32,2176]{1,0:T(8,128)(2,1)S(1)} %collective-permute-done.4.refs_3_, ...), custom_call_target="tpu_custom_call" | custom-call | tf_op jit(solution)/shard_map/sum_slots/pallas_call | solution.py:291
  47.4 0.1 collective-permute-start.8
  47.5 2.6 %collective-permute-done.8 = f32[2048,128]{1,0:T(8,128)S(1)} collective-permute-done((f32[2048,128]{1,0:T(8,128)S(1)}, f32[2048,128]{1,0:T(8,128)S(1)}, u32[]{:S(2)}, u32[]{:S(2)}) %collective-permute-start.8) | collective-permute-done | bytes 1048608 | tf_op jit(solution)/shard_map/ppermute | solution.py:371
  50.2 1.1 %add.31 = f32[2048,128]{1,0:T(8,128)} add(f32[2048,128]{1,0:T(8,128)S(1)} %sum_slots.1, f32[2048,128]{1,0:T(8,128)S(1)} %collective-permute-done.8) | non-fusion elementwise | flops 262144 | bytes 3145728 | tf_op jit(solution)/shard_map/add | solution.py:371
  (5 shorter events, 0.0 us)
Async XLA Ops:
  0.0 2.6 %collective-permute-start = (bf16[256,2,512]{2,1,0:T(2,128)(2,1)}, bf16[256,2,512]{2,1,0:T(2,128)(2,1)S(1)}, u32[]{:S(2)}, u32[]{:S(2)}) collective-permute-start(bf16[256,2,512]{2,1,0:T(2,128)(2,1)} %bitcast.25), channel_id=1, source_target_pairs={{0,8},{8,0},{1,9},{9,1},{2,10},{10,2},{3,11},{11,3},{4,12},{12,4},... | collective-permute-start | bytes 1572872 | tf_op jit(solution)/shard_map/ppermute | solution.py:321
  0.5 0.7 %copy-start.5 = (s32[256,1]{0,1:T(1,128)S(1)}, s32[256,1]{0,1:T(1,128)}, u32[]{:S(2)}) copy-start(s32[256,1]{0,1:T(1,128)} %param.9) | copy-start | bytes 3076
  0.5 0.7 %copy-start.7 = (s32[8]{0:T(128)S(1)}, s32[8]{0:T(128)}, u32[]{:S(2)}) copy-start(s32[8]{0:T(128)} %param.11) | copy-start | bytes 100
  1.8 0.7 %copy-start.6 = (s32[256]{0:T(256)S(1)}, s32[256]{0:T(256)}, u32[]{:S(2)}) copy-start(s32[256]{0:T(256)} %param.10) | copy-start | bytes 3076
  2.6 0.7 %copy-start.4 = (s32[256]{0:T(256)S(1)}, s32[256]{0:T(256)}, u32[]{:S(2)}) copy-start(s32[256]{0:T(256)} %count_ref.5) | copy-start | bytes 3076
  3.3 1.2 %copy-start = (f32[256,2,512]{2,1,0:T(2,128)S(1)}, f32[256,2,512]{2,1,0:T(2,128)}, u32[]{:S(2)}) copy-start(f32[256,2,512]{2,1,0:T(2,128)} %param.7) | copy-start | bytes 3145732
  4.6 1.0 %copy-start.2 = (bf16[1,256,2,512]{3,2,1,0:T(2,128)(2,1)S(1)}, bf16[1,256,2,512]{3,2,1,0:T(2,128)(2,1)}, u32[]{:S(2)}) copy-start(bf16[1,256,2,512]{3,2,1,0:T(2,128)(2,1)} %param.6) | copy-start | bytes 1572868
  5.6 10.0 %copy-start.1 = (f32[256,2,512]{2,1,0:T(2,128)S(1)}, f32[256,2,512]{2,1,0:T(2,128)}, u32[]{:S(2)}) copy-start(f32[256,2,512]{2,1,0:T(2,128)} %param.7) | copy-start | bytes 3145732
  5.6 10.0 %copy-start.3 = (bf16[1,256,2,512]{3,2,1,0:T(2,128)(2,1)S(1)}, bf16[1,256,2,512]{3,2,1,0:T(2,128)(2,1)}, u32[]{:S(2)}) copy-start(bf16[1,256,2,512]{3,2,1,0:T(2,128)(2,1)} %param.6) | copy-start | bytes 1572868
  8.7 22.6 %collective-permute-start.1 = (bf16[32,2176]{1,0:T(8,128)(2,1)S(1)}, bf16[32,2176]{1,0:T(8,128)(2,1)S(1)}, u32[]{:S(2)}, u32[]{:S(2)}) collective-permute-start(bf16[32,2176]{1,0:T(8,128)(2,1)S(1)} %get-tuple-element.15), channel_id=1, source_target_pairs={{0,7},{1,6},{2,5},{3,4},{4,3},{5,2},{6,1},{7,0},{8,15},{9,14},{10,... | collective-permute-start | bytes 417800 | tf_op jit(solution)/shard_map/ppermute | solution.py:362
  15.6 17.5 %collective-permute-start.2 = (bf16[32,2176]{1,0:T(8,128)(2,1)S(1)}, bf16[32,2176]{1,0:T(8,128)(2,1)S(1)}, u32[]{:S(2)}, u32[]{:S(2)}) collective-permute-start(bf16[32,2176]{1,0:T(8,128)(2,1)S(1)} %get-tuple-element.16), channel_id=1, source_target_pairs={{0,6},{1,7},{2,4},{3,5},{4,2},{5,3},{6,0},{7,1},{8,14},{9,15},{10,... | collective-permute-start | bytes 417800 | tf_op jit(solution)/shard_map/ppermute | solution.py:362
  27.9 8.2 %collective-permute-start.5 = (bf16[32,2176]{1,0:T(8,128)(2,1)S(1)}, bf16[32,2176]{1,0:T(8,128)(2,1)S(1)}, u32[]{:S(2)}, u32[]{:S(2)}) collective-permute-start(bf16[32,2176]{1,0:T(8,128)(2,1)S(1)} %get-tuple-element.21), channel_id=1, source_target_pairs={{0,3},{1,2},{2,1},{3,0},{4,7},{5,6},{6,5},{7,4},{8,11},{9,10},{10,... | collective-permute-start | bytes 417800 | tf_op jit(solution)/shard_map/ppermute | solution.py:362
  28.8 10.9 %collective-permute-start.6 = (bf16[32,2176]{1,0:T(8,128)(2,1)S(1)}, bf16[32,2176]{1,0:T(8,128)(2,1)S(1)}, u32[]{:S(2)}, u32[]{:S(2)}) collective-permute-start(bf16[32,2176]{1,0:T(8,128)(2,1)S(1)} %get-tuple-element.22), channel_id=1, source_target_pairs={{0,2},{1,3},{2,0},{3,1},{4,6},{5,7},{6,4},{7,5},{8,10},{9,11},{10,... | collective-permute-start | bytes 417800 | tf_op jit(solution)/shard_map/ppermute | solution.py:362
  30.6 9.0 %collective-permute-start.7 = (bf16[32,2176]{1,0:T(8,128)(2,1)S(1)}, bf16[32,2176]{1,0:T(8,128)(2,1)S(1)}, u32[]{:S(2)}, u32[]{:S(2)}) collective-permute-start(bf16[32,2176]{1,0:T(8,128)(2,1)S(1)} %get-tuple-element.23), channel_id=1, source_target_pairs={{0,1},{1,0},{2,3},{3,2},{4,5},{5,4},{6,7},{7,6},{8,9},{9,8},{10,11... | collective-permute-start | bytes 417800 | tf_op jit(solution)/shard_map/ppermute | solution.py:362
  31.4 13.9 %collective-permute-start.3 = (bf16[32,2176]{1,0:T(8,128)(2,1)S(1)}, bf16[32,2176]{1,0:T(8,128)(2,1)S(1)}, u32[]{:S(2)}, u32[]{:S(2)}) collective-permute-start(bf16[32,2176]{1,0:T(8,128)(2,1)S(1)} %get-tuple-element.18), channel_id=1, source_target_pairs={{0,5},{1,4},{2,7},{3,6},{4,1},{5,0},{6,3},{7,2},{8,13},{9,12},{10,... | collective-permute-start | bytes 417800 | tf_op jit(solution)/shard_map/ppermute | solution.py:362
  33.1 13.2 %collective-permute-start.4 = (bf16[32,2176]{1,0:T(8,128)(2,1)S(1)}, bf16[32,2176]{1,0:T(8,128)(2,1)S(1)}, u32[]{:S(2)}, u32[]{:S(2)}) collective-permute-start(bf16[32,2176]{1,0:T(8,128)(2,1)S(1)} %get-tuple-element.19), channel_id=1, source_target_pairs={{0,4},{1,5},{2,6},{3,7},{4,0},{5,1},{6,2},{7,3},{8,12},{9,13},{10,... | collective-permute-start | bytes 417800 | tf_op jit(solution)/shard_map/ppermute | solution.py:362
  47.4 2.7 %collective-permute-start.8 = (f32[2048,128]{1,0:T(8,128)S(1)}, f32[2048,128]{1,0:T(8,128)S(1)}, u32[]{:S(2)}, u32[]{:S(2)}) collective-permute-start(f32[2048,128]{1,0:T(8,128)S(1)} %sum_slots.1), channel_id=1, source_target_pairs={{0,8},{8,0},{1,9},{9,1},{2,10},{10,2},{3,11},{11,3},{4,12},{12,4},... | collective-permute-start | bytes 3145736 | tf_op jit(solution)/shard_map/ppermute | solution.py:371

commit v5 on v4

--- a/solution.py
+++ b/solution.py
@@ -5,6 +5,7 @@
 import numpy as np
 from jax import lax
 from jax.experimental import pallas as pl
+from jax.experimental.layout import Layout, with_layout_constraint
 from jax.experimental.pallas import tpu as pltpu
 from jax.sharding import PartitionSpec as P
 
@@ -19,8 +20,8 @@
 GROUP = 8
 QUAD = 4
 TABLES = 12
+COUNT_SPAN = 4096
 PAIRED_MAX = 16
-CALLS = (0, 2, 4, 8)
 VMEM_LIMIT = 48 * 1024 * 1024
 
 
@@ -74,10 +75,11 @@
 
 
 def subgrid_kernel(
-    first, destinations, capacity, order_ref, row_ref, slot_ref, start_ref, count_ref, token_ref,
-    uv_ref, own_ref, other_ref, *refs
+    first, destinations, capacity, block_ref, row_ref, start_ref, token_ref, uv_any, res_ref, *refs
 ):
-    out_refs, next_ref, scratch = refs[:-13], refs[-13], refs[-12:]
+    out_refs, next_ref, uv_ref, uv_sem, scratch = refs[:-15], refs[-15], refs[-14], refs[-13], refs[-12:]
+    fetch = pltpu.make_async_copy(uv_any, uv_ref, uv_sem)
+    fetch.start()
     next_ref[...] = jnp.zeros_like(next_ref)
     gathered, cos_u, sin_u, cos_v, sin_v, dense, left_a, right_a, left_b, right_b, stage, tags = scratch
     tiles = gathered.shape[0] // (4 * GROUP)
@@ -88,7 +90,7 @@
     )
     low, high = start_ref[first], start_ref[first + destinations]
     turns = (high - low + GROUP - 1) // GROUP
-    last = order_ref.shape[0] - 1
+    last = block_ref.shape[0] - 1
 
     def wide(ref, row, stride=1, step=GROUP):
         return jnp.concatenate(
@@ -97,13 +99,11 @@
 
     def tabulate(g):
         for i in range(GROUP):
-            block = order_ref[jnp.minimum(low + g * GROUP + i, last)]
+            packed = block_ref[jnp.minimum(low + g * GROUP + i, last)]
+            block, count = packed // COUNT_SPAN, packed % COUNT_SPAN
             at = pl.ds(pl.multiple_of(block * 2 * tiles, 2 * tiles), 2 * tiles)
             gathered[pl.ds(i, 2 * tiles, stride=GROUP), :] = uv_ref[at, :]
-            two = pl.ds(pl.multiple_of((block // 2) * 4 * tiles, 4 * tiles), 4 * tiles)
-            both = own_ref[two, :].astype(jnp.float32) + other_ref[two, :].astype(jnp.float32)
-            both = jnp.where(block % 2 == 1, both[2 * tiles :], both[: 2 * tiles])
-            both = jnp.where(vis_at < count_ref[block], both, 0.0)
+            both = jnp.where(vis_at < count, res_ref[at, :], 0.0)
             gathered[pl.ds(2 * tiles * GROUP + i, 2 * tiles, stride=GROUP), :] = both
         u, v, re, im = [
             wide(gathered, (k // 2) * 2 * tiles * GROUP + (k % 2) * GROUP, step=2 * GROUP)
@@ -175,7 +175,7 @@
             index = low + turn * QUAD + b
             known = (index >= low) & (index < high)
             index = jnp.clip(index, 0, last)
-            row = jnp.where(known, row_ref[index] - first * capacity, rows)
+            row = jnp.where(known, row_ref[index] // SLOTS - first * capacity, rows)
             for part in range(2):
                 if part == 0:
                     whole = with_cos[:SUB] - with_sin[SUB:]
@@ -188,7 +188,7 @@
                         moved = pltpu.roll(moved, ((k - b) % 4) * SUB, 1)
                     total = moved if total is None else jnp.where(lane == k, moved, total)
                 stage[pl.ds(pl.multiple_of(row * PIECES, PIECES) + part * GROUP, GROUP), :] = total
-            tag = (slot_ref[index] + 1).astype(jnp.float32)
+            tag = (row_ref[index] % SLOTS + 1).astype(jnp.float32)
             tags[pl.ds(row, 1), :] = jnp.full((1, LANES), tag, jnp.float32)
 
     @pl.loop(0, rows // GROUP)
@@ -197,6 +197,7 @@
         stage[pl.ds(at * PIECES, GROUP * PIECES), :] = jnp.zeros((GROUP * PIECES, LANES), jnp.float32)
         tags[pl.ds(at, GROUP), :] = jnp.zeros((GROUP, LANES), jnp.float32)
 
+    fetch.wait()
     pl.loop(0, turns)(tabulate)
 
     @pl.loop(0, turns)
@@ -226,11 +227,11 @@
         at += out_ref.shape[0]
 
 
-def make_subgrids(first, outs, token, capacity, order, row, slot, start, counts, uv, own, other, vis):
+def make_subgrids(first, outs, token, capacity, block, row, start, uv, res, vis):
     tiles = vis // LANES
     destinations = sum(outs)
     rows = destinations * capacity
-    groups = min(rows, order.shape[0]) // GROUP + 1
+    groups = min(rows, block.shape[0]) // GROUP + 1
     vmem = pl.BlockSpec(memory_space=pltpu.VMEM)
     smem = pl.BlockSpec(memory_space=pltpu.SMEM)
     table = pltpu.VMEM((groups * GROUP * GROUP * tiles, LANES), jnp.float32)
@@ -239,9 +240,11 @@
         functools.partial(subgrid_kernel, first, destinations, capacity),
         out_shape=[jax.ShapeDtypeStruct((n * capacity, WIDTH), jnp.bfloat16) for n in outs]
         + [jax.ShapeDtypeStruct(token.shape, token.dtype)],
-        in_specs=[smem] * 5 + [vmem] * 4,
+        in_specs=[smem] * 3 + [vmem, pl.BlockSpec(memory_space=pl.ANY), vmem],
         out_specs=[vmem] * (len(outs) + 1),
         scratch_shapes=[
+            pltpu.VMEM(uv.shape, uv.dtype),
+            pltpu.SemaphoreType.DMA,
             pltpu.VMEM((4 * tiles * GROUP, LANES), jnp.float32),
             table, table, table, table,
             pltpu.VMEM((groups * TABLES * tiles * GROUP, LANES), jnp.float32),
@@ -254,7 +257,7 @@
             flops=rows * 8 * SUB * SUB * vis, bytes_accessed=8 * rows * FEATURE, transcendentals=0
         ),
         name="subgrids",
-    )(order, row, slot, start, counts, token, uv, own, other)
+    )(block, row, start, token, uv, res)
 
 
 def gather_kernel(*refs):
@@ -310,6 +313,10 @@
     return split.transpose(0, 2, 1, 3).reshape(blocks * tiles * parts, LANES)
 
 
+def in_rows(array):
+    return with_layout_constraint(array, Layout(major_to_minor=(0, 1)))
+
+
 def local(residual, uv_offsets, counts, tile_of_block, slot_of_block, owner_map):
     blocks, _, vis = uv_offsets.shape
     owners = owner_map.shape[0]
@@ -317,8 +324,8 @@
     core = lax.axis_index("samp")
     me = lax.axis_index(("blk", "tile"))
     swap = [(0, 1), (1, 0)]
-    own = residual[0]
-    other = lax.ppermute(own, "samp", swap)
+    own = in_rows(rows_of(residual[0]))
+    other = in_rows(lax.ppermute(own, "samp", swap))
 
     tile_ids = tile_of_block[:, 0]
     owner_range = jnp.arange(owners, dtype=jnp.int32)
@@ -337,22 +344,20 @@
     place = jnp.where(mine, before + rank // 2, -1)
     wanted = jnp.arange((blocks + owners) // 2 + GROUP, dtype=jnp.int32)
     chosen = place[None, :] == wanted[:, None]
-    order = jnp.sum(jnp.where(chosen, index[None, :], 0), 1)
-    row = jnp.sum(jnp.where(chosen, (offset * capacity + rank // 2)[None, :], 0), 1)
-    slot = jnp.sum(jnp.where(chosen, slot_of_block[None, :], 0), 1)
+    block_and_count = index * COUNT_SPAN + counts
+    row_and_slot = (offset * capacity + rank // 2) * SLOTS + slot_of_block
+    block = jnp.sum(jnp.where(chosen, block_and_count[None, :], 0), 1)
+    row = jnp.sum(jnp.where(chosen, row_and_slot[None, :], 0), 1)
 
     subgrids = functools.partial(
-        make_subgrids, capacity=capacity, order=order, row=row, slot=slot, start=start,
-        counts=counts, uv=rows_of(uv_offsets), own=rows_of(own), other=rows_of(other), vis=vis,
+        make_subgrids, capacity=capacity, block=block, row=row, start=start, uv=rows_of(uv_offsets),
+        res=own.astype(jnp.float32) + other.astype(jnp.float32), vis=vis,
     )
     token = jnp.zeros((GROUP, LANES), jnp.int32)
     if paired:
-        rows = []
-        for first, last in zip(CALLS[:-1], CALLS[1:]):
-            first, last = owners * first // CALLS[-1], owners * last // CALLS[-1]
-            if first < last:
-                *more, token = subgrids(first, (1,) * (last - first), token)
-                rows += more
+        far = owners * 3 // 8
+        *rows, token = subgrids(0, (1,) * far, token)
+        rows += subgrids(far, (1,) * (owners - far), token)[:-1]
         arrived = []
         for turn in range(owners):
             distance = owners - 1 - turn

time: 51 us -> 47.8 us (0.937)
  local copies, waits for them, and re-layouts: 4.29 us -> 1.31 us
  starting transfers between devices: 14.5 us -> 13.3 us
  other arithmetic: 1.87 us -> 3.05 us
  Pallas kernels: 16.5 us -> 15.4 us
  waiting for transfers between devices: 13.9 us -> 14.5 us
    unnamed x16 -> x10, local copies, waits for them, and re-layouts: 4.29 us -> 1.31 us
    add x1, other arithmetic: 0.01 us -> 1.23 us  [local(): own.astype(jnp.float32) + other.astype(jnp.float32)]
    ppermute x7, starting transfers between devices: 14 us -> 12.8 us  [local(): piece = lax.ppermute(piece, ('blk', 'tile'), pairs)]
    pallas_call x3 -> x2, Pallas kernels: 15.4 us -> 14.2 us  [make_subgrids(): pl.pallas_call(functools.partial(subgrid_kernel, first, destinations, cap...]
    ppermute x7, waiting for transfers between devices: 11.3 us -> 11.9 us  [local(): piece = lax.ppermute(piece, ('blk', 'tile'), pairs)]
  transfers between devices with their start and end apart: 9 -> 9, of which waited for: 5 -> 5; matrix products, arithmetic and copies ran while one was open for 2% -> 2% of each run, Pallas kernels for 24% -> 18%
where the time goes in v5:
time: 47.8 us; the launch traced here: 47.7 us
  Pallas kernels  15.4 us (32%)
  waiting for transfers between devices  14.5 us (30%)
  starting transfers between devices  13.3 us (28%)
  other arithmetic  3.05 us (6%)
  local copies, waits for them, and re-layouts  1.31 us (3%)
    pallas_call x2, Pallas kernels, make_subgrids(): pl.pallas_call(functools.partial(subgrid_kernel, first, destinations, cap...  14.2 us
    ppermute x7, starting transfers between devices, local(): piece = lax.ppermute(piece, ('blk', 'tile'), pairs)  12.8 us
    ppermute x7, waiting for transfers between devices, local(): piece = lax.ppermute(piece, ('blk', 'tile'), pairs)  11.9 us
    ppermute x1, waiting for transfers between devices, local(): whole = part + lax.ppermute(part, 'samp', swap)  2.65 us
    unnamed x10, local copies, waits for them, and re-layouts  1.31 us
    add x1, other arithmetic, local(): own.astype(jnp.float32) + other.astype(jnp.float32)  1.23 us
    pallas_call x1, Pallas kernels, sum_slots(): pl.pallas_call(gather_kernel, out_shape=jax.ShapeDtypeStruct((SUB * 64, L...  1.16 us
    add x1, other arithmetic, local(): whole = part + lax.ppermute(part, 'samp', swap)  1.08 us
  transfers between devices with their start and end apart: 9, of which 5 were waited for; matrix products, arithmetic and copies ran while one was open for 2% of the time, Pallas kernels for 18%

profile of v5, /device:TPU:0, one launch (start us, length us, event | category | flops | bytes accessed | tf_op | source)
XLA Modules:
  0.0 47.7 jit_solution(16889651550863334164)
XLA Ops:
  0.0 0.5 collective-permute-start
  0.5 0.0 copy-start.3
  0.5 0.0 copy-start.4
  0.5 0.7 %copy-done.3 = s32[256,1]{0,1:T(1,128)S(1)} copy-done((s32[256,1]{0,1:T(1,128)S(1)}, s32[256,1]{0,1:T(1,128)}, u32[]{:S(2)}) %copy-start.3) | copy-done | bytes 1048
  1.1 0.0 copy-done.4
  1.1 0.1 select_reduce_fusion.2
  1.2 0.2 convert_reduce_fusion.1
  1.4 0.1 convert_reduce_fusion.2.start_ref
  1.5 0.0 copy-start.1
  1.6 0.0 copy-start.2
  1.6 0.2 convert_reduce_fusion
  1.7 0.5 %copy-done.1 = s32[256]{0:T(256)S(1)} copy-done((s32[256]{0:T(256)S(1)}, s32[256]{0:T(256)}, u32[]{:S(2)}) %copy-start.1) | copy-done | bytes 1048
  2.2 0.0 copy-done.2
  2.3 0.2 select_reduce_fusion
  2.4 0.0 copy-start
  2.4 0.0 collective-permute-done
  2.4 1.2 %convert_add_fusion.res_ref = f32[2048,128]{1,0:T(8,128)S(1)} fusion(bf16[2048,128]{1,0:T(8,128)(2,1)S(1)} %collective-permute-done, bf16[2048,128]{1,0:T(8,128)(2,1)} %bitcast.19), kind=kLoop, calls=%fused_computation | loop fusion | flops 786432 | bytes 2097152 | tf_op jit(solution)/shard_map/add | solution.py:354
  3.7 0.1 copy-done
  3.8 5.8 %subgrids.2 = (bf16[32,2176]{1,0:T(8,128)(2,1)S(1)}, bf16[32,2176]{1,0:T(8,128)(2,1)S(1)}, bf16[32,2176]{1,0:T(8,128)(2,1)S(1)}, s32[8,128]{1,0:T(8,128)S(1)}) custom-call(s32[140]{0:T(256)S(1)} %get-tuple-element.24.block_ref, s32[140]{0:T(256)S(1)} %get-tuple-element.23.row_ref, s32[9]{0:T(128)S(1)} %convert_reduce_fusion.2.start_ref, ...), custom_call_target="tpu_custom_call" | custom-call | flops 402653184 | bytes 1572864 | tf_op jit(solution)/shard_map/subgrids/pallas_call | solution.py:239
  9.6 5.6 %collective-permute-start.1 = (bf16[32,2176]{1,0:T(8,128)(2,1)S(1)}, bf16[32,2176]{1,0:T(8,128)(2,1)S(1)}, u32[]{:S(2)}, u32[]{:S(2)}) collective-permute-start(bf16[32,2176]{1,0:T(8,128)(2,1)S(1)} %get-tuple-element.14), channel_id=1, source_target_pairs={{0,7},{1,6},{2,5},{3,4},{4,3},{5,2},{6,1},{7,0},{8,15},{9,14},{10,... | collective-permute-start | bytes 417800 | tf_op jit(solution)/shard_map/ppermute | solution.py:367
  15.2 0.0 collective-permute-start.2
  15.2 1.0 %collective-permute-start.3 = (bf16[32,2176]{1,0:T(8,128)(2,1)S(1)}, bf16[32,2176]{1,0:T(8,128)(2,1)S(1)}, u32[]{:S(2)}, u32[]{:S(2)}) collective-permute-start(bf16[32,2176]{1,0:T(8,128)(2,1)S(1)} %get-tuple-element.16), channel_id=1, source_target_pairs={{0,5},{1,4},{2,7},{3,6},{4,1},{5,0},{6,3},{7,2},{8,13},{9,12},{10,... | collective-permute-start | bytes 417800 | tf_op jit(solution)/shard_map/ppermute | solution.py:367
  16.2 8.5 %subgrids.3 = (bf16[32,2176]{1,0:T(8,128)(2,1)S(1)}, bf16[32,2176]{1,0:T(8,128)(2,1)S(1)}, bf16[32,2176]{1,0:T(8,128)(2,1)S(1)}, bf16[32,2176]{1,0:T(8,128)(2,1)...) custom-call(s32[140]{0:T(256)S(1)} %get-tuple-element.24.block_ref, s32[140]{0:T(256)S(1)} %get-tuple-element.23.row_ref, ...), custom_call_target="tpu_custom_call" | custom-call | flops 671088640 | bytes 2621440 | tf_op jit(solution)/shard_map/subgrids/pallas_call | solution.py:239
  24.7 2.1 %collective-permute-start.4 = (bf16[32,2176]{1,0:T(8,128)(2,1)S(1)}, bf16[32,2176]{1,0:T(8,128)(2,1)S(1)}, u32[]{:S(2)}, u32[]{:S(2)}) collective-permute-start(bf16[32,2176]{1,0:T(8,128)(2,1)S(1)} %get-tuple-element.18), channel_id=1, source_target_pairs={{0,4},{1,5},{2,6},{3,7},{4,0},{5,1},{6,2},{7,3},{8,12},{9,13},{10,... | collective-permute-start | bytes 417800 | tf_op jit(solution)/shard_map/ppermute | solution.py:367
  26.7 1.7 %collective-permute-start.5 = (bf16[32,2176]{1,0:T(8,128)(2,1)S(1)}, bf16[32,2176]{1,0:T(8,128)(2,1)S(1)}, u32[]{:S(2)}, u32[]{:S(2)}) collective-permute-start(bf16[32,2176]{1,0:T(8,128)(2,1)S(1)} %get-tuple-element.19), channel_id=1, source_target_pairs={{0,3},{1,2},{2,1},{3,0},{4,7},{5,6},{6,5},{7,4},{8,11},{9,10},{10,... | collective-permute-start | bytes 417800 | tf_op jit(solution)/shard_map/ppermute | solution.py:367
  28.5 0.0 collective-permute-done.1.refs_0_
  28.5 2.4 %collective-permute-start.6 = (bf16[32,2176]{1,0:T(8,128)(2,1)S(1)}, bf16[32,2176]{1,0:T(8,128)(2,1)S(1)}, u32[]{:S(2)}, u32[]{:S(2)}) collective-permute-start(bf16[32,2176]{1,0:T(8,128)(2,1)S(1)} %get-tuple-element.20), channel_id=1, source_target_pairs={{0,2},{1,3},{2,0},{3,1},{4,6},{5,7},{6,4},{7,5},{8,10},{9,11},{10,... | collective-permute-start | bytes 417800 | tf_op jit(solution)/shard_map/ppermute | solution.py:367
  30.9 0.0 collective-permute-done.2.refs_1_
  30.9 0.0 collective-permute-start.7
  30.9 6.2 %collective-permute-done.3.refs_2_ = bf16[32,2176]{1,0:T(8,128)(2,1)S(1)} collective-permute-done((bf16[32,2176]{1,0:T(8,128)(2,1)S(1)}, bf16[32,2176]{1,0:T(8,128)(2,1)S(1)}, u32[]{:S(2)}, u32[]{:S(2)}) %collective-permute-start.3) | collective-permute-done | bytes 139296 | tf_op jit(solution)/shard_map/ppermute | solution.py:367
  37.0 2.4 %collective-permute-done.4.refs_3_ = bf16[32,2176]{1,0:T(8,128)(2,1)S(1)} collective-permute-done((bf16[32,2176]{1,0:T(8,128)(2,1)S(1)}, bf16[32,2176]{1,0:T(8,128)(2,1)S(1)}, u32[]{:S(2)}, u32[]{:S(2)}) %collective-permute-start.4) | collective-permute-done | bytes 139296 | tf_op jit(solution)/shard_map/ppermute | solution.py:367
  39.5 0.2 collective-permute-done.5.refs_4_
  39.7 3.0 %collective-permute-done.6.refs_5_ = bf16[32,2176]{1,0:T(8,128)(2,1)S(1)} collective-permute-done((bf16[32,2176]{1,0:T(8,128)(2,1)S(1)}, bf16[32,2176]{1,0:T(8,128)(2,1)S(1)}, u32[]{:S(2)}, u32[]{:S(2)}) %collective-permute-start.6) | collective-permute-done | bytes 139296 | tf_op jit(solution)/shard_map/ppermute | solution.py:367
  42.7 0.0 collective-permute-done.7.refs_6_
  42.7 1.2 %sum_slots.1 = f32[2048,128]{1,0:T(8,128)S(1)} custom-call(bf16[32,2176]{1,0:T(8,128)(2,1)S(1)} %collective-permute-done.1.refs_0_, bf16[32,2176]{1,0:T(8,128)(2,1)S(1)} %collective-permute-done.2.refs_1_, bf16[32,2176]{1,0:T(8,128)(2,1)S(1)} %collective-permute-done.3.refs_2_, bf16[32,2176]{1,0:T(8,128)(2,1)S(1)} %collective-permute-done.4.refs_3_, ...), custom_call_target="tpu_custom_call" | custom-call | tf_op jit(solution)/shard_map/sum_slots/pallas_call | solution.py:294
  43.9 0.1 collective-permute-start.8
  44.0 2.6 %collective-permute-done.8 = f32[2048,128]{1,0:T(8,128)S(1)} collective-permute-done((f32[2048,128]{1,0:T(8,128)S(1)}, f32[2048,128]{1,0:T(8,128)S(1)}, u32[]{:S(2)}, u32[]{:S(2)}) %collective-permute-start.8) | collective-permute-done | bytes 1048608 | tf_op jit(solution)/shard_map/ppermute | solution.py:376
  46.6 1.1 %add.36 = f32[2048,128]{1,0:T(8,128)} add(f32[2048,128]{1,0:T(8,128)S(1)} %sum_slots.1, f32[2048,128]{1,0:T(8,128)S(1)} %collective-permute-done.8) | non-fusion elementwise | flops 262144 | bytes 3145728 | tf_op jit(solution)/shard_map/add | solution.py:376
  (4 shorter events, 0.0 us)
Async XLA Ops:
  0.0 2.4 %collective-permute-start = (bf16[2048,128]{1,0:T(8,128)(2,1)}, bf16[2048,128]{1,0:T(8,128)(2,1)S(1)}, u32[]{:S(2)}, u32[]{:S(2)}) collective-permute-start(bf16[2048,128]{1,0:T(8,128)(2,1)} %bitcast.18), channel_id=1, source_target_pairs={{0,8},{8,0},{1,9},{9,1},{2,10},{10,2},{3,11},{11,3},{4,12},{12,4},... | collective-permute-start | bytes 1572872 | tf_op jit(solution)/shard_map/ppermute | solution.py:328
  0.5 0.7 %copy-start.3 = (s32[256,1]{0,1:T(1,128)S(1)}, s32[256,1]{0,1:T(1,128)}, u32[]{:S(2)}) copy-start(s32[256,1]{0,1:T(1,128)} %param.9) | copy-start | bytes 3076
  0.5 0.7 %copy-start.4 = (s32[8]{0:T(128)S(1)}, s32[8]{0:T(128)}, u32[]{:S(2)}) copy-start(s32[8]{0:T(128)} %param.11) | copy-start | bytes 100
  1.5 0.7 %copy-start.1 = (s32[256]{0:T(256)S(1)}, s32[256]{0:T(256)}, u32[]{:S(2)}) copy-start(s32[256]{0:T(256)} %param.10) | copy-start | bytes 3076
  1.6 0.7 %copy-start.2 = (s32[256]{0:T(256)S(1)}, s32[256]{0:T(256)}, u32[]{:S(2)}) copy-start(s32[256]{0:T(256)} %param.8) | copy-start | bytes 3076
  2.4 1.4 %copy-start = (f32[256,2,512]{2,1,0:T(2,128)S(1)}, f32[256,2,512]{2,1,0:T(2,128)}, u32[]{:S(2)}) copy-start(f32[256,2,512]{2,1,0:T(2,128)} %param.7) | copy-start | bytes 3145732
  9.6 18.9 %collective-permute-start.1 = (bf16[32,2176]{1,0:T(8,128)(2,1)S(1)}, bf16[32,2176]{1,0:T(8,128)(2,1)S(1)}, u32[]{:S(2)}, u32[]{:S(2)}) collective-permute-start(bf16[32,2176]{1,0:T(8,128)(2,1)S(1)} %get-tuple-element.14), channel_id=1, source_target_pairs={{0,7},{1,6},{2,5},{3,4},{4,3},{5,2},{6,1},{7,0},{8,15},{9,14},{10,... | collective-permute-start | bytes 417800 | tf_op jit(solution)/shard_map/ppermute | solution.py:367
  15.2 15.7 %collective-permute-start.2 = (bf16[32,2176]{1,0:T(8,128)(2,1)S(1)}, bf16[32,2176]{1,0:T(8,128)(2,1)S(1)}, u32[]{:S(2)}, u32[]{:S(2)}) collective-permute-start(bf16[32,2176]{1,0:T(8,128)(2,1)S(1)} %get-tuple-element.15), channel_id=1, source_target_pairs={{0,6},{1,7},{2,4},{3,5},{4,2},{5,3},{6,0},{7,1},{8,14},{9,15},{10,... | collective-permute-start | bytes 417800 | tf_op jit(solution)/shard_map/ppermute | solution.py:367
  15.2 21.9 %collective-permute-start.3 = (bf16[32,2176]{1,0:T(8,128)(2,1)S(1)}, bf16[32,2176]{1,0:T(8,128)(2,1)S(1)}, u32[]{:S(2)}, u32[]{:S(2)}) collective-permute-start(bf16[32,2176]{1,0:T(8,128)(2,1)S(1)} %get-tuple-element.16), channel_id=1, source_target_pairs={{0,5},{1,4},{2,7},{3,6},{4,1},{5,0},{6,3},{7,2},{8,13},{9,12},{10,... | collective-permute-start | bytes 417800 | tf_op jit(solution)/shard_map/ppermute | solution.py:367
  24.7 14.8 %collective-permute-start.4 = (bf16[32,2176]{1,0:T(8,128)(2,1)S(1)}, bf16[32,2176]{1,0:T(8,128)(2,1)S(1)}, u32[]{:S(2)}, u32[]{:S(2)}) collective-permute-start(bf16[32,2176]{1,0:T(8,128)(2,1)S(1)} %get-tuple-element.18), channel_id=1, source_target_pairs={{0,4},{1,5},{2,6},{3,7},{4,0},{5,1},{6,2},{7,3},{8,12},{9,13},{10,... | collective-permute-start | bytes 417800 | tf_op jit(solution)/shard_map/ppermute | solution.py:367
  26.7 12.9 %collective-permute-start.5 = (bf16[32,2176]{1,0:T(8,128)(2,1)S(1)}, bf16[32,2176]{1,0:T(8,128)(2,1)S(1)}, u32[]{:S(2)}, u32[]{:S(2)}) collective-permute-start(bf16[32,2176]{1,0:T(8,128)(2,1)S(1)} %get-tuple-element.19), channel_id=1, source_target_pairs={{0,3},{1,2},{2,1},{3,0},{4,7},{5,6},{6,5},{7,4},{8,11},{9,10},{10,... | collective-permute-start | bytes 417800 | tf_op jit(solution)/shard_map/ppermute | solution.py:367
  28.5 14.3 %collective-permute-start.6 = (bf16[32,2176]{1,0:T(8,128)(2,1)S(1)}, bf16[32,2176]{1,0:T(8,128)(2,1)S(1)}, u32[]{:S(2)}, u32[]{:S(2)}) collective-permute-start(bf16[32,2176]{1,0:T(8,128)(2,1)S(1)} %get-tuple-element.20), channel_id=1, source_target_pairs={{0,2},{1,3},{2,0},{3,1},{4,6},{5,7},{6,4},{7,5},{8,10},{9,11},{10,... | collective-permute-start | bytes 417800 | tf_op jit(solution)/shard_map/ppermute | solution.py:367
  30.9 11.9 %collective-permute-start.7 = (bf16[32,2176]{1,0:T(8,128)(2,1)S(1)}, bf16[32,2176]{1,0:T(8,128)(2,1)S(1)}, u32[]{:S(2)}, u32[]{:S(2)}) collective-permute-start(bf16[32,2176]{1,0:T(8,128)(2,1)S(1)} %get-tuple-element.21), channel_id=1, source_target_pairs={{0,1},{1,0},{2,3},{3,2},{4,5},{5,4},{6,7},{7,6},{8,9},{9,8},{10,11... | collective-permute-start | bytes 417800 | tf_op jit(solution)/shard_map/ppermute | solution.py:367
  43.9 2.7 %collective-permute-start.8 = (f32[2048,128]{1,0:T(8,128)S(1)}, f32[2048,128]{1,0:T(8,128)S(1)}, u32[]{:S(2)}, u32[]{:S(2)}) collective-permute-start(f32[2048,128]{1,0:T(8,128)S(1)} %sum_slots.1), channel_id=1, source_target_pairs={{0,8},{8,0},{1,9},{9,1},{2,10},{10,2},{3,11},{11,3},{4,12},{12,4},... | collective-permute-start | bytes 3145736 | tf_op jit(solution)/shard_map/ppermute | solution.py:376

commit v6 on v5

v6 whole, which is shorter than its diff:
```python
import functools

import jax
import jax.numpy as jnp
import numpy as np
from jax import lax
from jax.experimental import pallas as pl
from jax.experimental.layout import Layout, with_layout_constraint
from jax.experimental.pallas import tpu as pltpu
from jax.sharding import PartitionSpec as P

SUB = 32
STEPS = SUB // 2
SLOTS = 128
LANES = 128
FEATURE = 2 * SUB * SUB
PIECES = FEATURE // LANES
CAP_MIN = 8
GROUP = 8
QUAD = 4
TAG_ROWS = 16
COUNT_SPAN = 4096
PAIRED_MAX = 16
VMEM_LIMIT = 48 * 1024 * 1024


def turn_coefficients():
    knots = np.cos(np.pi * (np.arange(400) + 0.5) / 400)
    cheb = np.polynomial.chebyshev
    even = cheb.cheb2poly(cheb.chebfit(knots, np.cos(np.pi * knots), 12))[0::2]
    odd = cheb.cheb2poly(cheb.chebfit(knots, np.sin(np.pi * knots), 13))[1::2]
    return [float(x) for x in even], [float(x) for x in odd]


COS_COEF, SIN_COEF = turn_coefficients()


def horner(coef, x):
    total = coef[-1] * x + coef[-2]
    for value in coef[-3::-1]:
        total = total * x + value
    return total


def first_angle(offset):
    y = offset * (1.0 / STEPS)
    x = y * y
    return horner(COS_COEF, x), horner(SIN_COEF, x) * y


def tile_of(value, t):
    return value[:, t * LANES : (t + 1) * LANES]


def by_quad(even, odd):
    top = lax.broadcasted_iota(jnp.int32, even.shape, 0) < QUAD
    return (
        jnp.where(top, even, pltpu.roll(odd, QUAD, 0)),
        jnp.where(top, pltpu.roll(even, QUAD, 0), odd),
    )


def sequence(before, middle, factor):
    values = [None] * STEPS
    values[STEPS // 2 - 1], values[STEPS // 2] = before, middle
    for j in range(STEPS // 2 + 1, STEPS):
        values[j] = factor * values[j - 1] - values[j - 2]
    for j in range(STEPS // 2 - 2, -1, -1):
        values[j] = factor * values[j + 1] - values[j + 2]
    return values


def subgrid_kernel(
    first, destinations, capacity, block_ref, row_ref, start_ref, token_ref, uv_any, res_ref, *refs
):
    out_refs, (next_ref, uv_ref, uv_sem, gathered, found, tags, mover) = refs[:-7], refs[-7:]
    fetch = pltpu.make_async_copy(uv_any, uv_ref, uv_sem)
    fetch.start()
    next_ref[...] = jnp.zeros_like(next_ref)
    tiles = gathered.shape[0] // (4 * GROUP)
    spare = destinations * capacity // QUAD
    low, high = start_ref[first], start_ref[first + destinations]
    last = block_ref.shape[0] - 1
    vis_at = lax.broadcasted_iota(jnp.int32, (2 * tiles, LANES), 1) + LANES * (
        lax.broadcasted_iota(jnp.int32, (2 * tiles, LANES), 0) // 2
    )
    same_block = (
        lax.broadcasted_iota(jnp.int32, (2 * STEPS * QUAD, LANES), 0) % QUAD
        == lax.broadcasted_iota(jnp.int32, (2 * STEPS * QUAD, LANES), 1) % QUAD
    )
    quad_row = lax.broadcasted_iota(jnp.int32, (QUAD, LANES), 0)
    top = lax.broadcasted_iota(jnp.int32, (GROUP, LANES), 0) < QUAD

    source = lax.broadcasted_iota(jnp.int32, mover.shape, 0)
    lane = lax.broadcasted_iota(jnp.int32, mover.shape, 1)
    moves = (source // LANES == lane // SUB) & (source % LANES // QUAD == lane % SUB)
    mover[...] = jnp.where(moves, 1.0, 0.0).astype(jnp.bfloat16)
    tags[...] = jnp.zeros_like(tags)
    fetch.wait()

    @pl.loop(0, (high - low + 1) // 2)
    def _(g):
        quad_at = low + 2 * g
        for i in range(GROUP):
            packed = block_ref[jnp.minimum(quad_at * QUAD + i, last)]
            block, count = packed // COUNT_SPAN, packed % COUNT_SPAN
            at = pl.ds(pl.multiple_of(block * 2 * tiles, 2 * tiles), 2 * tiles)
            both = jnp.where(vis_at < count, res_ref[at, :], 0.0)
            gathered[pl.ds(i, 2 * tiles, stride=GROUP), :] = uv_ref[at, :]
            gathered[pl.ds(2 * tiles * GROUP + i, 2 * tiles, stride=GROUP), :] = both
        u, v, re, im = [
            jnp.concatenate(
                [
                    gathered[pl.ds(((k // 2) * 2 * tiles + 2 * t + k % 2) * GROUP, GROUP), :]
                    for t in range(tiles)
                ],
                1,
            )
            for k in range(4)
        ]
        c, s = first_angle(u)
        a, b, e, f = re * c, im * s, im * c, re * s
        after = (a - b, e + f)
        before = (a + b, e - f)
        second = [2.0 * c * near - far for near, far in zip(before, (re, im))]
        left_mid = [by_quad(x, y) for x, y in zip((re, im), after)]
        left_low = [by_quad(x, y) for x, y in zip(second, before)]
        factor = 2.0 - 4.0 * s * s
        left_factor = by_quad(factor, factor)
        c, s = first_angle(v)
        c2, s2 = 1.0 - 2.0 * s * s, 2.0 * s * c
        right_mid = [by_quad(jnp.ones_like(c), c), by_quad(jnp.zeros_like(s), s)]
        right_low = [by_quad(c2, c), by_quad(-s2, -s)]
        factor = 2.0 * c2
        right_factor = by_quad(factor, factor)
        for quad in range(2):
            left, right = [], []
            for part in range(2):
                left += sequence(left_low[part][quad], left_mid[part][quad], left_factor[quad])
                right += sequence(right_low[part][quad], right_mid[part][quad], right_factor[quad])
            product = lax.dot_general(
                jnp.concatenate(left, 0).astype(jnp.bfloat16),
                jnp.concatenate(right, 0).astype(jnp.bfloat16),
                (((1,), (1,)), ((), ())),
                preferred_element_type=jnp.float32,
            )
            half = product.shape[0] // 2
            wholes = (
                product[:half, :LANES] - product[half:, LANES:],
                product[half:, :LANES] + product[:half, LANES:],
            )
            rows = []
            for whole in wholes:
                whole = jnp.where(same_block, whole, 0.0)
                for j in range(0, STEPS, 4):
                    four = [whole[(j + k) * GROUP : (j + k + 1) * GROUP] for k in range(4)]
                    rows.append(jnp.concatenate(four, 1))
            index = (quad_at + quad) * QUAD
            known = quad_at + quad < high
            index = jnp.minimum(index, last + 1 - QUAD)
            place = row_ref[index] // (2 * SLOTS * QUAD) - first * (capacity // QUAD)
            place = jnp.where(known, place, spare)
            found[place] = jnp.concatenate(rows, 0).astype(jnp.bfloat16)
            tag = jnp.zeros((QUAD, LANES), jnp.int32)
            for b in range(QUAD):
                tag = jnp.where(quad_row == b, row_ref[index + b] % (2 * SLOTS), tag)
            tags[place] = tag.astype(jnp.float32)

    shares = capacity // TAG_ROWS
    share = lax.broadcasted_iota(jnp.int32, (TAG_ROWS, LANES), 1) // (LANES // shares)
    for d, out_ref in enumerate(out_refs):
        for m in range(out_ref.shape[0] // message_rows(capacity)):
            base = m * message_rows(capacity)
            sent = start_ref[first + d + m + 1] - start_ref[first + d + m]
            slot = (d + m) * (capacity // QUAD)
            tag = jnp.zeros((TAG_ROWS, LANES), jnp.float32)
            for n in range(shares):
                at = slot + n * 4
                four = jnp.concatenate([tags[at + k] for k in range(4)], 0)
                tag = jnp.where(share == n, four, tag)
                rows = jnp.concatenate([found[at + k] for k in range(4)], 0)
                moved = jnp.dot(rows, mover[...], preferred_element_type=jnp.float32)
                for piece in range(PIECES // 2):
                    part = []
                    for k in range(4):
                        value = moved[(k * 8 + piece) * GROUP : (k * 8 + piece + 1) * GROUP]
                        part.append(jnp.where(n * 4 + k < sent, value, 0.0))
                    for parity in range(2):
                        pair = []
                        for k in (0, 2):
                            if parity == 0:
                                pair.append(jnp.where(top, part[k], pltpu.roll(part[k + 1], QUAD, 0)))
                            else:
                                pair.append(jnp.where(top, pltpu.roll(part[k], QUAD, 0), part[k + 1]))
                        put = base + (piece * 2 + parity) * capacity + n * TAG_ROWS
                        out_ref[pl.ds(put, TAG_ROWS), :] = jnp.concatenate(pair, 0).astype(jnp.bfloat16)
            out_ref[pl.ds(base + PIECES * capacity, TAG_ROWS), :] = tag.astype(jnp.bfloat16)


def message_rows(capacity):
    return PIECES * capacity + TAG_ROWS


def make_subgrids(first, outs, token, capacity, block, row, start, uv, res, vis):
    tiles = vis // LANES
    destinations = sum(outs)
    quads = destinations * capacity // QUAD
    vmem = pl.BlockSpec(memory_space=pltpu.VMEM)
    smem = pl.BlockSpec(memory_space=pltpu.SMEM)
    return pl.pallas_call(
        functools.partial(subgrid_kernel, first, destinations, capacity),
        out_shape=[
            jax.ShapeDtypeStruct((n * message_rows(capacity), LANES), jnp.bfloat16) for n in outs
        ]
        + [jax.ShapeDtypeStruct(token.shape, token.dtype)],
        in_specs=[smem] * 3 + [vmem, pl.BlockSpec(memory_space=pl.ANY), vmem],
        out_specs=[vmem] * (len(outs) + 1),
        scratch_shapes=[
            pltpu.VMEM(uv.shape, uv.dtype),
            pltpu.SemaphoreType.DMA,
            pltpu.VMEM((4 * tiles * GROUP, LANES), jnp.float32),
            pltpu.VMEM((quads + 1, FEATURE // SUB, 4 * LANES), jnp.bfloat16),
            pltpu.VMEM((quads + 1, QUAD, LANES), jnp.float32),
            pltpu.VMEM((4 * LANES, LANES), jnp.bfloat16),
        ],
        compiler_params=pltpu.CompilerParams(vmem_limit_bytes=VMEM_LIMIT),
        cost_estimate=pl.CostEstimate(
            flops=quads * 32 * SUB * SUB * vis, bytes_accessed=16 * quads * FEATURE, transcendentals=0
        ),
        name="subgrids",
    )(block, row, start, token, uv, res)


def gather_kernel(capacity, *refs):
    x_refs, (out_ref, xs, tags, hot, part) = refs[:-5], refs[-5:]
    lane = lax.broadcasted_iota(jnp.int32, (GROUP, LANES), 1) // SUB
    shares = capacity // TAG_ROWS
    at = 0
    for x_ref in x_refs:
        for base in range(0, x_ref.shape[0], message_rows(capacity)):
            for piece in range(PIECES):
                xs[piece, pl.ds(at, capacity), :] = x_ref[pl.ds(base + piece * capacity, capacity), :]
            tag = x_ref[pl.ds(base + PIECES * capacity, TAG_ROWS), :].astype(jnp.float32)
            for n in range(shares):
                column = n * (LANES // shares)
                tags[pl.ds(at + n * TAG_ROWS, TAG_ROWS), :] = jnp.broadcast_to(
                    tag[:, column : column + 1], (TAG_ROWS, LANES)
                )
            at += capacity
    wanted = lax.broadcasted_iota(jnp.int32, tags.shape, 1)
    wanted = (wanted % 32) * 4 + wanted // 32 + 1
    hot[...] = jnp.where(tags[...] == wanted.astype(jnp.float32), 1.0, 0.0).T.astype(jnp.bfloat16)
    for piece in range(PIECES):
        c, rows, parity = piece // 8, piece // 2 % 4, piece % 2
        part[...] = jnp.dot(hot[...], xs[piece], preferred_element_type=jnp.float32)
        for grp in range(4):
            given = [part[pl.ds(32 * jl + 8 * grp, 8), :] for jl in range(4)]
            for a in range(4):
                total = None
                for jl in range(4):
                    moved = given[jl]
                    if a != jl:
                        moved = pltpu.roll(moved, ((jl - a) % 4) * SUB, 1)
                    total = moved if total is None else jnp.where(lane == jl, moved, total)
                p = rows * 8 + a * 2 + parity
                out_ref[pl.ds(p * 64 + grp * 16 + c, 8, stride=2), :] = total


def sum_slots(arrived, capacity):
    rows = sum(x.shape[0] for x in arrived) // message_rows(capacity) * capacity
    vmem = pl.BlockSpec(memory_space=pltpu.VMEM)
    return pl.pallas_call(
        functools.partial(gather_kernel, capacity),
        out_shape=jax.ShapeDtypeStruct((SUB * 64, LANES), jnp.float32),
        in_specs=[vmem] * len(arrived),
        out_specs=vmem,
        scratch_shapes=[
            pltpu.VMEM((PIECES, rows, LANES), jnp.bfloat16),
            pltpu.VMEM((rows, LANES), jnp.float32),
            pltpu.VMEM((SLOTS, rows), jnp.bfloat16),
            pltpu.VMEM((SLOTS, LANES), jnp.float32),
        ],
        compiler_params=pltpu.CompilerParams(vmem_limit_bytes=VMEM_LIMIT),
        name="sum_slots",
    )(*arrived)


def rows_of(array):
    blocks, parts, vis = array.shape
    tiles = vis // LANES
    split = array.reshape(blocks, parts, tiles, LANES)
    return split.transpose(0, 2, 1, 3).reshape(blocks * tiles * parts, LANES)


def in_rows(array):
    return with_layout_constraint(array, Layout(major_to_minor=(0, 1)))


def local(residual, uv_offsets, counts, tile_of_block, slot_of_block, owner_map):
    blocks, _, vis = uv_offsets.shape
    owners = owner_map.shape[0]
    capacity = -(-max(CAP_MIN, 2 * blocks // owners) // 32) * 16
    core = lax.axis_index("samp")
    me = lax.axis_index(("blk", "tile"))
    swap = [(0, 1), (1, 0)]
    own = in_rows(rows_of(residual[0]))
    other = in_rows(lax.ppermute(own, "samp", swap))

    tile_ids = tile_of_block[:, 0]
    owner_range = jnp.arange(owners, dtype=jnp.int32)
    owner_ids = jnp.sum(
        jnp.where(tile_ids[:, None] == owner_range[None, :], owner_map[None, :], 0), 1
    )
    paired = owners <= PAIRED_MAX and owners & (owners - 1) == 0
    offset = (owners - 1) - jnp.bitwise_xor(owner_ids, me) if paired else owner_ids
    index = jnp.arange(blocks, dtype=jnp.int32)
    same = (offset[None, :] == offset[:, None]) & (index[None, :] < index[:, None])
    rank = jnp.sum(same.astype(jnp.int32), 1)
    mine = (rank & 1) == core
    counted = jnp.sum((mine[None, :] & (offset[None, :] == owner_range[:, None])).astype(jnp.int32), 1)
    quads = (counted + QUAD - 1) // QUAD
    edges = jnp.arange(owners + 1, dtype=jnp.int32)
    start = jnp.sum(jnp.where(owner_range[None, :] < edges[:, None], quads[None, :], 0), 1)
    before = jnp.sum(jnp.where(owner_range[None, :] < offset[:, None], quads[None, :], 0), 1)
    place = jnp.where(mine, before * QUAD + rank // 2, -1)
    longest = ((blocks + owners) // 2 + owners * (QUAD - 1)) // GROUP * GROUP + GROUP
    wanted = jnp.arange(longest, dtype=jnp.int32)
    chosen = place[None, :] == wanted[:, None]
    block_and_count = index * COUNT_SPAN + counts
    row_and_tag = (offset * capacity + rank // 2) * (2 * SLOTS) + slot_of_block + 1
    block = jnp.sum(jnp.where(chosen, block_and_count[None, :], 0), 1)
    row = jnp.sum(jnp.where(chosen, row_and_tag[None, :], 0), 1)

    subgrids = functools.partial(
        make_subgrids, capacity=capacity, block=block, row=row, start=start, uv=rows_of(uv_offsets),
        res=own.astype(jnp.float32) + other.astype(jnp.float32), vis=vis,
    )
    token = jnp.zeros((GROUP, LANES), jnp.int32)
    if paired:
        far = owners * 3 // 8
        *rows, token = subgrids(0, (1,) * far, token)
        rows += subgrids(far, (1,) * (owners - far), token)[:-1]
        arrived = []
        for turn in range(owners):
            distance = owners - 1 - turn
            piece = rows[turn]
            if distance:
                pairs = [(k, k ^ distance) for k in range(owners)]
                piece = lax.ppermute(piece, ("blk", "tile"), pairs)
            arrived.append(piece)
    else:
        each = max(d for d in range(1, 17) if owners % d == 0)
        rows = [subgrids(k, (each,), token)[0] for k in range(0, owners, each)]
        rows = jnp.concatenate(rows, 0).reshape(owners, message_rows(capacity), LANES)
        rows = lax.all_to_all(rows, ("blk", "tile"), split_axis=0, concat_axis=0, tiled=True)
        arrived = [rows.reshape(owners * message_rows(capacity), LANES)]
    part = sum_slots(arrived, capacity)
    whole = part + lax.ppermute(part, "samp", swap)
    whole = whole.reshape(SUB, SLOTS // 4, 2, LANES).transpose(0, 2, 1, 3)
    return whole.reshape(SUB, 2, SLOTS * SUB)


def solution(mesh):
    in_specs = (
        P("samp", ("cuts", "blk", "tile"), None, None),
        P(("cuts", "blk", "tile"), None, None),
        P(("cuts", "blk", "tile")),
        P(("cuts", "blk", "tile"), None),
        P(("cuts", "blk", "tile")),
        P(),
    )
    out_specs = P(("cuts", "blk", "tile"), None, None)
    return jax.shard_map(local, mesh=mesh, in_specs=in_specs, out_specs=out_specs, check_vma=False)
```

time: 47.8 us -> 45.1 us (0.944); the launches traced: 47.7 us -> 44.3 us
  waiting for transfers between devices: 14.5 us -> 11.9 us
  Pallas kernels: 15.4 us -> 13.7 us
  starting transfers between devices: 13.3 us -> 14.1 us
    ppermute x7, waiting for transfers between devices: 11.9 us -> 9.28 us  [local(): piece = lax.ppermute(piece, ('blk', 'tile'), pairs)]
    pallas_call x2, Pallas kernels: 14.2 us -> 12.4 us  [make_subgrids(): pl.pallas_call(functools.partial(subgrid_kernel, first, destinations, cap...]
    ppermute x7, starting transfers between devices: 12.8 us -> 13.6 us  [local(): piece = lax.ppermute(piece, ('blk', 'tile'), pairs)]
  transfers between devices with their start and end apart: 9 -> 9, of which waited for: 5 -> 4; matrix products, arithmetic and copies ran while one was open for 2% -> 2% of each run, Pallas kernels for 18% -> 16%
where the time goes in v6:
time: 45.1 us; the launch traced here: 44.3 us
  starting transfers between devices  14.1 us (31%)
  Pallas kernels  13.7 us (30%)
  waiting for transfers between devices  11.9 us (26%)
  other arithmetic  3.06 us (7%)
  local copies, waits for them, and re-layouts  1.42 us (3%)
    ppermute x7, starting transfers between devices, local(): piece = lax.ppermute(piece, ('blk', 'tile'), pairs)  13.6 us
    pallas_call x2, Pallas kernels, make_subgrids(): pl.pallas_call(functools.partial(subgrid_kernel, first, destinations, cap...  12.4 us
    ppermute x7, waiting for transfers between devices, local(): piece = lax.ppermute(piece, ('blk', 'tile'), pairs)  9.28 us
    ppermute x1, waiting for transfers between devices, local(): whole = part + lax.ppermute(part, 'samp', swap)  2.65 us
    unnamed x10, local copies, waits for them, and re-layouts  1.41 us
    add x1, other arithmetic, local(): own.astype(jnp.float32) + other.astype(jnp.float32)  1.23 us
    pallas_call x1, Pallas kernels, sum_slots(): pl.pallas_call(functools.partial(gather_kernel, capacity), out_shape=jax....  1.23 us
    add x1, other arithmetic, local(): whole = part + lax.ppermute(part, 'samp', swap)  1.08 us
  transfers between devices with their start and end apart: 9, of which 4 were waited for; matrix products, arithmetic and copies ran while one was open for 2% of the time, Pallas kernels for 16%

profile of v6, /device:TPU:0, one launch (start us, length us, event | category | flops | bytes accessed | tf_op | source)
XLA Modules:
  0.0 44.3 jit_solution(15571326612696005567)
XLA Ops:
  0.0 0.5 %collective-permute-start = (bf16[2048,128]{1,0:T(8,128)(2,1)}, bf16[2048,128]{1,0:T(8,128)(2,1)S(1)}, u32[]{:S(2)}, u32[]{:S(2)}) collective-permute-start(bf16[2048,128]{1,0:T(8,128)(2,1)} %bitcast.18), channel_id=1, source_target_pairs={{0,8},{8,0},{1,9},{9,1},{2,10},{10,2},{3,11},{11,3},{4,12},{12,4},... | collective-permute-start | bytes 1572872 | tf_op jit(solution)/shard_map/ppermute | solution.py:307
  0.5 0.0 copy-start.3
  0.5 0.0 copy-start.4
  0.5 0.7 %copy-done.3 = s32[256,1]{0,1:T(1,128)S(1)} copy-done((s32[256,1]{0,1:T(1,128)S(1)}, s32[256,1]{0,1:T(1,128)}, u32[]{:S(2)}) %copy-start.3) | copy-done | bytes 1048
  1.1 0.0 copy-done.4
  1.1 0.1 select_reduce_fusion.3
  1.2 0.2 convert_reduce_fusion
  1.4 0.1 convert_reduce_fusion.1
  1.6 0.1 select_reduce_fusion.4.start_ref
  1.6 0.0 copy-start.1
  1.6 0.0 copy-start.2
  1.7 0.1 select_reduce_fusion.2
  1.7 0.6 %copy-done.1 = s32[256]{0:T(256)S(1)} copy-done((s32[256]{0:T(256)S(1)}, s32[256]{0:T(256)}, u32[]{:S(2)}) %copy-start.1) | copy-done | bytes 1048
  2.3 0.0 copy-done.2
  2.4 0.2 select_reduce_fusion
  2.5 0.0 copy-start
  2.5 0.0 collective-permute-done
  2.5 1.2 %convert_add_fusion.res_ref = f32[2048,128]{1,0:T(8,128)S(1)} fusion(bf16[2048,128]{1,0:T(8,128)(2,1)S(1)} %collective-permute-done, bf16[2048,128]{1,0:T(8,128)(2,1)} %bitcast.19), kind=kLoop, calls=%fused_computation | loop fusion | flops 786432 | bytes 2097152 | tf_op jit(solution)/shard_map/add | solution.py:336
  3.8 0.1 copy-done
  3.9 5.4 %subgrids.2 = (bf16[528,128]{1,0:T(8,128)(2,1)S(1)}, bf16[528,128]{1,0:T(8,128)(2,1)S(1)}, bf16[528,128]{1,0:T(8,128)(2,1)S(1)}, s32[8,128]{1,0:T(8,128)S(1)}) custom-call(s32[160]{0:T(256)S(1)} %get-tuple-element.24.block_ref, s32[160]{0:T(256)S(1)} %get-tuple-element.23.row_ref, s32[9]{0:T(128)S(1)} %select_reduce_fusion.4.start_ref, ...), custom_call_target="tpu_custom_call" | custom-call | flops 402653184 | bytes 786432 | tf_op jit(solution)/shard_map/subgrids/pallas_call | solution.py:210
  9.3 4.6 %collective-permute-start.1 = (bf16[528,128]{1,0:T(8,128)(2,1)S(1)}, bf16[528,128]{1,0:T(8,128)(2,1)S(1)}, u32[]{:S(2)}, u32[]{:S(2)}) collective-permute-start(bf16[528,128]{1,0:T(8,128)(2,1)S(1)} %get-tuple-element.14), channel_id=1, source_target_pairs={{0,7},{1,6},{2,5},{3,4},{4,3},{5,2},{6,1},{7,0},{8,15},{9,14},{10,... | collective-permute-start | bytes 405512 | tf_op jit(solution)/shard_map/ppermute | solution.py:349
  13.9 0.0 collective-permute-start.2
  13.9 2.0 %collective-permute-start.3 = (bf16[528,128]{1,0:T(8,128)(2,1)S(1)}, bf16[528,128]{1,0:T(8,128)(2,1)S(1)}, u32[]{:S(2)}, u32[]{:S(2)}) collective-permute-start(bf16[528,128]{1,0:T(8,128)(2,1)S(1)} %get-tuple-element.16), channel_id=1, source_target_pairs={{0,5},{1,4},{2,7},{3,6},{4,1},{5,0},{6,3},{7,2},{8,13},{9,12},{10,... | collective-permute-start | bytes 405512 | tf_op jit(solution)/shard_map/ppermute | solution.py:349
  15.9 7.0 %subgrids.3 = (bf16[528,128]{1,0:T(8,128)(2,1)S(1)}, bf16[528,128]{1,0:T(8,128)(2,1)S(1)}, bf16[528,128]{1,0:T(8,128)(2,1)S(1)}, bf16[528,128]{1,0:T(8,128)(2,1)...) custom-call(s32[160]{0:T(256)S(1)} %get-tuple-element.24.block_ref, s32[160]{0:T(256)S(1)} %get-tuple-element.23.row_ref, ...), custom_call_target="tpu_custom_call" | custom-call | flops 671088640 | bytes 1310720 | tf_op jit(solution)/shard_map/subgrids/pallas_call | solution.py:210
  22.9 1.2 %collective-permute-start.4 = (bf16[528,128]{1,0:T(8,128)(2,1)S(1)}, bf16[528,128]{1,0:T(8,128)(2,1)S(1)}, u32[]{:S(2)}, u32[]{:S(2)}) collective-permute-start(bf16[528,128]{1,0:T(8,128)(2,1)S(1)} %get-tuple-element.18), channel_id=1, source_target_pairs={{0,4},{1,5},{2,6},{3,7},{4,0},{5,1},{6,2},{7,3},{8,12},{9,13},{10,... | collective-permute-start | bytes 405512 | tf_op jit(solution)/shard_map/ppermute | solution.py:349
  24.1 2.7 %collective-permute-start.5 = (bf16[528,128]{1,0:T(8,128)(2,1)S(1)}, bf16[528,128]{1,0:T(8,128)(2,1)S(1)}, u32[]{:S(2)}, u32[]{:S(2)}) collective-permute-start(bf16[528,128]{1,0:T(8,128)(2,1)S(1)} %get-tuple-element.19), channel_id=1, source_target_pairs={{0,3},{1,2},{2,1},{3,0},{4,7},{5,6},{6,5},{7,4},{8,11},{9,10},{10,... | collective-permute-start | bytes 405512 | tf_op jit(solution)/shard_map/ppermute | solution.py:349
  26.9 0.0 collective-permute-done.1.refs_0_
  26.9 3.1 %collective-permute-start.6 = (bf16[528,128]{1,0:T(8,128)(2,1)S(1)}, bf16[528,128]{1,0:T(8,128)(2,1)S(1)}, u32[]{:S(2)}, u32[]{:S(2)}) collective-permute-start(bf16[528,128]{1,0:T(8,128)(2,1)S(1)} %get-tuple-element.20), channel_id=1, source_target_pairs={{0,2},{1,3},{2,0},{3,1},{4,6},{5,7},{6,4},{7,5},{8,10},{9,11},{10,... | collective-permute-start | bytes 405512 | tf_op jit(solution)/shard_map/ppermute | solution.py:349
  29.9 0.0 collective-permute-done.2.refs_1_
  29.9 0.0 collective-permute-start.7
  29.9 5.7 %collective-permute-done.3.refs_2_ = bf16[528,128]{1,0:T(8,128)(2,1)S(1)} collective-permute-done((bf16[528,128]{1,0:T(8,128)(2,1)S(1)}, bf16[528,128]{1,0:T(8,128)(2,1)S(1)}, u32[]{:S(2)}, u32[]{:S(2)}) %collective-permute-start.3) | collective-permute-done | bytes 135200 | tf_op jit(solution)/shard_map/ppermute | solution.py:349
  35.7 2.3 %collective-permute-done.4.refs_3_ = bf16[528,128]{1,0:T(8,128)(2,1)S(1)} collective-permute-done((bf16[528,128]{1,0:T(8,128)(2,1)S(1)}, bf16[528,128]{1,0:T(8,128)(2,1)S(1)}, u32[]{:S(2)}, u32[]{:S(2)}) %collective-permute-start.4) | collective-permute-done | bytes 135200 | tf_op jit(solution)/shard_map/ppermute | solution.py:349
  37.9 0.0 collective-permute-done.5.refs_4_
  37.9 1.3 %collective-permute-done.6.refs_5_ = bf16[528,128]{1,0:T(8,128)(2,1)S(1)} collective-permute-done((bf16[528,128]{1,0:T(8,128)(2,1)S(1)}, bf16[528,128]{1,0:T(8,128)(2,1)S(1)}, u32[]{:S(2)}, u32[]{:S(2)}) %collective-permute-start.6) | collective-permute-done | bytes 135200 | tf_op jit(solution)/shard_map/ppermute | solution.py:349
  39.2 0.0 collective-permute-done.7.refs_6_
  39.2 1.2 %sum_slots.1 = f32[2048,128]{1,0:T(8,128)S(1)} custom-call(bf16[528,128]{1,0:T(8,128)(2,1)S(1)} %collective-permute-done.1.refs_0_, bf16[528,128]{1,0:T(8,128)(2,1)S(1)} %collective-permute-done.2.refs_1_, bf16[528,128]{1,0:T(8,128)(2,1)S(1)} %collective-permute-done.3.refs_2_, bf16[528,128]{1,0:T(8,128)(2,1)S(1)} %collective-permute-done.4.refs_3_, ...), custom_call_target="tpu_custom_call" | custom-call | tf_op jit(solution)/shard_map/sum_slots/pallas_call | solution.py:272
  40.5 0.1 collective-permute-start.8
  40.5 2.6 %collective-permute-done.8 = f32[2048,128]{1,0:T(8,128)S(1)} collective-permute-done((f32[2048,128]{1,0:T(8,128)S(1)}, f32[2048,128]{1,0:T(8,128)S(1)}, u32[]{:S(2)}, u32[]{:S(2)}) %collective-permute-start.8) | collective-permute-done | bytes 1048608 | tf_op jit(solution)/shard_map/ppermute | solution.py:358
  43.2 1.1 %add.54 = f32[2048,128]{1,0:T(8,128)} add(f32[2048,128]{1,0:T(8,128)S(1)} %sum_slots.1, f32[2048,128]{1,0:T(8,128)S(1)} %collective-permute-done.8) | non-fusion elementwise | flops 262144 | bytes 3145728 | tf_op jit(solution)/shard_map/add | solution.py:358
  (5 shorter events, 0.0 us)
Async XLA Ops:
  0.0 2.5 %collective-permute-start = (bf16[2048,128]{1,0:T(8,128)(2,1)}, bf16[2048,128]{1,0:T(8,128)(2,1)S(1)}, u32[]{:S(2)}, u32[]{:S(2)}) collective-permute-start(bf16[2048,128]{1,0:T(8,128)(2,1)} %bitcast.18), channel_id=1, source_target_pairs={{0,8},{8,0},{1,9},{9,1},{2,10},{10,2},{3,11},{11,3},{4,12},{12,4},... | collective-permute-start | bytes 1572872 | tf_op jit(solution)/shard_map/ppermute | solution.py:307
  0.5 0.7 %copy-start.3 = (s32[256,1]{0,1:T(1,128)S(1)}, s32[256,1]{0,1:T(1,128)}, u32[]{:S(2)}) copy-start(s32[256,1]{0,1:T(1,128)} %param.9) | copy-start | bytes 3076
  0.5 0.7 %copy-start.4 = (s32[8]{0:T(128)S(1)}, s32[8]{0:T(128)}, u32[]{:S(2)}) copy-start(s32[8]{0:T(128)} %param.11) | copy-start | bytes 100
  1.6 0.7 %copy-start.1 = (s32[256]{0:T(256)S(1)}, s32[256]{0:T(256)}, u32[]{:S(2)}) copy-start(s32[256]{0:T(256)} %param.10) | copy-start | bytes 3076
  1.6 0.7 %copy-start.2 = (s32[256]{0:T(256)S(1)}, s32[256]{0:T(256)}, u32[]{:S(2)}) copy-start(s32[256]{0:T(256)} %param.8) | copy-start | bytes 3076
  2.5 1.4 %copy-start = (f32[256,2,512]{2,1,0:T(2,128)S(1)}, f32[256,2,512]{2,1,0:T(2,128)}, u32[]{:S(2)}) copy-start(f32[256,2,512]{2,1,0:T(2,128)} %param.7) | copy-start | bytes 3145732
  9.3 17.6 %collective-permute-start.1 = (bf16[528,128]{1,0:T(8,128)(2,1)S(1)}, bf16[528,128]{1,0:T(8,128)(2,1)S(1)}, u32[]{:S(2)}, u32[]{:S(2)}) collective-permute-start(bf16[528,128]{1,0:T(8,128)(2,1)S(1)} %get-tuple-element.14), channel_id=1, source_target_pairs={{0,7},{1,6},{2,5},{3,4},{4,3},{5,2},{6,1},{7,0},{8,15},{9,14},{10,... | collective-permute-start | bytes 405512 | tf_op jit(solution)/shard_map/ppermute | solution.py:349
  13.9 16.1 %collective-permute-start.2 = (bf16[528,128]{1,0:T(8,128)(2,1)S(1)}, bf16[528,128]{1,0:T(8,128)(2,1)S(1)}, u32[]{:S(2)}, u32[]{:S(2)}) collective-permute-start(bf16[528,128]{1,0:T(8,128)(2,1)S(1)} %get-tuple-element.15), channel_id=1, source_target_pairs={{0,6},{1,7},{2,4},{3,5},{4,2},{5,3},{6,0},{7,1},{8,14},{9,15},{10,... | collective-permute-start | bytes 405512 | tf_op jit(solution)/shard_map/ppermute | solution.py:349
  13.9 21.8 %collective-permute-start.3 = (bf16[528,128]{1,0:T(8,128)(2,1)S(1)}, bf16[528,128]{1,0:T(8,128)(2,1)S(1)}, u32[]{:S(2)}, u32[]{:S(2)}) collective-permute-start(bf16[528,128]{1,0:T(8,128)(2,1)S(1)} %get-tuple-element.16), channel_id=1, source_target_pairs={{0,5},{1,4},{2,7},{3,6},{4,1},{5,0},{6,3},{7,2},{8,13},{9,12},{10,... | collective-permute-start | bytes 405512 | tf_op jit(solution)/shard_map/ppermute | solution.py:349
  22.9 15.0 %collective-permute-start.4 = (bf16[528,128]{1,0:T(8,128)(2,1)S(1)}, bf16[528,128]{1,0:T(8,128)(2,1)S(1)}, u32[]{:S(2)}, u32[]{:S(2)}) collective-permute-start(bf16[528,128]{1,0:T(8,128)(2,1)S(1)} %get-tuple-element.18), channel_id=1, source_target_pairs={{0,4},{1,5},{2,6},{3,7},{4,0},{5,1},{6,2},{7,3},{8,12},{9,13},{10,... | collective-permute-start | bytes 405512 | tf_op jit(solution)/shard_map/ppermute | solution.py:349
  24.1 13.8 %collective-permute-start.5 = (bf16[528,128]{1,0:T(8,128)(2,1)S(1)}, bf16[528,128]{1,0:T(8,128)(2,1)S(1)}, u32[]{:S(2)}, u32[]{:S(2)}) collective-permute-start(bf16[528,128]{1,0:T(8,128)(2,1)S(1)} %get-tuple-element.19), channel_id=1, source_target_pairs={{0,3},{1,2},{2,1},{3,0},{4,7},{5,6},{6,5},{7,4},{8,11},{9,10},{10,... | collective-permute-start | bytes 405512 | tf_op jit(solution)/shard_map/ppermute | solution.py:349
  26.9 12.4 %collective-permute-start.6 = (bf16[528,128]{1,0:T(8,128)(2,1)S(1)}, bf16[528,128]{1,0:T(8,128)(2,1)S(1)}, u32[]{:S(2)}, u32[]{:S(2)}) collective-permute-start(bf16[528,128]{1,0:T(8,128)(2,1)S(1)} %get-tuple-element.20), channel_id=1, source_target_pairs={{0,2},{1,3},{2,0},{3,1},{4,6},{5,7},{6,4},{7,5},{8,10},{9,11},{10,... | collective-permute-start | bytes 405512 | tf_op jit(solution)/shard_map/ppermute | solution.py:349
  29.9 9.3 %collective-permute-start.7 = (bf16[528,128]{1,0:T(8,128)(2,1)S(1)}, bf16[528,128]{1,0:T(8,128)(2,1)S(1)}, u32[]{:S(2)}, u32[]{:S(2)}) collective-permute-start(bf16[528,128]{1,0:T(8,128)(2,1)S(1)} %get-tuple-element.21), channel_id=1, source_target_pairs={{0,1},{1,0},{2,3},{3,2},{4,5},{5,4},{6,7},{7,6},{8,9},{9,8},{10,11... | collective-permute-start | bytes 405512 | tf_op jit(solution)/shard_map/ppermute | solution.py:349
  40.5 2.7 %collective-permute-start.8 = (f32[2048,128]{1,0:T(8,128)S(1)}, f32[2048,128]{1,0:T(8,128)S(1)}, u32[]{:S(2)}, u32[]{:S(2)}) collective-permute-start(f32[2048,128]{1,0:T(8,128)S(1)} %sum_slots.1), channel_id=1, source_target_pairs={{0,8},{8,0},{1,9},{9,1},{2,10},{10,2},{3,11},{11,3},{4,12},{12,4},... | collective-permute-start | bytes 3145736 | tf_op jit(solution)/shard_map/ppermute | solution.py:358

commit v7 on v6

--- a/solution.py
+++ b/solution.py
@@ -21,6 +21,7 @@
 TAG_ROWS = 16
 COUNT_SPAN = 4096
 PAIRED_MAX = 16
+CALLS = (0, 1, 4, 8)
 VMEM_LIMIT = 48 * 1024 * 1024
 
 
@@ -71,11 +72,9 @@
 
 
 def subgrid_kernel(
-    first, destinations, capacity, block_ref, row_ref, start_ref, token_ref, uv_any, res_ref, *refs
+    first, destinations, capacity, block_ref, row_ref, start_ref, token_ref, uv_ref, res_ref, *refs
 ):
-    out_refs, (next_ref, uv_ref, uv_sem, gathered, found, tags, mover) = refs[:-7], refs[-7:]
-    fetch = pltpu.make_async_copy(uv_any, uv_ref, uv_sem)
-    fetch.start()
+    out_refs, (next_ref, gathered, found, tags, mover) = refs[:-5], refs[-5:]
     next_ref[...] = jnp.zeros_like(next_ref)
     tiles = gathered.shape[0] // (4 * GROUP)
     spare = destinations * capacity // QUAD
@@ -96,11 +95,34 @@
     moves = (source // LANES == lane // SUB) & (source % LANES // QUAD == lane % SUB)
     mover[...] = jnp.where(moves, 1.0, 0.0).astype(jnp.bfloat16)
     tags[...] = jnp.zeros_like(tags)
-    fetch.wait()
-
-    @pl.loop(0, (high - low + 1) // 2)
-    def _(g):
+
+    def finish(operands, quad_at):
+        product = lax.dot_general(
+            *operands, (((1,), (1,)), ((), ())), preferred_element_type=jnp.float32
+        )
+        half = product.shape[0] // 2
+        wholes = (
+            product[:half, :LANES] - product[half:, LANES:],
+            product[half:, :LANES] + product[:half, LANES:],
+        )
+        rows = []
+        for whole in wholes:
+            whole = jnp.where(same_block, whole, 0.0)
+            for j in range(0, STEPS, 4):
+                four = [whole[(j + k) * GROUP : (j + k + 1) * GROUP] for k in range(4)]
+                rows.append(jnp.concatenate(four, 1))
+        index = jnp.clip(quad_at * QUAD, 0, last + 1 - QUAD)
+        place = row_ref[index] // (2 * SLOTS * QUAD) - first * (capacity // QUAD)
+        place = jnp.where((quad_at >= low) & (quad_at < high), place, spare)
+        found[place] = jnp.concatenate(rows, 0).astype(jnp.bfloat16)
+        tag = jnp.zeros((QUAD, LANES), jnp.int32)
+        for b in range(QUAD):
+            tag = jnp.where(quad_row == b, row_ref[index + b] % (2 * SLOTS), tag)
+        tags[place] = tag.astype(jnp.float32)
+
+    def turn(g, carried):
         quad_at = low + 2 * g
+        finish(carried, quad_at - 1)
         for i in range(GROUP):
             packed = block_ref[jnp.minimum(quad_at * QUAD + i, last)]
             block, count = packed // COUNT_SPAN, packed % COUNT_SPAN
@@ -133,38 +155,19 @@
         right_low = [by_quad(c2, c), by_quad(-s2, -s)]
         factor = 2.0 * c2
         right_factor = by_quad(factor, factor)
+        rows = []
         for quad in range(2):
             left, right = [], []
             for part in range(2):
                 left += sequence(left_low[part][quad], left_mid[part][quad], left_factor[quad])
                 right += sequence(right_low[part][quad], right_mid[part][quad], right_factor[quad])
-            product = lax.dot_general(
-                jnp.concatenate(left, 0).astype(jnp.bfloat16),
-                jnp.concatenate(right, 0).astype(jnp.bfloat16),
-                (((1,), (1,)), ((), ())),
-                preferred_element_type=jnp.float32,
-            )
-            half = product.shape[0] // 2
-            wholes = (
-                product[:half, :LANES] - product[half:, LANES:],
-                product[half:, :LANES] + product[:half, LANES:],
-            )
-            rows = []
-            for whole in wholes:
-                whole = jnp.where(same_block, whole, 0.0)
-                for j in range(0, STEPS, 4):
-                    four = [whole[(j + k) * GROUP : (j + k + 1) * GROUP] for k in range(4)]
-                    rows.append(jnp.concatenate(four, 1))
-            index = (quad_at + quad) * QUAD
-            known = quad_at + quad < high
-            index = jnp.minimum(index, last + 1 - QUAD)
-            place = row_ref[index] // (2 * SLOTS * QUAD) - first * (capacity // QUAD)
-            place = jnp.where(known, place, spare)
-            found[place] = jnp.concatenate(rows, 0).astype(jnp.bfloat16)
-            tag = jnp.zeros((QUAD, LANES), jnp.int32)
-            for b in range(QUAD):
-                tag = jnp.where(quad_row == b, row_ref[index + b] % (2 * SLOTS), tag)
-            tags[place] = tag.astype(jnp.float32)
+            rows.append([jnp.concatenate(x, 0).astype(jnp.bfloat16) for x in (left, right)])
+        finish(rows[0], quad_at)
+        return rows[1]
+
+    turns = (high - low + 1) // 2
+    nothing = jnp.zeros((4 * STEPS * QUAD, tiles * LANES), jnp.bfloat16)
+    finish(lax.fori_loop(0, turns, turn, [nothing, nothing]), low + 2 * turns - 1)
 
     shares = capacity // TAG_ROWS
     share = lax.broadcasted_iota(jnp.int32, (TAG_ROWS, LANES), 1) // (LANES // shares)
@@ -213,11 +216,9 @@
             jax.ShapeDtypeStruct((n * message_rows(capacity), LANES), jnp.bfloat16) for n in outs
         ]
         + [jax.ShapeDtypeStruct(token.shape, token.dtype)],
-        in_specs=[smem] * 3 + [vmem, pl.BlockSpec(memory_space=pl.ANY), vmem],
+        in_specs=[smem] * 3 + [vmem] * 3,
         out_specs=[vmem] * (len(outs) + 1),
         scratch_shapes=[
-            pltpu.VMEM(uv.shape, uv.dtype),
-            pltpu.SemaphoreType.DMA,
             pltpu.VMEM((4 * tiles * GROUP, LANES), jnp.float32),
             pltpu.VMEM((quads + 1, FEATURE // SUB, 4 * LANES), jnp.bfloat16),
             pltpu.VMEM((quads + 1, QUAD, LANES), jnp.float32),
@@ -337,9 +338,12 @@
     )
     token = jnp.zeros((GROUP, LANES), jnp.int32)
     if paired:
-        far = owners * 3 // 8
-        *rows, token = subgrids(0, (1,) * far, token)
-        rows += subgrids(far, (1,) * (owners - far), token)[:-1]
+        rows = []
+        for first, last in zip(CALLS[:-1], CALLS[1:]):
+            first, last = owners * first // CALLS[-1], owners * last // CALLS[-1]
+            if first < last:
+                *more, token = subgrids(first, (1,) * (last - first), token)
+                rows += more
         arrived = []
         for turn in range(owners):
             distance = owners - 1 - turn

time: 45.1 us -> 47.6 us (1.055); the launches traced: 44.3 us -> 47.5 us
  Pallas kernels: 13.7 us -> 16 us
  starting transfers between devices: 14.1 us -> 15.8 us
  waiting for transfers between devices: 11.9 us -> 11.2 us
    pallas_call x2 -> x3, Pallas kernels: 12.4 us -> 14.7 us  [make_subgrids(): pl.pallas_call(functools.partial(subgrid_kernel, first, destinations, cap...]
    ppermute x7, starting transfers between devices: 13.6 us -> 15.2 us  [local(): piece = lax.ppermute(piece, ('blk', 'tile'), pairs)]
    ppermute x7, waiting for transfers between devices: 9.28 us -> 8.55 us  [local(): piece = lax.ppermute(piece, ('blk', 'tile'), pairs)]
  transfers between devices with their start and end apart: 9 -> 9, of which waited for: 4 -> 5; matrix products, arithmetic and copies ran while one was open for 2% -> 2% of each run, Pallas kernels for 16% -> 26%
where the time goes in v7:
time: 47.6 us; the launch traced here: 47.5 us
  Pallas kernels  16 us (34%)
  starting transfers between devices  15.8 us (33%)
  waiting for transfers between devices  11.2 us (24%)
  other arithmetic  3.06 us (6%)
  local copies, waits for them, and re-layouts  1.42 us (3%)
    ppermute x7, starting transfers between devices, local(): piece = lax.ppermute(piece, ('blk', 'tile'), pairs)  15.2 us
    pallas_call x3, Pallas kernels, make_subgrids(): pl.pallas_call(functools.partial(subgrid_kernel, first, destinations, cap...  14.7 us
    ppermute x7, waiting for transfers between devices, local(): piece = lax.ppermute(piece, ('blk', 'tile'), pairs)  8.55 us
    ppermute x1, waiting for transfers between devices, local(): whole = part + lax.ppermute(part, 'samp', swap)  2.64 us
    unnamed x10, local copies, waits for them, and re-layouts  1.41 us
    add x1, other arithmetic, local(): own.astype(jnp.float32) + other.astype(jnp.float32)  1.23 us
    pallas_call x1, Pallas kernels, sum_slots(): pl.pallas_call(functools.partial(gather_kernel, capacity), out_shape=jax....  1.21 us
    add x1, other arithmetic, local(): whole = part + lax.ppermute(part, 'samp', swap)  1.08 us
  transfers between devices with their start and end apart: 9, of which 5 were waited for; matrix products, arithmetic and copies ran while one was open for 2% of the time, Pallas kernels for 26%

profile of v7, /device:TPU:0, one launch (start us, length us, event | category | flops | bytes accessed | tf_op | source)
XLA Modules:
  0.0 47.5 jit_solution(1063828599984557327)
XLA Ops:
  0.0 0.5 collective-permute-start
  0.5 0.0 copy-start.3
  0.5 0.0 copy-start.4
  0.5 0.7 %copy-done.3 = s32[256,1]{0,1:T(1,128)S(1)} copy-done((s32[256,1]{0,1:T(1,128)S(1)}, s32[256,1]{0,1:T(1,128)}, u32[]{:S(2)}) %copy-start.3) | copy-done | bytes 1048
  1.1 0.0 copy-done.4
  1.1 0.1 select_reduce_fusion.3
  1.2 0.2 convert_reduce_fusion
  1.4 0.1 convert_reduce_fusion.1
  1.6 0.1 select_reduce_fusion.4.start_ref
  1.6 0.0 copy-start.1
  1.6 0.0 copy-start.2
  1.7 0.1 select_reduce_fusion.2
  1.7 0.6 %copy-done.1 = s32[256]{0:T(256)S(1)} copy-done((s32[256]{0:T(256)S(1)}, s32[256]{0:T(256)}, u32[]{:S(2)}) %copy-start.1) | copy-done | bytes 1048
  2.3 0.0 copy-done.2
  2.4 0.2 select_reduce_fusion
  2.5 0.0 copy-start
  2.5 0.0 collective-permute-done
  2.5 1.2 %convert_add_fusion.res_ref = f32[2048,128]{1,0:T(8,128)S(1)} fusion(bf16[2048,128]{1,0:T(8,128)(2,1)S(1)} %collective-permute-done, bf16[2048,128]{1,0:T(8,128)(2,1)} %bitcast.20), kind=kLoop, calls=%fused_computation | loop fusion | flops 786432 | bytes 2097152 | tf_op jit(solution)/shard_map/add | solution.py:337
  3.8 0.1 copy-done
  3.9 2.5 %subgrids.3 = (bf16[528,128]{1,0:T(8,128)(2,1)S(1)}, s32[8,128]{1,0:T(8,128)S(1)}) custom-call(s32[160]{0:T(256)S(1)} %get-tuple-element.26.block_ref, s32[160]{0:T(256)S(1)} %get-tuple-element.25.row_ref, s32[9]{0:T(128)S(1)} %select_reduce_fusion.4.start_ref, s32[8,128]{1,0:T(8,128)S(1)} %broadcast_in_dim.80.token_ref, f32[2048,128]{1,0:T(8,128)S(1)} %bitcast.16, ...), custom_call_target="tpu_custom_call" | custom-call | flops 134217728 | bytes 262144 | tf_op jit(solution)/shard_map/subgrids/pallas_call | solution.py:213
  6.4 5.1 %collective-permute-start.1 = (bf16[528,128]{1,0:T(8,128)(2,1)S(1)}, bf16[528,128]{1,0:T(8,128)(2,1)S(1)}, u32[]{:S(2)}, u32[]{:S(2)}) collective-permute-start(bf16[528,128]{1,0:T(8,128)(2,1)S(1)} %get-tuple-element.15), channel_id=1, source_target_pairs={{0,7},{1,6},{2,5},{3,4},{4,3},{5,2},{6,1},{7,0},{8,15},{9,14},{10,... | collective-permute-start | bytes 405512 | tf_op jit(solution)/shard_map/ppermute | solution.py:353
  11.4 3.8 %subgrids.4 = (bf16[528,128]{1,0:T(8,128)(2,1)S(1)}, bf16[528,128]{1,0:T(8,128)(2,1)S(1)}, bf16[528,128]{1,0:T(8,128)(2,1)S(1)}, s32[8,128]{1,0:T(8,128)S(1)}) custom-call(s32[160]{0:T(256)S(1)} %get-tuple-element.26.block_ref, s32[160]{0:T(256)S(1)} %get-tuple-element.25.row_ref, s32[9]{0:T(128)S(1)} %select_reduce_fusion.4.start_ref, ...), custom_call_target="tpu_custom_call" | custom-call | flops 402653184 | bytes 786432 | tf_op jit(solution)/shard_map/subgrids/pallas_call | solution.py:213
  15.2 2.9 %collective-permute-start.2 = (bf16[528,128]{1,0:T(8,128)(2,1)S(1)}, bf16[528,128]{1,0:T(8,128)(2,1)S(1)}, u32[]{:S(2)}, u32[]{:S(2)}) collective-permute-start(bf16[528,128]{1,0:T(8,128)(2,1)S(1)} %get-tuple-element.17), channel_id=1, source_target_pairs={{0,6},{1,7},{2,4},{3,5},{4,2},{5,3},{6,0},{7,1},{8,14},{9,15},{10,... | collective-permute-start | bytes 405512 | tf_op jit(solution)/shard_map/ppermute | solution.py:353
  18.2 0.0 collective-permute-start.3
  18.2 3.8 %collective-permute-start.4 = (bf16[528,128]{1,0:T(8,128)(2,1)S(1)}, bf16[528,128]{1,0:T(8,128)(2,1)S(1)}, u32[]{:S(2)}, u32[]{:S(2)}) collective-permute-start(bf16[528,128]{1,0:T(8,128)(2,1)S(1)} %get-tuple-element.19), channel_id=1, source_target_pairs={{0,4},{1,5},{2,6},{3,7},{4,0},{5,1},{6,2},{7,3},{8,12},{9,13},{10,... | collective-permute-start | bytes 405512 | tf_op jit(solution)/shard_map/ppermute | solution.py:353
  21.9 8.5 %subgrids.5 = (bf16[528,128]{1,0:T(8,128)(2,1)S(1)}, bf16[528,128]{1,0:T(8,128)(2,1)S(1)}, bf16[528,128]{1,0:T(8,128)(2,1)S(1)}, bf16[528,128]{1,0:T(8,128)(2,1)S(1)}, s32[8,128]{1,0:T(8,128)}) custom-call(s32[160]{0:T(256)S(1)} %get-tuple-element.26.block_ref, s32[160]{0:T(256)S(1)} %get-tuple-element.25.row_ref, s32[9]{0:T(128)S(1)} %select_reduce_fusion.4.start_ref, ...), custom_call_target="tpu_custom_call" | custom-call | flops 536870912 | bytes 1048576 | tf_op jit(solution)/shard_map/subgrids/pallas_call | solution.py:213
  30.4 0.4 collective-permute-start.5
  30.8 0.0 collective-permute-done.1.refs_0_
  30.8 1.2 %collective-permute-start.6 = (bf16[528,128]{1,0:T(8,128)(2,1)S(1)}, bf16[528,128]{1,0:T(8,128)(2,1)S(1)}, u32[]{:S(2)}, u32[]{:S(2)}) collective-permute-start(bf16[528,128]{1,0:T(8,128)(2,1)S(1)} %get-tuple-element.22), channel_id=1, source_target_pairs={{0,2},{1,3},{2,0},{3,1},{4,6},{5,7},{6,4},{7,5},{8,10},{9,11},{10,... | collective-permute-start | bytes 405512 | tf_op jit(solution)/shard_map/ppermute | solution.py:353
  32.0 0.0 collective-permute-done.2.refs_1_
  32.0 1.9 %collective-permute-start.7 = (bf16[528,128]{1,0:T(8,128)(2,1)S(1)}, bf16[528,128]{1,0:T(8,128)(2,1)S(1)}, u32[]{:S(2)}, u32[]{:S(2)}) collective-permute-start(bf16[528,128]{1,0:T(8,128)(2,1)S(1)} %get-tuple-element.23), channel_id=1, source_target_pairs={{0,1},{1,0},{2,3},{3,2},{4,5},{5,4},{6,7},{7,6},{8,9},{9,8},{10,11... | collective-permute-start | bytes 405512 | tf_op jit(solution)/shard_map/ppermute | solution.py:353
  33.9 0.1 collective-permute-done.3.refs_2_
  34.0 2.7 %collective-permute-done.4.refs_3_ = bf16[528,128]{1,0:T(8,128)(2,1)S(1)} collective-permute-done((bf16[528,128]{1,0:T(8,128)(2,1)S(1)}, bf16[528,128]{1,0:T(8,128)(2,1)S(1)}, u32[]{:S(2)}, u32[]{:S(2)}) %collective-permute-start.4) | collective-permute-done | bytes 135200 | tf_op jit(solution)/shard_map/ppermute | solution.py:353
  36.7 3.1 %collective-permute-done.5.refs_4_ = bf16[528,128]{1,0:T(8,128)(2,1)S(1)} collective-permute-done((bf16[528,128]{1,0:T(8,128)(2,1)S(1)}, bf16[528,128]{1,0:T(8,128)(2,1)S(1)}, u32[]{:S(2)}, u32[]{:S(2)}) %collective-permute-start.5) | collective-permute-done | bytes 135200 | tf_op jit(solution)/shard_map/ppermute | solution.py:353
  39.8 2.7 %collective-permute-done.6.refs_5_ = bf16[528,128]{1,0:T(8,128)(2,1)S(1)} collective-permute-done((bf16[528,128]{1,0:T(8,128)(2,1)S(1)}, bf16[528,128]{1,0:T(8,128)(2,1)S(1)}, u32[]{:S(2)}, u32[]{:S(2)}) %collective-permute-start.6) | collective-permute-done | bytes 135200 | tf_op jit(solution)/shard_map/ppermute | solution.py:353
  42.4 0.0 collective-permute-done.7.refs_6_
  42.5 1.2 %sum_slots.1 = f32[2048,128]{1,0:T(8,128)S(1)} custom-call(bf16[528,128]{1,0:T(8,128)(2,1)S(1)} %collective-permute-done.1.refs_0_, bf16[528,128]{1,0:T(8,128)(2,1)S(1)} %collective-permute-done.2.refs_1_, bf16[528,128]{1,0:T(8,128)(2,1)S(1)} %collective-permute-done.3.refs_2_, bf16[528,128]{1,0:T(8,128)(2,1)S(1)} %collective-permute-done.4.refs_3_, ...), custom_call_target="tpu_custom_call" | custom-call | tf_op jit(solution)/shard_map/sum_slots/pallas_call | solution.py:273
  43.7 0.1 collective-permute-start.8
  43.8 2.6 %collective-permute-done.8 = f32[2048,128]{1,0:T(8,128)S(1)} collective-permute-done((f32[2048,128]{1,0:T(8,128)S(1)}, f32[2048,128]{1,0:T(8,128)S(1)}, u32[]{:S(2)}, u32[]{:S(2)}) %collective-permute-start.8) | collective-permute-done | bytes 1048608 | tf_op jit(solution)/shard_map/ppermute | solution.py:362
  46.4 1.1 %add.54 = f32[2048,128]{1,0:T(8,128)} add(f32[2048,128]{1,0:T(8,128)S(1)} %sum_slots.1, f32[2048,128]{1,0:T(8,128)S(1)} %collective-permute-done.8) | non-fusion elementwise | flops 262144 | bytes 3145728 | tf_op jit(solution)/shard_map/add | solution.py:362
  (5 shorter events, 0.0 us)
Async XLA Ops:
  0.0 2.5 %collective-permute-start = (bf16[2048,128]{1,0:T(8,128)(2,1)}, bf16[2048,128]{1,0:T(8,128)(2,1)S(1)}, u32[]{:S(2)}, u32[]{:S(2)}) collective-permute-start(bf16[2048,128]{1,0:T(8,128)(2,1)} %bitcast.19), channel_id=1, source_target_pairs={{0,8},{8,0},{1,9},{9,1},{2,10},{10,2},{3,11},{11,3},{4,12},{12,4},... | collective-permute-start | bytes 1572872 | tf_op jit(solution)/shard_map/ppermute | solution.py:308
  0.5 0.7 %copy-start.3 = (s32[256,1]{0,1:T(1,128)S(1)}, s32[256,1]{0,1:T(1,128)}, u32[]{:S(2)}) copy-start(s32[256,1]{0,1:T(1,128)} %param.9) | copy-start | bytes 3076
  0.5 0.7 %copy-start.4 = (s32[8]{0:T(128)S(1)}, s32[8]{0:T(128)}, u32[]{:S(2)}) copy-start(s32[8]{0:T(128)} %param.11) | copy-start | bytes 100
  1.6 0.7 %copy-start.1 = (s32[256]{0:T(256)S(1)}, s32[256]{0:T(256)}, u32[]{:S(2)}) copy-start(s32[256]{0:T(256)} %param.10) | copy-start | bytes 3076
  1.6 0.7 %copy-start.2 = (s32[256]{0:T(256)S(1)}, s32[256]{0:T(256)}, u32[]{:S(2)}) copy-start(s32[256]{0:T(256)} %param.8) | copy-start | bytes 3076
  2.5 1.4 %copy-start = (f32[256,2,512]{2,1,0:T(2,128)S(1)}, f32[256,2,512]{2,1,0:T(2,128)}, u32[]{:S(2)}) copy-start(f32[256,2,512]{2,1,0:T(2,128)} %param.7) | copy-start | bytes 3145732
  6.4 24.4 %collective-permute-start.1 = (bf16[528,128]{1,0:T(8,128)(2,1)S(1)}, bf16[528,128]{1,0:T(8,128)(2,1)S(1)}, u32[]{:S(2)}, u32[]{:S(2)}) collective-permute-start(bf16[528,128]{1,0:T(8,128)(2,1)S(1)} %get-tuple-element.15), channel_id=1, source_target_pairs={{0,7},{1,6},{2,5},{3,4},{4,3},{5,2},{6,1},{7,0},{8,15},{9,14},{10,... | collective-permute-start | bytes 405512 | tf_op jit(solution)/shard_map/ppermute | solution.py:353
  15.2 16.7 %collective-permute-start.2 = (bf16[528,128]{1,0:T(8,128)(2,1)S(1)}, bf16[528,128]{1,0:T(8,128)(2,1)S(1)}, u32[]{:S(2)}, u32[]{:S(2)}) collective-permute-start(bf16[528,128]{1,0:T(8,128)(2,1)S(1)} %get-tuple-element.17), channel_id=1, source_target_pairs={{0,6},{1,7},{2,4},{3,5},{4,2},{5,3},{6,0},{7,1},{8,14},{9,15},{10,... | collective-permute-start | bytes 405512 | tf_op jit(solution)/shard_map/ppermute | solution.py:353
  18.2 15.9 %collective-permute-start.3 = (bf16[528,128]{1,0:T(8,128)(2,1)S(1)}, bf16[528,128]{1,0:T(8,128)(2,1)S(1)}, u32[]{:S(2)}, u32[]{:S(2)}) collective-permute-start(bf16[528,128]{1,0:T(8,128)(2,1)S(1)} %get-tuple-element.18), channel_id=1, source_target_pairs={{0,5},{1,4},{2,7},{3,6},{4,1},{5,0},{6,3},{7,2},{8,13},{9,12},{10,... | collective-permute-start | bytes 405512 | tf_op jit(solution)/shard_map/ppermute | solution.py:353
  18.2 18.5 %collective-permute-start.4 = (bf16[528,128]{1,0:T(8,128)(2,1)S(1)}, bf16[528,128]{1,0:T(8,128)(2,1)S(1)}, u32[]{:S(2)}, u32[]{:S(2)}) collective-permute-start(bf16[528,128]{1,0:T(8,128)(2,1)S(1)} %get-tuple-element.19), channel_id=1, source_target_pairs={{0,4},{1,5},{2,6},{3,7},{4,0},{5,1},{6,2},{7,3},{8,12},{9,13},{10,... | collective-permute-start | bytes 405512 | tf_op jit(solution)/shard_map/ppermute | solution.py:353
  30.4 9.4 %collective-permute-start.5 = (bf16[528,128]{1,0:T(8,128)(2,1)S(1)}, bf16[528,128]{1,0:T(8,128)(2,1)S(1)}, u32[]{:S(2)}, u32[]{:S(2)}) collective-permute-start(bf16[528,128]{1,0:T(8,128)(2,1)S(1)} %get-tuple-element.21), channel_id=1, source_target_pairs={{0,3},{1,2},{2,1},{3,0},{4,7},{5,6},{6,5},{7,4},{8,11},{9,10},{10,... | collective-permute-start | bytes 405512 | tf_op jit(solution)/shard_map/ppermute | solution.py:353
  30.8 11.7 %collective-permute-start.6 = (bf16[528,128]{1,0:T(8,128)(2,1)S(1)}, bf16[528,128]{1,0:T(8,128)(2,1)S(1)}, u32[]{:S(2)}, u32[]{:S(2)}) collective-permute-start(bf16[528,128]{1,0:T(8,128)(2,1)S(1)} %get-tuple-element.22), channel_id=1, source_target_pairs={{0,2},{1,3},{2,0},{3,1},{4,6},{5,7},{6,4},{7,5},{8,10},{9,11},{10,... | collective-permute-start | bytes 405512 | tf_op jit(solution)/shard_map/ppermute | solution.py:353
  32.0 10.5 %collective-permute-start.7 = (bf16[528,128]{1,0:T(8,128)(2,1)S(1)}, bf16[528,128]{1,0:T(8,128)(2,1)S(1)}, u32[]{:S(2)}, u32[]{:S(2)}) collective-permute-start(bf16[528,128]{1,0:T(8,128)(2,1)S(1)} %get-tuple-element.23), channel_id=1, source_target_pairs={{0,1},{1,0},{2,3},{3,2},{4,5},{5,4},{6,7},{7,6},{8,9},{9,8},{10,11... | collective-permute-start | bytes 405512 | tf_op jit(solution)/shard_map/ppermute | solution.py:353
  43.7 2.7 %collective-permute-start.8 = (f32[2048,128]{1,0:T(8,128)S(1)}, f32[2048,128]{1,0:T(8,128)S(1)}, u32[]{:S(2)}, u32[]{:S(2)}) collective-permute-start(f32[2048,128]{1,0:T(8,128)S(1)} %sum_slots.1), channel_id=1, source_target_pairs={{0,8},{8,0},{1,9},{9,1},{2,10},{10,2},{3,11},{11,3},{4,12},{12,4},... | collective-permute-start | bytes 3145736 | tf_op jit(solution)/shard_map/ppermute | solution.py:362

commit v8 on v7

--- a/solution.py
+++ b/solution.py
@@ -21,7 +21,6 @@
 TAG_ROWS = 16
 COUNT_SPAN = 4096
 PAIRED_MAX = 16
-CALLS = (0, 1, 4, 8)
 VMEM_LIMIT = 48 * 1024 * 1024
 
 
@@ -62,13 +61,21 @@
 
 
 def sequence(before, middle, factor):
-    values = [None] * STEPS
-    values[STEPS // 2 - 1], values[STEPS // 2] = before, middle
-    for j in range(STEPS // 2 + 1, STEPS):
-        values[j] = factor * values[j - 1] - values[j - 2]
-    for j in range(STEPS // 2 - 2, -1, -1):
-        values[j] = factor * values[j + 1] - values[j + 2]
-    return values
+    def pair(*two):
+        return jnp.concatenate(two, 0).astype(jnp.bfloat16)
+
+    up, down = [], []
+    last, value = before, middle
+    for _ in range(STEPS // 4):
+        after = factor * value - last
+        up.append(pair(value, after))
+        last, value = after, factor * after - value
+    last, value = middle, before
+    for _ in range(STEPS // 4):
+        after = factor * value - last
+        down.append(pair(after, value))
+        last, value = after, factor * after - value
+    return down[::-1] + up
 
 
 def subgrid_kernel(
@@ -161,7 +168,7 @@
             for part in range(2):
                 left += sequence(left_low[part][quad], left_mid[part][quad], left_factor[quad])
                 right += sequence(right_low[part][quad], right_mid[part][quad], right_factor[quad])
-            rows.append([jnp.concatenate(x, 0).astype(jnp.bfloat16) for x in (left, right)])
+            rows.append([jnp.concatenate(x, 0) for x in (left, right)])
         finish(rows[0], quad_at)
         return rows[1]
 
@@ -293,6 +300,12 @@
     return split.transpose(0, 2, 1, 3).reshape(blocks * tiles * parts, LANES)
 
 
+def sending_order(owners):
+    near = [d for d in range(1, owners // 2) if d & 1] + [d for d in range(2, owners // 2, 2)]
+    far = list(range(owners - 1, max(owners // 2, 1) - 1, -1))
+    return near[:2] + far + near[2:] + [0]
+
+
 def in_rows(array):
     return with_layout_constraint(array, Layout(major_to_minor=(0, 1)))
 
@@ -313,7 +326,13 @@
         jnp.where(tile_ids[:, None] == owner_range[None, :], owner_map[None, :], 0), 1
     )
     paired = owners <= PAIRED_MAX and owners & (owners - 1) == 0
-    offset = (owners - 1) - jnp.bitwise_xor(owner_ids, me) if paired else owner_ids
+    distances = sending_order(owners)
+    offset = owner_ids
+    if paired:
+        offset = jnp.bitwise_xor(owner_ids, me)
+        offset = jnp.sum(
+            jnp.where(offset[:, None] == jnp.array(distances)[None, :], owner_range[None, :], 0), 1
+        )
     index = jnp.arange(blocks, dtype=jnp.int32)
     same = (offset[None, :] == offset[:, None]) & (index[None, :] < index[:, None])
     rank = jnp.sum(same.astype(jnp.int32), 1)
@@ -338,16 +357,9 @@
     )
     token = jnp.zeros((GROUP, LANES), jnp.int32)
     if paired:
-        rows = []
-        for first, last in zip(CALLS[:-1], CALLS[1:]):
-            first, last = owners * first // CALLS[-1], owners * last // CALLS[-1]
-            if first < last:
-                *more, token = subgrids(first, (1,) * (last - first), token)
-                rows += more
+        rows = subgrids(0, (1,) * owners, token)[:-1]
         arrived = []
-        for turn in range(owners):
-            distance = owners - 1 - turn
-            piece = rows[turn]
+        for distance, piece in zip(distances, rows):
             if distance:
                 pairs = [(k, k ^ distance) for k in range(owners)]
                 piece = lax.ppermute(piece, ("blk", "tile"), pairs)

time: 47.6 us -> 52.9 us (1.11)
  waiting for transfers between devices: 11.2 us -> 17.7 us
  Pallas kernels: 16 us -> 13.3 us
  local copies, waits for them, and re-layouts: 1.42 us -> 2.07 us
    ppermute x7, waiting for transfers between devices: 8.55 us -> 15.1 us  [local(): piece = lax.ppermute(piece, ('blk', 'tile'), pairs)]
    pallas_call x3 -> x1, Pallas kernels: 14.7 us -> 12.1 us  [make_subgrids(): pl.pallas_call(functools.partial(subgrid_kernel, first, destinations, cap...]
    unnamed x10 -> x12, local copies, waits for them, and re-layouts: 1.41 us -> 2.06 us
    ppermute x7, starting transfers between devices: 15.2 us -> 15.8 us  [local(): piece = lax.ppermute(piece, ('blk', 'tile'), pairs)]
  transfers between devices with their start and end apart: 9 -> 9, of which waited for: 5 -> 5; matrix products, arithmetic and copies ran while one was open for 2% -> 2% of each run, Pallas kernels for 26% -> 0%
where the time goes in v8:
time: 52.9 us; the launch traced here: 52.7 us
  waiting for transfers between devices  17.7 us (33%)
  starting transfers between devices  16.3 us (31%)
  Pallas kernels  13.3 us (25%)
  other arithmetic  3.14 us (6%)
  local copies, waits for them, and re-layouts  2.07 us (4%)
    ppermute x7, starting transfers between devices, local(): piece = lax.ppermute(piece, ('blk', 'tile'), pairs)  15.8 us
    ppermute x7, waiting for transfers between devices, local(): piece = lax.ppermute(piece, ('blk', 'tile'), pairs)  15.1 us
    pallas_call x1, Pallas kernels, make_subgrids(): pl.pallas_call(functools.partial(subgrid_kernel, first, destinations, cap...  12.1 us
    ppermute x1, waiting for transfers between devices, local(): whole = part + lax.ppermute(part, 'samp', swap)  2.65 us
    unnamed x12, local copies, waits for them, and re-layouts  2.06 us
    add x1, other arithmetic, local(): own.astype(jnp.float32) + other.astype(jnp.float32)  1.23 us
    pallas_call x1, Pallas kernels, sum_slots(): pl.pallas_call(functools.partial(gather_kernel, capacity), out_shape=jax....  1.21 us
    add x1, other arithmetic, local(): whole = part + lax.ppermute(part, 'samp', swap)  1.08 us
  transfers between devices with their start and end apart: 9, of which 5 were waited for; matrix products, arithmetic and copies ran while one was open for 2% of the time, Pallas kernels for 0%

profile of v8, /device:TPU:0, one launch (start us, length us, event | category | flops | bytes accessed | tf_op | source)
XLA Modules:
  0.0 52.7 jit_solution(6610527258290291015)
XLA Ops:
  0.0 0.5 collective-permute-start
  0.5 0.0 copy-start.3
  0.5 0.0 copy-start.4
  0.5 0.7 %copy-done.3 = s32[256,1]{0,1:T(1,128)S(1)} copy-done((s32[256,1]{0,1:T(1,128)S(1)}, s32[256,1]{0,1:T(1,128)}, u32[]{:S(2)}) %copy-start.3) | copy-done | bytes 1048
  1.1 0.0 copy-done.4
  1.1 0.1 select_reduce_fusion.4
  1.2 0.0 copy-start.5
  1.2 0.6 %copy-done.5 = s32[8]{0:T(128)S(1)} copy-done((s32[8]{0:T(128)S(1)}, s32[8]{0:T(128)}, u32[]{:S(2)}) %copy-start.5) | copy-done | bytes 56
  1.9 0.1 select_reduce_fusion.3
  2.0 0.2 convert_reduce_fusion
  2.2 0.1 convert_reduce_fusion.1
  2.3 0.1 select_reduce_fusion.5.start_ref
  2.4 0.0 copy-start.1
  2.4 0.0 copy-start.2
  2.4 0.1 select_reduce_fusion.2
  2.5 0.6 %copy-done.1 = s32[256]{0:T(256)S(1)} copy-done((s32[256]{0:T(256)S(1)}, s32[256]{0:T(256)}, u32[]{:S(2)}) %copy-start.1) | copy-done | bytes 1048
  3.1 0.0 copy-done.2
  3.1 0.2 select_reduce_fusion
  3.2 0.0 copy-start
  3.3 0.0 collective-permute-done
  3.3 1.2 %convert_add_fusion.res_ref = f32[2048,128]{1,0:T(8,128)S(1)} fusion(bf16[2048,128]{1,0:T(8,128)(2,1)S(1)} %collective-permute-done, bf16[2048,128]{1,0:T(8,128)(2,1)} %bitcast.18), kind=kLoop, calls=%fused_computation | loop fusion | flops 786432 | bytes 2097152 | tf_op jit(solution)/shard_map/add | solution.py:356
  4.5 0.1 copy-done
  4.6 12.1 %subgrids.1 = (bf16[528,128]{1,0:T(8,128)(2,1)S(1)}, bf16[528,128]{1,0:T(8,128)(2,1)S(1)}, bf16[528,128]{1,0:T(8,128)(2,1)S(1)}, bf16[528,128]{1,0:T(8,128)(2,1)...) custom-call(s32[160]{0:T(256)S(1)} %get-tuple-element.22.block_ref, ...), custom_call_target="tpu_custom_call" | custom-call | flops 1073741824 | bytes 2097152 | tf_op jit(solution)/shard_map/subgrids/pallas_call | solution.py:220
  16.8 2.5 %collective-permute-start.1 = (bf16[528,128]{1,0:T(8,128)(2,1)S(1)}, bf16[528,128]{1,0:T(8,128)(2,1)S(1)}, u32[]{:S(2)}, u32[]{:S(2)}) collective-permute-start(bf16[528,128]{1,0:T(8,128)(2,1)S(1)} %get-tuple-element.13), channel_id=1, source_target_pairs={{0,1},{1,0},{2,3},{3,2},{4,5},{5,4},{6,7},{7,6},{8,9},{9,8},{10,11... | collective-permute-start | bytes 405512 | tf_op jit(solution)/shard_map/ppermute | solution.py:365
  19.3 1.5 %collective-permute-start.2 = (bf16[528,128]{1,0:T(8,128)(2,1)S(1)}, bf16[528,128]{1,0:T(8,128)(2,1)S(1)}, u32[]{:S(2)}, u32[]{:S(2)}) collective-permute-start(bf16[528,128]{1,0:T(8,128)(2,1)S(1)} %get-tuple-element.14), channel_id=1, source_target_pairs={{0,3},{1,2},{2,1},{3,0},{4,7},{5,6},{6,5},{7,4},{8,11},{9,10},{10,... | collective-permute-start | bytes 405512 | tf_op jit(solution)/shard_map/ppermute | solution.py:365
  20.8 3.4 %collective-permute-start.3 = (bf16[528,128]{1,0:T(8,128)(2,1)S(1)}, bf16[528,128]{1,0:T(8,128)(2,1)S(1)}, u32[]{:S(2)}, u32[]{:S(2)}) collective-permute-start(bf16[528,128]{1,0:T(8,128)(2,1)S(1)} %get-tuple-element.15), channel_id=1, source_target_pairs={{0,7},{1,6},{2,5},{3,4},{4,3},{5,2},{6,1},{7,0},{8,15},{9,14},{10,... | collective-permute-start | bytes 405512 | tf_op jit(solution)/shard_map/ppermute | solution.py:365
  24.2 1.3 %collective-permute-start.4 = (bf16[528,128]{1,0:T(8,128)(2,1)S(1)}, bf16[528,128]{1,0:T(8,128)(2,1)S(1)}, u32[]{:S(2)}, u32[]{:S(2)}) collective-permute-start(bf16[528,128]{1,0:T(8,128)(2,1)S(1)} %get-tuple-element.16), channel_id=1, source_target_pairs={{0,6},{1,7},{2,4},{3,5},{4,2},{5,3},{6,0},{7,1},{8,14},{9,15},{10,... | collective-permute-start | bytes 405512 | tf_op jit(solution)/shard_map/ppermute | solution.py:365
  25.5 0.2 collective-permute-start.5
  25.8 0.6 %collective-permute-done.1.refs_0_ = bf16[528,128]{1,0:T(8,128)(2,1)S(1)} collective-permute-done((bf16[528,128]{1,0:T(8,128)(2,1)S(1)}, bf16[528,128]{1,0:T(8,128)(2,1)S(1)}, u32[]{:S(2)}, u32[]{:S(2)}) %collective-permute-start.1) | collective-permute-done | bytes 135200 | tf_op jit(solution)/shard_map/ppermute | solution.py:365
  26.4 4.4 %collective-permute-start.6 = (bf16[528,128]{1,0:T(8,128)(2,1)S(1)}, bf16[528,128]{1,0:T(8,128)(2,1)S(1)}, u32[]{:S(2)}, u32[]{:S(2)}) collective-permute-start(bf16[528,128]{1,0:T(8,128)(2,1)S(1)} %get-tuple-element.18), channel_id=1, source_target_pairs={{0,4},{1,5},{2,6},{3,7},{4,0},{5,1},{6,2},{7,3},{8,12},{9,13},{10,... | collective-permute-start | bytes 405512 | tf_op jit(solution)/shard_map/ppermute | solution.py:365
  30.7 0.0 collective-permute-done.2.refs_1_
  30.7 2.4 %collective-permute-start.7 = (bf16[528,128]{1,0:T(8,128)(2,1)S(1)}, bf16[528,128]{1,0:T(8,128)(2,1)S(1)}, u32[]{:S(2)}, u32[]{:S(2)}) collective-permute-start(bf16[528,128]{1,0:T(8,128)(2,1)S(1)} %get-tuple-element.19), channel_id=1, source_target_pairs={{0,2},{1,3},{2,0},{3,1},{4,6},{5,7},{6,4},{7,5},{8,10},{9,11},{10,... | collective-permute-start | bytes 405512 | tf_op jit(solution)/shard_map/ppermute | solution.py:365
  33.2 0.0 collective-permute-done.3.refs_2_
  33.2 0.4 collective-permute-done.4.refs_3_
  33.6 13.1 %collective-permute-done.5.refs_4_ = bf16[528,128]{1,0:T(8,128)(2,1)S(1)} collective-permute-done((bf16[528,128]{1,0:T(8,128)(2,1)S(1)}, bf16[528,128]{1,0:T(8,128)(2,1)S(1)}, u32[]{:S(2)}, u32[]{:S(2)}) %collective-permute-start.5) | collective-permute-done | bytes 135200 | tf_op jit(solution)/shard_map/ppermute | solution.py:365
  46.7 1.0 %collective-permute-done.6.refs_5_ = bf16[528,128]{1,0:T(8,128)(2,1)S(1)} collective-permute-done((bf16[528,128]{1,0:T(8,128)(2,1)S(1)}, bf16[528,128]{1,0:T(8,128)(2,1)S(1)}, u32[]{:S(2)}, u32[]{:S(2)}) %collective-permute-start.6) | collective-permute-done | bytes 135200 | tf_op jit(solution)/shard_map/ppermute | solution.py:365
  47.7 0.0 collective-permute-done.7.refs_6_
  47.7 1.2 %sum_slots.1 = f32[2048,128]{1,0:T(8,128)S(1)} custom-call(bf16[528,128]{1,0:T(8,128)(2,1)S(1)} %collective-permute-done.1.refs_0_, bf16[528,128]{1,0:T(8,128)(2,1)S(1)} %collective-permute-done.2.refs_1_, bf16[528,128]{1,0:T(8,128)(2,1)S(1)} %collective-permute-done.3.refs_2_, bf16[528,128]{1,0:T(8,128)(2,1)S(1)} %collective-permute-done.4.refs_3_, ...), custom_call_target="tpu_custom_call" | custom-call | tf_op jit(solution)/shard_map/sum_slots/pallas_call | solution.py:280
  48.9 0.1 collective-permute-start.8
  49.0 2.6 %collective-permute-done.8 = f32[2048,128]{1,0:T(8,128)S(1)} collective-permute-done((f32[2048,128]{1,0:T(8,128)S(1)}, f32[2048,128]{1,0:T(8,128)S(1)}, u32[]{:S(2)}, u32[]{:S(2)}) %collective-permute-start.8) | collective-permute-done | bytes 1048608 | tf_op jit(solution)/shard_map/ppermute | solution.py:374
  51.6 1.1 %add.54 = f32[2048,128]{1,0:T(8,128)} add(f32[2048,128]{1,0:T(8,128)S(1)} %sum_slots.1, f32[2048,128]{1,0:T(8,128)S(1)} %collective-permute-done.8) | non-fusion elementwise | flops 262144 | bytes 3145728 | tf_op jit(solution)/shard_map/add | solution.py:374
  (5 shorter events, 0.0 us)
Async XLA Ops:
  0.0 3.3 %collective-permute-start = (bf16[2048,128]{1,0:T(8,128)(2,1)}, bf16[2048,128]{1,0:T(8,128)(2,1)S(1)}, u32[]{:S(2)}, u32[]{:S(2)}) collective-permute-start(bf16[2048,128]{1,0:T(8,128)(2,1)} %bitcast.17), channel_id=1, source_target_pairs={{0,8},{8,0},{1,9},{9,1},{2,10},{10,2},{3,11},{11,3},{4,12},{12,4},... | collective-permute-start | bytes 1572872 | tf_op jit(solution)/shard_map/ppermute | solution.py:321
  0.5 0.7 %copy-start.3 = (s32[256,1]{0,1:T(1,128)S(1)}, s32[256,1]{0,1:T(1,128)}, u32[]{:S(2)}) copy-start(s32[256,1]{0,1:T(1,128)} %param.10) | copy-start | bytes 3076
  0.5 0.7 %copy-start.4 = (s32[8]{0:T(128)S(1)}, s32[8]{0:T(128)}, u32[]{:S(2)}) copy-start(s32[8]{0:T(128)} %param.12) | copy-start | bytes 100
  1.2 0.7 %copy-start.5 = (s32[8]{0:T(128)S(1)}, s32[8]{0:T(128)}, u32[]{:S(2)}) copy-start(s32[8]{0:T(128)} %constant.58.clone) | copy-start | bytes 100
  2.4 0.7 %copy-start.1 = (s32[256]{0:T(256)S(1)}, s32[256]{0:T(256)}, u32[]{:S(2)}) copy-start(s32[256]{0:T(256)} %param.11) | copy-start | bytes 3076
  2.4 0.7 %copy-start.2 = (s32[256]{0:T(256)S(1)}, s32[256]{0:T(256)}, u32[]{:S(2)}) copy-start(s32[256]{0:T(256)} %param.9) | copy-start | bytes 3076
  3.2 1.4 %copy-start = (f32[256,2,512]{2,1,0:T(2,128)S(1)}, f32[256,2,512]{2,1,0:T(2,128)}, u32[]{:S(2)}) copy-start(f32[256,2,512]{2,1,0:T(2,128)} %param.8) | copy-start | bytes 3145732
  16.8 9.6 %collective-permute-start.1 = (bf16[528,128]{1,0:T(8,128)(2,1)S(1)}, bf16[528,128]{1,0:T(8,128)(2,1)S(1)}, u32[]{:S(2)}, u32[]{:S(2)}) collective-permute-start(bf16[528,128]{1,0:T(8,128)(2,1)S(1)} %get-tuple-element.13), channel_id=1, source_target_pairs={{0,1},{1,0},{2,3},{3,2},{4,5},{5,4},{6,7},{7,6},{8,9},{9,8},{10,11... | collective-permute-start | bytes 405512 | tf_op jit(solution)/shard_map/ppermute | solution.py:365
  19.3 11.5 %collective-permute-start.2 = (bf16[528,128]{1,0:T(8,128)(2,1)S(1)}, bf16[528,128]{1,0:T(8,128)(2,1)S(1)}, u32[]{:S(2)}, u32[]{:S(2)}) collective-permute-start(bf16[528,128]{1,0:T(8,128)(2,1)S(1)} %get-tuple-element.14), channel_id=1, source_target_pairs={{0,3},{1,2},{2,1},{3,0},{4,7},{5,6},{6,5},{7,4},{8,11},{9,10},{10,... | collective-permute-start | bytes 405512 | tf_op jit(solution)/shard_map/ppermute | solution.py:365
  20.8 12.4 %collective-permute-start.3 = (bf16[528,128]{1,0:T(8,128)(2,1)S(1)}, bf16[528,128]{1,0:T(8,128)(2,1)S(1)}, u32[]{:S(2)}, u32[]{:S(2)}) collective-permute-start(bf16[528,128]{1,0:T(8,128)(2,1)S(1)} %get-tuple-element.15), channel_id=1, source_target_pairs={{0,7},{1,6},{2,5},{3,4},{4,3},{5,2},{6,1},{7,0},{8,15},{9,14},{10,... | collective-permute-start | bytes 405512 | tf_op jit(solution)/shard_map/ppermute | solution.py:365
  24.2 9.4 %collective-permute-start.4 = (bf16[528,128]{1,0:T(8,128)(2,1)S(1)}, bf16[528,128]{1,0:T(8,128)(2,1)S(1)}, u32[]{:S(2)}, u32[]{:S(2)}) collective-permute-start(bf16[528,128]{1,0:T(8,128)(2,1)S(1)} %get-tuple-element.16), channel_id=1, source_target_pairs={{0,6},{1,7},{2,4},{3,5},{4,2},{5,3},{6,0},{7,1},{8,14},{9,15},{10,... | collective-permute-start | bytes 405512 | tf_op jit(solution)/shard_map/ppermute | solution.py:365
  25.5 21.1 %collective-permute-start.5 = (bf16[528,128]{1,0:T(8,128)(2,1)S(1)}, bf16[528,128]{1,0:T(8,128)(2,1)S(1)}, u32[]{:S(2)}, u32[]{:S(2)}) collective-permute-start(bf16[528,128]{1,0:T(8,128)(2,1)S(1)} %get-tuple-element.17), channel_id=1, source_target_pairs={{0,5},{1,4},{2,7},{3,6},{4,1},{5,0},{6,3},{7,2},{8,13},{9,12},{10,... | collective-permute-start | bytes 405512 | tf_op jit(solution)/shard_map/ppermute | solution.py:365
  26.4 21.3 %collective-permute-start.6 = (bf16[528,128]{1,0:T(8,128)(2,1)S(1)}, bf16[528,128]{1,0:T(8,128)(2,1)S(1)}, u32[]{:S(2)}, u32[]{:S(2)}) collective-permute-start(bf16[528,128]{1,0:T(8,128)(2,1)S(1)} %get-tuple-element.18), channel_id=1, source_target_pairs={{0,4},{1,5},{2,6},{3,7},{4,0},{5,1},{6,2},{7,3},{8,12},{9,13},{10,... | collective-permute-start | bytes 405512 | tf_op jit(solution)/shard_map/ppermute | solution.py:365
  30.7 16.9 %collective-permute-start.7 = (bf16[528,128]{1,0:T(8,128)(2,1)S(1)}, bf16[528,128]{1,0:T(8,128)(2,1)S(1)}, u32[]{:S(2)}, u32[]{:S(2)}) collective-permute-start(bf16[528,128]{1,0:T(8,128)(2,1)S(1)} %get-tuple-element.19), channel_id=1, source_target_pairs={{0,2},{1,3},{2,0},{3,1},{4,6},{5,7},{6,4},{7,5},{8,10},{9,11},{10,... | collective-permute-start | bytes 405512 | tf_op jit(solution)/shard_map/ppermute | solution.py:365
  48.9 2.7 %collective-permute-start.8 = (f32[2048,128]{1,0:T(8,128)S(1)}, f32[2048,128]{1,0:T(8,128)S(1)}, u32[]{:S(2)}, u32[]{:S(2)}) collective-permute-start(f32[2048,128]{1,0:T(8,128)S(1)} %sum_slots.1), channel_id=1, source_target_pairs={{0,8},{8,0},{1,9},{9,1},{2,10},{10,2},{3,11},{11,3},{4,12},{12,4},... | collective-permute-start | bytes 3145736 | tf_op jit(solution)/shard_map/ppermute | solution.py:374

commit v9 on v8

--- a/solution.py
+++ b/solution.py
@@ -20,6 +20,7 @@
 QUAD = 4
 TAG_ROWS = 16
 COUNT_SPAN = 4096
+CHUNK = 2 * LANES
 PAIRED_MAX = 16
 VMEM_LIMIT = 48 * 1024 * 1024
 
@@ -103,33 +104,7 @@
     mover[...] = jnp.where(moves, 1.0, 0.0).astype(jnp.bfloat16)
     tags[...] = jnp.zeros_like(tags)
 
-    def finish(operands, quad_at):
-        product = lax.dot_general(
-            *operands, (((1,), (1,)), ((), ())), preferred_element_type=jnp.float32
-        )
-        half = product.shape[0] // 2
-        wholes = (
-            product[:half, :LANES] - product[half:, LANES:],
-            product[half:, :LANES] + product[:half, LANES:],
-        )
-        rows = []
-        for whole in wholes:
-            whole = jnp.where(same_block, whole, 0.0)
-            for j in range(0, STEPS, 4):
-                four = [whole[(j + k) * GROUP : (j + k + 1) * GROUP] for k in range(4)]
-                rows.append(jnp.concatenate(four, 1))
-        index = jnp.clip(quad_at * QUAD, 0, last + 1 - QUAD)
-        place = row_ref[index] // (2 * SLOTS * QUAD) - first * (capacity // QUAD)
-        place = jnp.where((quad_at >= low) & (quad_at < high), place, spare)
-        found[place] = jnp.concatenate(rows, 0).astype(jnp.bfloat16)
-        tag = jnp.zeros((QUAD, LANES), jnp.int32)
-        for b in range(QUAD):
-            tag = jnp.where(quad_row == b, row_ref[index + b] % (2 * SLOTS), tag)
-        tags[place] = tag.astype(jnp.float32)
-
-    def turn(g, carried):
-        quad_at = low + 2 * g
-        finish(carried, quad_at - 1)
+    def angles(quad_at):
         for i in range(GROUP):
             packed = block_ref[jnp.minimum(quad_at * QUAD + i, last)]
             block, count = packed // COUNT_SPAN, packed % COUNT_SPAN
@@ -152,29 +127,72 @@
         after = (a - b, e + f)
         before = (a + b, e - f)
         second = [2.0 * c * near - far for near, far in zip(before, (re, im))]
-        left_mid = [by_quad(x, y) for x, y in zip((re, im), after)]
-        left_low = [by_quad(x, y) for x, y in zip(second, before)]
         factor = 2.0 - 4.0 * s * s
         left_factor = by_quad(factor, factor)
+        left = [(by_quad(x, y), by_quad(z, w)) for x, y, z, w in zip(second, before, (re, im), after)]
         c, s = first_angle(v)
         c2, s2 = 1.0 - 2.0 * s * s, 2.0 * s * c
-        right_mid = [by_quad(jnp.ones_like(c), c), by_quad(jnp.zeros_like(s), s)]
-        right_low = [by_quad(c2, c), by_quad(-s2, -s)]
         factor = 2.0 * c2
         right_factor = by_quad(factor, factor)
+        right = [
+            (by_quad(c2, c), by_quad(jnp.ones_like(c), c)),
+            (by_quad(-s2, -s), by_quad(jnp.zeros_like(s), s)),
+        ]
+        return [
+            [
+                (left[0][0][q], left[0][1][q], left[1][0][q], left[1][1][q], left_factor[q]),
+                (right[0][0][q], right[0][1][q], right[1][0][q], right[1][1][q], right_factor[q]),
+            ]
+            for q in range(2)
+        ]
+
+    def finish(seeds, quad_at):
+        product = None
+        for lanes in range(0, tiles * LANES, CHUNK):
+            operands = []
+            for side in seeds[::-1]:
+                before, middle, before_imag, middle_imag, factor = [
+                    x[:, lanes : lanes + CHUNK] for x in side
+                ]
+                operands.append(
+                    jnp.concatenate(
+                        sequence(before, middle, factor)
+                        + sequence(before_imag, middle_imag, factor),
+                        0,
+                    )
+                )
+            term = lax.dot_general(
+                operands[1], operands[0], (((1,), (1,)), ((), ())),
+                preferred_element_type=jnp.float32,
+            )
+            product = term if product is None else product + term
+        half = product.shape[0] // 2
+        wholes = (
+            product[:half, :LANES] - product[half:, LANES:],
+            product[half:, :LANES] + product[:half, LANES:],
+        )
         rows = []
-        for quad in range(2):
-            left, right = [], []
-            for part in range(2):
-                left += sequence(left_low[part][quad], left_mid[part][quad], left_factor[quad])
-                right += sequence(right_low[part][quad], right_mid[part][quad], right_factor[quad])
-            rows.append([jnp.concatenate(x, 0) for x in (left, right)])
-        finish(rows[0], quad_at)
-        return rows[1]
-
-    turns = (high - low + 1) // 2
-    nothing = jnp.zeros((4 * STEPS * QUAD, tiles * LANES), jnp.bfloat16)
-    finish(lax.fori_loop(0, turns, turn, [nothing, nothing]), low + 2 * turns - 1)
+        for whole in wholes:
+            whole = jnp.where(same_block, whole, 0.0)
+            for j in range(0, STEPS, 4):
+                four = [whole[(j + k) * GROUP : (j + k + 1) * GROUP] for k in range(4)]
+                rows.append(jnp.concatenate(four, 1))
+        index = jnp.clip(quad_at * QUAD, 0, last + 1 - QUAD)
+        place = row_ref[index] // (2 * SLOTS * QUAD) - first * (capacity // QUAD)
+        place = jnp.where((quad_at >= low) & (quad_at < high), place, spare)
+        found[place] = jnp.concatenate(rows, 0).astype(jnp.bfloat16)
+        tag = jnp.zeros((QUAD, LANES), jnp.int32)
+        for b in range(QUAD):
+            tag = jnp.where(quad_row == b, row_ref[index + b] % (2 * SLOTS), tag)
+        tags[place] = tag.astype(jnp.float32)
+
+    def turn(g, seeds):
+        quad_at = low + 2 * g
+        for q in range(2):
+            finish(seeds[q], quad_at + q)
+        return angles(quad_at + 2)
+
+    lax.fori_loop(0, (high - low + 1) // 2, turn, angles(low))
 
     shares = capacity // TAG_ROWS
     share = lax.broadcasted_iota(jnp.int32, (TAG_ROWS, LANES), 1) // (LANES // shares)
@@ -301,9 +319,7 @@
 
 
 def sending_order(owners):
-    near = [d for d in range(1, owners // 2) if d & 1] + [d for d in range(2, owners // 2, 2)]
-    far = list(range(owners - 1, max(owners // 2, 1) - 1, -1))
-    return near[:2] + far + near[2:] + [0]
+    return list(range(owners - 1, -1, -1))
 
 
 def in_rows(array):
@@ -357,7 +373,12 @@
     )
     token = jnp.zeros((GROUP, LANES), jnp.int32)
     if paired:
-        rows = subgrids(0, (1,) * owners, token)[:-1]
+        far = owners * 3 // 8
+        rows = []
+        for first, last in ((0, far), (far, owners)):
+            if first < last:
+                *more, token = subgrids(first, (1,) * (last - first), token)
+                rows += more
         arrived = []
         for distance, piece in zip(distances, rows):
             if distance:

time: 52.9 us -> 45.5 us (0.86); the launches traced: 52.7 us -> 44.7 us
  waiting for transfers between devices: 17.7 us -> 10.7 us
  starting transfers between devices: 16.3 us -> 15.7 us
    ppermute x7, waiting for transfers between devices: 15.1 us -> 8.1 us  [local(): piece = lax.ppermute(piece, ('blk', 'tile'), pairs)]
    ppermute x7, starting transfers between devices: 15.8 us -> 15.1 us  [local(): piece = lax.ppermute(piece, ('blk', 'tile'), pairs)]
    pallas_call x1 -> x2, Pallas kernels: 12.1 us -> 11.8 us  [make_subgrids(): pl.pallas_call(functools.partial(subgrid_kernel, first, destinations, cap...]
  transfers between devices with their start and end apart: 9 -> 9, of which waited for: 5 -> 5; matrix products, arithmetic and copies ran while one was open for 2% -> 2% of each run, Pallas kernels for 0% -> 18%
where the time goes in v9:
time: 45.5 us; the launch traced here: 44.7 us
  starting transfers between devices  15.7 us (35%)
  Pallas kernels  13 us (29%)
  waiting for transfers between devices  10.7 us (24%)
  other arithmetic  3.14 us (7%)
  local copies, waits for them, and re-layouts  2.07 us (5%)
    ppermute x7, starting transfers between devices, local(): piece = lax.ppermute(piece, ('blk', 'tile'), pairs)  15.1 us
    pallas_call x2, Pallas kernels, make_subgrids(): pl.pallas_call(functools.partial(subgrid_kernel, first, destinations, cap...  11.8 us
    ppermute x7, waiting for transfers between devices, local(): piece = lax.ppermute(piece, ('blk', 'tile'), pairs)  8.1 us
    ppermute x1, waiting for transfers between devices, local(): whole = part + lax.ppermute(part, 'samp', swap)  2.65 us
    unnamed x12, local copies, waits for them, and re-layouts  2.06 us
    add x1, other arithmetic, local(): own.astype(jnp.float32) + other.astype(jnp.float32)  1.23 us
    pallas_call x1, Pallas kernels, sum_slots(): pl.pallas_call(functools.partial(gather_kernel, capacity), out_shape=jax....  1.23 us
    add x1, other arithmetic, local(): whole = part + lax.ppermute(part, 'samp', swap)  1.08 us
  transfers between devices with their start and end apart: 9, of which 5 were waited for; matrix products, arithmetic and copies ran while one was open for 2% of the time, Pallas kernels for 18%

profile of v9, /device:TPU:0, one launch (start us, length us, event | category | flops | bytes accessed | tf_op | source)
XLA Modules:
  0.0 44.7 jit_solution(140636868156685840)
XLA Ops:
  0.0 0.5 %collective-permute-start = (bf16[2048,128]{1,0:T(8,128)(2,1)}, bf16[2048,128]{1,0:T(8,128)(2,1)S(1)}, u32[]{:S(2)}, u32[]{:S(2)}) collective-permute-start(bf16[2048,128]{1,0:T(8,128)(2,1)} %bitcast.18), channel_id=1, source_target_pairs={{0,8},{8,0},{1,9},{9,1},{2,10},{10,2},{3,11},{11,3},{4,12},{12,4},... | collective-permute-start | bytes 1572872 | tf_op jit(solution)/shard_map/ppermute | solution.py:337
  0.5 0.0 copy-start.3
  0.5 0.0 copy-start.4
  0.5 0.7 %copy-done.3 = s32[256,1]{0,1:T(1,128)S(1)} copy-done((s32[256,1]{0,1:T(1,128)S(1)}, s32[256,1]{0,1:T(1,128)}, u32[]{:S(2)}) %copy-start.3) | copy-done | bytes 1048
  1.1 0.0 copy-done.4
  1.1 0.1 select_reduce_fusion.4
  1.2 0.0 copy-start.5
  1.2 0.6 %copy-done.5 = s32[8]{0:T(128)S(1)} copy-done((s32[8]{0:T(128)S(1)}, s32[8]{0:T(128)}, u32[]{:S(2)}) %copy-start.5) | copy-done | bytes 56
  1.9 0.1 select_reduce_fusion.3
  2.0 0.2 convert_reduce_fusion
  2.2 0.1 convert_reduce_fusion.1
  2.3 0.1 select_reduce_fusion.5.start_ref
  2.4 0.0 copy-start.1
  2.4 0.0 copy-start.2
  2.4 0.1 select_reduce_fusion.2
  2.5 0.6 %copy-done.1 = s32[256]{0:T(256)S(1)} copy-done((s32[256]{0:T(256)S(1)}, s32[256]{0:T(256)}, u32[]{:S(2)}) %copy-start.1) | copy-done | bytes 1048
  3.1 0.0 copy-done.2
  3.1 0.2 select_reduce_fusion
  3.2 0.0 copy-start
  3.3 0.0 collective-permute-done
  3.3 1.2 %convert_add_fusion.res_ref = f32[2048,128]{1,0:T(8,128)S(1)} fusion(bf16[2048,128]{1,0:T(8,128)(2,1)S(1)} %collective-permute-done, bf16[2048,128]{1,0:T(8,128)(2,1)} %bitcast.19), kind=kLoop, calls=%fused_computation | loop fusion | flops 786432 | bytes 2097152 | tf_op jit(solution)/shard_map/add | solution.py:372
  4.5 0.1 copy-done
  4.6 3.7 %subgrids.2 = (bf16[528,128]{1,0:T(8,128)(2,1)S(1)}, bf16[528,128]{1,0:T(8,128)(2,1)S(1)}, bf16[528,128]{1,0:T(8,128)(2,1)S(1)}, s32[8,128]{1,0:T(8,128)S(1)}) custom-call(s32[160]{0:T(256)S(1)} %get-tuple-element.24.block_ref, s32[160]{0:T(256)S(1)} %get-tuple-element.23.row_ref, s32[9]{0:T(128)S(1)} %select_reduce_fusion.5.start_ref, ...), custom_call_target="tpu_custom_call" | custom-call | flops 402653184 | bytes 786432 | tf_op jit(solution)/shard_map/subgrids/pallas_call | solution.py:238
  8.3 7.5 %collective-permute-start.1 = (bf16[528,128]{1,0:T(8,128)(2,1)S(1)}, bf16[528,128]{1,0:T(8,128)(2,1)S(1)}, u32[]{:S(2)}, u32[]{:S(2)}) collective-permute-start(bf16[528,128]{1,0:T(8,128)(2,1)S(1)} %get-tuple-element.14), channel_id=1, source_target_pairs={{0,7},{1,6},{2,5},{3,4},{4,3},{5,2},{6,1},{7,0},{8,15},{9,14},{10,... | collective-permute-start | bytes 405512 | tf_op jit(solution)/shard_map/ppermute | solution.py:386
  15.8 0.0 collective-permute-start.2
  15.8 1.4 %collective-permute-start.3 = (bf16[528,128]{1,0:T(8,128)(2,1)S(1)}, bf16[528,128]{1,0:T(8,128)(2,1)S(1)}, u32[]{:S(2)}, u32[]{:S(2)}) collective-permute-start(bf16[528,128]{1,0:T(8,128)(2,1)S(1)} %get-tuple-element.16), channel_id=1, source_target_pairs={{0,5},{1,4},{2,7},{3,6},{4,1},{5,0},{6,3},{7,2},{8,13},{9,12},{10,... | collective-permute-start | bytes 405512 | tf_op jit(solution)/shard_map/ppermute | solution.py:386
  17.3 8.1 %subgrids.3 = (bf16[528,128]{1,0:T(8,128)(2,1)S(1)}, bf16[528,128]{1,0:T(8,128)(2,1)S(1)}, bf16[528,128]{1,0:T(8,128)(2,1)S(1)}, bf16[528,128]{1,0:T(8,128)(2,1)...) custom-call(s32[160]{0:T(256)S(1)} %get-tuple-element.24.block_ref, s32[160]{0:T(256)S(1)} %get-tuple-element.23.row_ref, ...), custom_call_target="tpu_custom_call" | custom-call | flops 671088640 | bytes 1310720 | tf_op jit(solution)/shard_map/subgrids/pallas_call | solution.py:238
  25.3 0.0 collective-permute-start.4
  25.3 3.8 %collective-permute-start.5 = (bf16[528,128]{1,0:T(8,128)(2,1)S(1)}, bf16[528,128]{1,0:T(8,128)(2,1)S(1)}, u32[]{:S(2)}, u32[]{:S(2)}) collective-permute-start(bf16[528,128]{1,0:T(8,128)(2,1)S(1)} %get-tuple-element.19), channel_id=1, source_target_pairs={{0,3},{1,2},{2,1},{3,0},{4,7},{5,6},{6,5},{7,4},{8,11},{9,10},{10,... | collective-permute-start | bytes 405512 | tf_op jit(solution)/shard_map/ppermute | solution.py:386
  29.2 0.0 collective-permute-done.1.refs_0_
  29.2 1.0 %collective-permute-start.6 = (bf16[528,128]{1,0:T(8,128)(2,1)S(1)}, bf16[528,128]{1,0:T(8,128)(2,1)S(1)}, u32[]{:S(2)}, u32[]{:S(2)}) collective-permute-start(bf16[528,128]{1,0:T(8,128)(2,1)S(1)} %get-tuple-element.20), channel_id=1, source_target_pairs={{0,2},{1,3},{2,0},{3,1},{4,6},{5,7},{6,4},{7,5},{8,10},{9,11},{10,... | collective-permute-start | bytes 405512 | tf_op jit(solution)/shard_map/ppermute | solution.py:386
  30.2 0.0 collective-permute-done.2.refs_1_
  30.2 1.3 %collective-permute-start.7 = (bf16[528,128]{1,0:T(8,128)(2,1)S(1)}, bf16[528,128]{1,0:T(8,128)(2,1)S(1)}, u32[]{:S(2)}, u32[]{:S(2)}) collective-permute-start(bf16[528,128]{1,0:T(8,128)(2,1)S(1)} %get-tuple-element.21), channel_id=1, source_target_pairs={{0,1},{1,0},{2,3},{3,2},{4,5},{5,4},{6,7},{7,6},{8,9},{9,8},{10,11... | collective-permute-start | bytes 405512 | tf_op jit(solution)/shard_map/ppermute | solution.py:386
  31.6 4.6 %collective-permute-done.3.refs_2_ = bf16[528,128]{1,0:T(8,128)(2,1)S(1)} collective-permute-done((bf16[528,128]{1,0:T(8,128)(2,1)S(1)}, bf16[528,128]{1,0:T(8,128)(2,1)S(1)}, u32[]{:S(2)}, u32[]{:S(2)}) %collective-permute-start.3) | collective-permute-done | bytes 135200 | tf_op jit(solution)/shard_map/ppermute | solution.py:386
  36.1 2.4 %collective-permute-done.4.refs_3_ = bf16[528,128]{1,0:T(8,128)(2,1)S(1)} collective-permute-done((bf16[528,128]{1,0:T(8,128)(2,1)S(1)}, bf16[528,128]{1,0:T(8,128)(2,1)S(1)}, u32[]{:S(2)}, u32[]{:S(2)}) %collective-permute-start.4) | collective-permute-done | bytes 135200 | tf_op jit(solution)/shard_map/ppermute | solution.py:386
  38.5 0.5 %collective-permute-done.5.refs_4_ = bf16[528,128]{1,0:T(8,128)(2,1)S(1)} collective-permute-done((bf16[528,128]{1,0:T(8,128)(2,1)S(1)}, bf16[528,128]{1,0:T(8,128)(2,1)S(1)}, u32[]{:S(2)}, u32[]{:S(2)}) %collective-permute-start.5) | collective-permute-done | bytes 135200 | tf_op jit(solution)/shard_map/ppermute | solution.py:386
  39.0 0.6 %collective-permute-done.6.refs_5_ = bf16[528,128]{1,0:T(8,128)(2,1)S(1)} collective-permute-done((bf16[528,128]{1,0:T(8,128)(2,1)S(1)}, bf16[528,128]{1,0:T(8,128)(2,1)S(1)}, u32[]{:S(2)}, u32[]{:S(2)}) %collective-permute-start.6) | collective-permute-done | bytes 135200 | tf_op jit(solution)/shard_map/ppermute | solution.py:386
  39.6 0.0 collective-permute-done.7.refs_6_
  39.6 1.2 %sum_slots.1 = f32[2048,128]{1,0:T(8,128)S(1)} custom-call(bf16[528,128]{1,0:T(8,128)(2,1)S(1)} %collective-permute-done.1.refs_0_, bf16[528,128]{1,0:T(8,128)(2,1)S(1)} %collective-permute-done.2.refs_1_, bf16[528,128]{1,0:T(8,128)(2,1)S(1)} %collective-permute-done.3.refs_2_, bf16[528,128]{1,0:T(8,128)(2,1)S(1)} %collective-permute-done.4.refs_3_, ...), custom_call_target="tpu_custom_call" | custom-call | tf_op jit(solution)/shard_map/sum_slots/pallas_call | solution.py:298
  40.9 0.1 collective-permute-start.8
  41.0 2.6 %collective-permute-done.8 = f32[2048,128]{1,0:T(8,128)S(1)} collective-permute-done((f32[2048,128]{1,0:T(8,128)S(1)}, f32[2048,128]{1,0:T(8,128)S(1)}, u32[]{:S(2)}, u32[]{:S(2)}) %collective-permute-start.8) | collective-permute-done | bytes 1048608 | tf_op jit(solution)/shard_map/ppermute | solution.py:395
  43.6 1.1 %add.54 = f32[2048,128]{1,0:T(8,128)} add(f32[2048,128]{1,0:T(8,128)S(1)} %sum_slots.1, f32[2048,128]{1,0:T(8,128)S(1)} %collective-permute-done.8) | non-fusion elementwise | flops 262144 | bytes 3145728 | tf_op jit(solution)/shard_map/add | solution.py:395
  (5 shorter events, 0.0 us)
Async XLA Ops:
  0.0 3.3 %collective-permute-start = (bf16[2048,128]{1,0:T(8,128)(2,1)}, bf16[2048,128]{1,0:T(8,128)(2,1)S(1)}, u32[]{:S(2)}, u32[]{:S(2)}) collective-permute-start(bf16[2048,128]{1,0:T(8,128)(2,1)} %bitcast.18), channel_id=1, source_target_pairs={{0,8},{8,0},{1,9},{9,1},{2,10},{10,2},{3,11},{11,3},{4,12},{12,4},... | collective-permute-start | bytes 1572872 | tf_op jit(solution)/shard_map/ppermute | solution.py:337
  0.5 0.7 %copy-start.3 = (s32[256,1]{0,1:T(1,128)S(1)}, s32[256,1]{0,1:T(1,128)}, u32[]{:S(2)}) copy-start(s32[256,1]{0,1:T(1,128)} %param.10) | copy-start | bytes 3076
  0.5 0.7 %copy-start.4 = (s32[8]{0:T(128)S(1)}, s32[8]{0:T(128)}, u32[]{:S(2)}) copy-start(s32[8]{0:T(128)} %param.12) | copy-start | bytes 100
  1.2 0.7 %copy-start.5 = (s32[8]{0:T(128)S(1)}, s32[8]{0:T(128)}, u32[]{:S(2)}) copy-start(s32[8]{0:T(128)} %constant.58.clone) | copy-start | bytes 100
  2.4 0.7 %copy-start.1 = (s32[256]{0:T(256)S(1)}, s32[256]{0:T(256)}, u32[]{:S(2)}) copy-start(s32[256]{0:T(256)} %param.11) | copy-start | bytes 3076
  2.4 0.7 %copy-start.2 = (s32[256]{0:T(256)S(1)}, s32[256]{0:T(256)}, u32[]{:S(2)}) copy-start(s32[256]{0:T(256)} %param.9) | copy-start | bytes 3076
  3.2 1.4 %copy-start = (f32[256,2,512]{2,1,0:T(2,128)S(1)}, f32[256,2,512]{2,1,0:T(2,128)}, u32[]{:S(2)}) copy-start(f32[256,2,512]{2,1,0:T(2,128)} %param.8) | copy-start | bytes 3145732
  8.3 20.9 %collective-permute-start.1 = (bf16[528,128]{1,0:T(8,128)(2,1)S(1)}, bf16[528,128]{1,0:T(8,128)(2,1)S(1)}, u32[]{:S(2)}, u32[]{:S(2)}) collective-permute-start(bf16[528,128]{1,0:T(8,128)(2,1)S(1)} %get-tuple-element.14), channel_id=1, source_target_pairs={{0,7},{1,6},{2,5},{3,4},{4,3},{5,2},{6,1},{7,0},{8,15},{9,14},{10,... | collective-permute-start | bytes 405512 | tf_op jit(solution)/shard_map/ppermute | solution.py:386
  15.8 14.4 %collective-permute-start.2 = (bf16[528,128]{1,0:T(8,128)(2,1)S(1)}, bf16[528,128]{1,0:T(8,128)(2,1)S(1)}, u32[]{:S(2)}, u32[]{:S(2)}) collective-permute-start(bf16[528,128]{1,0:T(8,128)(2,1)S(1)} %get-tuple-element.15), channel_id=1, source_target_pairs={{0,6},{1,7},{2,4},{3,5},{4,2},{5,3},{6,0},{7,1},{8,14},{9,15},{10,... | collective-permute-start | bytes 405512 | tf_op jit(solution)/shard_map/ppermute | solution.py:386
  15.8 20.3 %collective-permute-start.3 = (bf16[528,128]{1,0:T(8,128)(2,1)S(1)}, bf16[528,128]{1,0:T(8,128)(2,1)S(1)}, u32[]{:S(2)}, u32[]{:S(2)}) collective-permute-start(bf16[528,128]{1,0:T(8,128)(2,1)S(1)} %get-tuple-element.16), channel_id=1, source_target_pairs={{0,5},{1,4},{2,7},{3,6},{4,1},{5,0},{6,3},{7,2},{8,13},{9,12},{10,... | collective-permute-start | bytes 405512 | tf_op jit(solution)/shard_map/ppermute | solution.py:386
  25.3 13.2 %collective-permute-start.4 = (bf16[528,128]{1,0:T(8,128)(2,1)S(1)}, bf16[528,128]{1,0:T(8,128)(2,1)S(1)}, u32[]{:S(2)}, u32[]{:S(2)}) collective-permute-start(bf16[528,128]{1,0:T(8,128)(2,1)S(1)} %get-tuple-element.18), channel_id=1, source_target_pairs={{0,4},{1,5},{2,6},{3,7},{4,0},{5,1},{6,2},{7,3},{8,12},{9,13},{10,... | collective-permute-start | bytes 405512 | tf_op jit(solution)/shard_map/ppermute | solution.py:386
  25.3 13.7 %collective-permute-start.5 = (bf16[528,128]{1,0:T(8,128)(2,1)S(1)}, bf16[528,128]{1,0:T(8,128)(2,1)S(1)}, u32[]{:S(2)}, u32[]{:S(2)}) collective-permute-start(bf16[528,128]{1,0:T(8,128)(2,1)S(1)} %get-tuple-element.19), channel_id=1, source_target_pairs={{0,3},{1,2},{2,1},{3,0},{4,7},{5,6},{6,5},{7,4},{8,11},{9,10},{10,... | collective-permute-start | bytes 405512 | tf_op jit(solution)/shard_map/ppermute | solution.py:386
  29.2 10.5 %collective-permute-start.6 = (bf16[528,128]{1,0:T(8,128)(2,1)S(1)}, bf16[528,128]{1,0:T(8,128)(2,1)S(1)}, u32[]{:S(2)}, u32[]{:S(2)}) collective-permute-start(bf16[528,128]{1,0:T(8,128)(2,1)S(1)} %get-tuple-element.20), channel_id=1, source_target_pairs={{0,2},{1,3},{2,0},{3,1},{4,6},{5,7},{6,4},{7,5},{8,10},{9,11},{10,... | collective-permute-start | bytes 405512 | tf_op jit(solution)/shard_map/ppermute | solution.py:386
  30.2 9.4 %collective-permute-start.7 = (bf16[528,128]{1,0:T(8,128)(2,1)S(1)}, bf16[528,128]{1,0:T(8,128)(2,1)S(1)}, u32[]{:S(2)}, u32[]{:S(2)}) collective-permute-start(bf16[528,128]{1,0:T(8,128)(2,1)S(1)} %get-tuple-element.21), channel_id=1, source_target_pairs={{0,1},{1,0},{2,3},{3,2},{4,5},{5,4},{6,7},{7,6},{8,9},{9,8},{10,11... | collective-permute-start | bytes 405512 | tf_op jit(solution)/shard_map/ppermute | solution.py:386
  40.9 2.7 %collective-permute-start.8 = (f32[2048,128]{1,0:T(8,128)S(1)}, f32[2048,128]{1,0:T(8,128)S(1)}, u32[]{:S(2)}, u32[]{:S(2)}) collective-permute-start(f32[2048,128]{1,0:T(8,128)S(1)} %sum_slots.1), channel_id=1, source_target_pairs={{0,8},{8,0},{1,9},{9,1},{2,10},{10,2},{3,11},{11,3},{4,12},{12,4},... | collective-permute-start | bytes 3145736 | tf_op jit(solution)/shard_map/ppermute | solution.py:395

commit v10 on v9

--- a/solution.py
+++ b/solution.py
@@ -22,6 +22,7 @@
 COUNT_SPAN = 4096
 CHUNK = 2 * LANES
 PAIRED_MAX = 16
+CALLS = (0, 2, 4, 8)
 VMEM_LIMIT = 48 * 1024 * 1024
 
 
@@ -338,9 +339,10 @@
 
     tile_ids = tile_of_block[:, 0]
     owner_range = jnp.arange(owners, dtype=jnp.int32)
-    owner_ids = jnp.sum(
-        jnp.where(tile_ids[:, None] == owner_range[None, :], owner_map[None, :], 0), 1
-    )
+    packed = jnp.sum(
+        jnp.where(tile_ids[:, None] == owner_range[None, :], owner_map[None, :] * (SLOTS * COUNT_SPAN), 0), 1
+    ) + (slot_of_block * COUNT_SPAN + counts)
+    owner_ids = packed // (SLOTS * COUNT_SPAN)
     paired = owners <= PAIRED_MAX and owners & (owners - 1) == 0
     distances = sending_order(owners)
     offset = owner_ids
@@ -362,8 +364,8 @@
     longest = ((blocks + owners) // 2 + owners * (QUAD - 1)) // GROUP * GROUP + GROUP
     wanted = jnp.arange(longest, dtype=jnp.int32)
     chosen = place[None, :] == wanted[:, None]
-    block_and_count = index * COUNT_SPAN + counts
-    row_and_tag = (offset * capacity + rank // 2) * (2 * SLOTS) + slot_of_block + 1
+    block_and_count = index * COUNT_SPAN + packed % COUNT_SPAN
+    row_and_tag = (offset * capacity + rank // 2) * (2 * SLOTS) + packed // COUNT_SPAN % SLOTS + 1
     block = jnp.sum(jnp.where(chosen, block_and_count[None, :], 0), 1)
     row = jnp.sum(jnp.where(chosen, row_and_tag[None, :], 0), 1)
 
@@ -373,9 +375,9 @@
     )
     token = jnp.zeros((GROUP, LANES), jnp.int32)
     if paired:
-        far = owners * 3 // 8
         rows = []
-        for first, last in ((0, far), (far, owners)):
+        for first, last in zip(CALLS[:-1], CALLS[1:]):
+            first, last = owners * first // CALLS[-1], owners * last // CALLS[-1]
             if first < last:
                 *more, token = subgrids(first, (1,) * (last - first), token)
                 rows += more

time: 45.5 us -> 47.6 us (1.046); the launches traced: 44.7 us -> 48.5 us
  waiting for transfers between devices: 10.7 us -> 13.2 us
  Pallas kernels: 13 us -> 14.4 us
  starting transfers between devices: 15.7 us -> 14.9 us
  local copies, waits for them, and re-layouts: 2.07 us -> 2.7 us
    ppermute x7, waiting for transfers between devices: 8.1 us -> 10.6 us  [local(): piece = lax.ppermute(piece, ('blk', 'tile'), pairs)]
    pallas_call x2 -> x3, Pallas kernels: 11.8 us -> 13.2 us  [make_subgrids(): pl.pallas_call(functools.partial(subgrid_kernel, first, destinations, cap...]
    ppermute x7, starting transfers between devices: 15.1 us -> 14.4 us  [local(): piece = lax.ppermute(piece, ('blk', 'tile'), pairs)]
    unnamed x12, local copies, waits for them, and re-layouts: 2.06 us -> 2.69 us
  transfers between devices with their start and end apart: 9 -> 9, of which waited for: 5 -> 5; matrix products, arithmetic and copies ran while one was open for 2% -> 2% of each run, Pallas kernels for 18% -> 19%
where the time goes in v10:
time: 47.6 us; the launch traced here: 48.5 us
  starting transfers between devices  14.9 us (31%)
  Pallas kernels  14.4 us (30%)
  waiting for transfers between devices  13.2 us (28%)
  other arithmetic  3.17 us (7%)
  local copies, waits for them, and re-layouts  2.7 us (6%)
    ppermute x7, starting transfers between devices, local(): piece = lax.ppermute(piece, ('blk', 'tile'), pairs)  14.4 us
    pallas_call x3, Pallas kernels, make_subgrids(): pl.pallas_call(functools.partial(subgrid_kernel, first, destinations, cap...  13.2 us
    ppermute x7, waiting for transfers between devices, local(): piece = lax.ppermute(piece, ('blk', 'tile'), pairs)  10.6 us
    unnamed x12, local copies, waits for them, and re-layouts  2.69 us
    ppermute x1, waiting for transfers between devices, local(): whole = part + lax.ppermute(part, 'samp', swap)  2.65 us
    add x1, other arithmetic, local(): own.astype(jnp.float32) + other.astype(jnp.float32)  1.23 us
    pallas_call x1, Pallas kernels, sum_slots(): pl.pallas_call(functools.partial(gather_kernel, capacity), out_shape=jax....  1.21 us
    add x1, other arithmetic, local(): whole = part + lax.ppermute(part, 'samp', swap)  1.08 us
  transfers between devices with their start and end apart: 9, of which 5 were waited for; matrix products, arithmetic and copies ran while one was open for 2% of the time, Pallas kernels for 19%

profile of v10, /device:TPU:0, one launch (start us, length us, event | category | flops | bytes accessed | tf_op | source)
XLA Modules:
  0.0 48.5 jit_solution(5262601304519591158)
XLA Ops:
  0.0 0.5 collective-permute-start
  0.5 0.0 copy-start.5
  0.5 0.7 %copy-done.5 = s32[8]{0:T(128)S(1)} copy-done((s32[8]{0:T(128)S(1)}, s32[8]{0:T(128)}, u32[]{:S(2)}) %copy-start.5) | copy-done | bytes 56
  1.1 0.0 copy-start.3
  1.1 0.7 %copy-done.3 = s32[256,1]{0,1:T(1,128)S(1)} copy-done((s32[256,1]{0,1:T(1,128)S(1)}, s32[256,1]{0,1:T(1,128)}, u32[]{:S(2)}) %copy-start.3) | copy-done | bytes 1048
  1.8 0.0 copy-start.1
  1.8 0.0 copy-start.2
  1.8 0.1 select_reduce_fusion.4
  1.9 0.6 %copy-done.1 = s32[256]{0:T(256)S(1)} copy-done((s32[256]{0:T(256)S(1)}, s32[256]{0:T(256)}, u32[]{:S(2)}) %copy-start.1) | copy-done | bytes 1048
  2.5 0.0 copy-done.2
  2.5 0.0 copy-start.4
  2.5 0.6 %copy-done.4 = s32[8]{0:T(128)S(1)} copy-done((s32[8]{0:T(128)S(1)}, s32[8]{0:T(128)}, u32[]{:S(2)}) %copy-start.4) | copy-done | bytes 56
  3.2 0.1 select_reduce_fusion.3
  3.2 0.2 convert_reduce_fusion
  3.4 0.1 convert_reduce_fusion.1
  3.6 0.1 select_reduce_fusion.5.start_ref
  3.7 0.1 select_reduce_fusion.2
  3.8 0.2 select_reduce_fusion
  3.9 0.0 copy-start
  3.9 0.0 collective-permute-done
  3.9 1.2 %convert_add_fusion.res_ref = f32[2048,128]{1,0:T(8,128)S(1)} fusion(bf16[2048,128]{1,0:T(8,128)(2,1)S(1)} %collective-permute-done, bf16[2048,128]{1,0:T(8,128)(2,1)} %bitcast.20), kind=kLoop, calls=%fused_computation | loop fusion | flops 786432 | bytes 2097152 | tf_op jit(solution)/shard_map/add | solution.py:374
  5.2 0.1 copy-done
  5.3 4.0 %subgrids.3 = (bf16[528,128]{1,0:T(8,128)(2,1)S(1)}, bf16[528,128]{1,0:T(8,128)(2,1)S(1)}, s32[8,128]{1,0:T(8,128)S(1)}) custom-call(s32[160]{0:T(256)S(1)} %get-tuple-element.26.block_ref, s32[160]{0:T(256)S(1)} %get-tuple-element.25.row_ref, s32[9]{0:T(128)S(1)} %select_reduce_fusion.5.start_ref, s32[8,128]{1,0:T(8,128)S(1)} %broadcast_in_dim.87.token_ref, ...), custom_call_target="tpu_custom_call" | custom-call | flops 268435456 | bytes 524288 | tf_op jit(solution)/shard_map/subgrids/pallas_call | solution.py:239
  9.3 4.6 %collective-permute-start.1 = (bf16[528,128]{1,0:T(8,128)(2,1)S(1)}, bf16[528,128]{1,0:T(8,128)(2,1)S(1)}, u32[]{:S(2)}, u32[]{:S(2)}) collective-permute-start(bf16[528,128]{1,0:T(8,128)(2,1)S(1)} %get-tuple-element.15), channel_id=1, source_target_pairs={{0,7},{1,6},{2,5},{3,4},{4,3},{5,2},{6,1},{7,0},{8,15},{9,14},{10,... | collective-permute-start | bytes 405512 | tf_op jit(solution)/shard_map/ppermute | solution.py:388
  14.0 0.2 collective-permute-start.2
  14.2 2.1 %subgrids.4 = (bf16[528,128]{1,0:T(8,128)(2,1)S(1)}, bf16[528,128]{1,0:T(8,128)(2,1)S(1)}, s32[8,128]{1,0:T(8,128)S(1)}) custom-call(s32[160]{0:T(256)S(1)} %get-tuple-element.26.block_ref, s32[160]{0:T(256)S(1)} %get-tuple-element.25.row_ref, s32[9]{0:T(128)S(1)} %select_reduce_fusion.5.start_ref, s32[8,128]{1,0:T(8,128)S(1)} %get-tuple-element.17.token_ref, ...), custom_call_target="tpu_custom_call" | custom-call | flops 268435456 | bytes 524288 | tf_op jit(solution)/shard_map/subgrids/pallas_call | solution.py:239
  16.4 4.1 %collective-permute-start.3 = (bf16[528,128]{1,0:T(8,128)(2,1)S(1)}, bf16[528,128]{1,0:T(8,128)(2,1)S(1)}, u32[]{:S(2)}, u32[]{:S(2)}) collective-permute-start(bf16[528,128]{1,0:T(8,128)(2,1)S(1)} %get-tuple-element.18), channel_id=1, source_target_pairs={{0,5},{1,4},{2,7},{3,6},{4,1},{5,0},{6,3},{7,2},{8,13},{9,12},{10,... | collective-permute-start | bytes 405512 | tf_op jit(solution)/shard_map/ppermute | solution.py:388
  20.5 0.0 collective-permute-start.4
  20.5 7.0 %subgrids.5 = (bf16[528,128]{1,0:T(8,128)(2,1)S(1)}, bf16[528,128]{1,0:T(8,128)(2,1)S(1)}, bf16[528,128]{1,0:T(8,128)(2,1)S(1)}, bf16[528,128]{1,0:T(8,128)(2,1)S(1)}, s32[8,128]{1,0:T(8,128)}) custom-call(s32[160]{0:T(256)S(1)} %get-tuple-element.26.block_ref, s32[160]{0:T(256)S(1)} %get-tuple-element.25.row_ref, s32[9]{0:T(128)S(1)} %select_reduce_fusion.5.start_ref, ...), custom_call_target="tpu_custom_call" | custom-call | flops 536870912 | bytes 1048576 | tf_op jit(solution)/shard_map/subgrids/pallas_call | solution.py:239
  27.5 3.4 %collective-permute-start.5 = (bf16[528,128]{1,0:T(8,128)(2,1)S(1)}, bf16[528,128]{1,0:T(8,128)(2,1)S(1)}, u32[]{:S(2)}, u32[]{:S(2)}) collective-permute-start(bf16[528,128]{1,0:T(8,128)(2,1)S(1)} %get-tuple-element.21), channel_id=1, source_target_pairs={{0,3},{1,2},{2,1},{3,0},{4,7},{5,6},{6,5},{7,4},{8,11},{9,10},{10,... | collective-permute-start | bytes 405512 | tf_op jit(solution)/shard_map/ppermute | solution.py:388
  30.9 0.0 collective-permute-done.1.refs_0_
  30.9 0.4 collective-permute-start.6
  31.3 0.0 collective-permute-done.2.refs_1_
  31.3 1.5 %collective-permute-start.7 = (bf16[528,128]{1,0:T(8,128)(2,1)S(1)}, bf16[528,128]{1,0:T(8,128)(2,1)S(1)}, u32[]{:S(2)}, u32[]{:S(2)}) collective-permute-start(bf16[528,128]{1,0:T(8,128)(2,1)S(1)} %get-tuple-element.23), channel_id=1, source_target_pairs={{0,1},{1,0},{2,3},{3,2},{4,5},{5,4},{6,7},{7,6},{8,9},{9,8},{10,11... | collective-permute-start | bytes 405512 | tf_op jit(solution)/shard_map/ppermute | solution.py:388
  32.9 3.0 %collective-permute-done.3.refs_2_ = bf16[528,128]{1,0:T(8,128)(2,1)S(1)} collective-permute-done((bf16[528,128]{1,0:T(8,128)(2,1)S(1)}, bf16[528,128]{1,0:T(8,128)(2,1)S(1)}, u32[]{:S(2)}, u32[]{:S(2)}) %collective-permute-start.3) | collective-permute-done | bytes 135200 | tf_op jit(solution)/shard_map/ppermute | solution.py:388
  35.8 2.3 %collective-permute-done.4.refs_3_ = bf16[528,128]{1,0:T(8,128)(2,1)S(1)} collective-permute-done((bf16[528,128]{1,0:T(8,128)(2,1)S(1)}, bf16[528,128]{1,0:T(8,128)(2,1)S(1)}, u32[]{:S(2)}, u32[]{:S(2)}) %collective-permute-start.4) | collective-permute-done | bytes 135200 | tf_op jit(solution)/shard_map/ppermute | solution.py:388
  38.1 3.1 %collective-permute-done.5.refs_4_ = bf16[528,128]{1,0:T(8,128)(2,1)S(1)} collective-permute-done((bf16[528,128]{1,0:T(8,128)(2,1)S(1)}, bf16[528,128]{1,0:T(8,128)(2,1)S(1)}, u32[]{:S(2)}, u32[]{:S(2)}) %collective-permute-start.5) | collective-permute-done | bytes 135200 | tf_op jit(solution)/shard_map/ppermute | solution.py:388
  41.2 2.2 %collective-permute-done.6.refs_5_ = bf16[528,128]{1,0:T(8,128)(2,1)S(1)} collective-permute-done((bf16[528,128]{1,0:T(8,128)(2,1)S(1)}, bf16[528,128]{1,0:T(8,128)(2,1)S(1)}, u32[]{:S(2)}, u32[]{:S(2)}) %collective-permute-start.6) | collective-permute-done | bytes 135200 | tf_op jit(solution)/shard_map/ppermute | solution.py:388
  43.4 0.0 collective-permute-done.7.refs_6_
  43.4 1.2 %sum_slots.1 = f32[2048,128]{1,0:T(8,128)S(1)} custom-call(bf16[528,128]{1,0:T(8,128)(2,1)S(1)} %collective-permute-done.1.refs_0_, bf16[528,128]{1,0:T(8,128)(2,1)S(1)} %collective-permute-done.2.refs_1_, bf16[528,128]{1,0:T(8,128)(2,1)S(1)} %collective-permute-done.3.refs_2_, bf16[528,128]{1,0:T(8,128)(2,1)S(1)} %collective-permute-done.4.refs_3_, ...), custom_call_target="tpu_custom_call" | custom-call | tf_op jit(solution)/shard_map/sum_slots/pallas_call | solution.py:299
  44.7 0.1 collective-permute-start.8
  44.7 2.6 %collective-permute-done.8 = f32[2048,128]{1,0:T(8,128)S(1)} collective-permute-done((f32[2048,128]{1,0:T(8,128)S(1)}, f32[2048,128]{1,0:T(8,128)S(1)}, u32[]{:S(2)}, u32[]{:S(2)}) %collective-permute-start.8) | collective-permute-done | bytes 1048608 | tf_op jit(solution)/shard_map/ppermute | solution.py:397
  47.4 1.1 %add.76 = f32[2048,128]{1,0:T(8,128)} add(f32[2048,128]{1,0:T(8,128)S(1)} %sum_slots.1, f32[2048,128]{1,0:T(8,128)S(1)} %collective-permute-done.8) | non-fusion elementwise | flops 262144 | bytes 3145728 | tf_op jit(solution)/shard_map/add | solution.py:397
  (7 shorter events, 0.1 us)
Async XLA Ops:
  0.0 3.9 %collective-permute-start = (bf16[2048,128]{1,0:T(8,128)(2,1)}, bf16[2048,128]{1,0:T(8,128)(2,1)S(1)}, u32[]{:S(2)}, u32[]{:S(2)}) collective-permute-start(bf16[2048,128]{1,0:T(8,128)(2,1)} %bitcast.19), channel_id=1, source_target_pairs={{0,8},{8,0},{1,9},{9,1},{2,10},{10,2},{3,11},{11,3},{4,12},{12,4},... | collective-permute-start | bytes 1572872 | tf_op jit(solution)/shard_map/ppermute | solution.py:338
  0.5 0.7 %copy-start.5 = (s32[8]{0:T(128)S(1)}, s32[8]{0:T(128)}, u32[]{:S(2)}) copy-start(s32[8]{0:T(128)} %param.12) | copy-start | bytes 100
  1.1 0.7 %copy-start.3 = (s32[256,1]{0,1:T(1,128)S(1)}, s32[256,1]{0,1:T(1,128)}, u32[]{:S(2)}) copy-start(s32[256,1]{0,1:T(1,128)} %param.10) | copy-start | bytes 3076
  1.8 0.7 %copy-start.1 = (s32[256]{0:T(256)S(1)}, s32[256]{0:T(256)}, u32[]{:S(2)}) copy-start(s32[256]{0:T(256)} %param.9) | copy-start | bytes 3076
  1.8 0.7 %copy-start.2 = (s32[256]{0:T(256)S(1)}, s32[256]{0:T(256)}, u32[]{:S(2)}) copy-start(s32[256]{0:T(256)} %param.11) | copy-start | bytes 3076
  2.5 0.7 %copy-start.4 = (s32[8]{0:T(128)S(1)}, s32[8]{0:T(128)}, u32[]{:S(2)}) copy-start(s32[8]{0:T(128)} %constant.104.clone) | copy-start | bytes 100
  3.9 1.4 %copy-start = (f32[256,2,512]{2,1,0:T(2,128)S(1)}, f32[256,2,512]{2,1,0:T(2,128)}, u32[]{:S(2)}) copy-start(f32[256,2,512]{2,1,0:T(2,128)} %param.8) | copy-start | bytes 3145732
  9.3 21.6 %collective-permute-start.1 = (bf16[528,128]{1,0:T(8,128)(2,1)S(1)}, bf16[528,128]{1,0:T(8,128)(2,1)S(1)}, u32[]{:S(2)}, u32[]{:S(2)}) collective-permute-start(bf16[528,128]{1,0:T(8,128)(2,1)S(1)} %get-tuple-element.15), channel_id=1, source_target_pairs={{0,7},{1,6},{2,5},{3,4},{4,3},{5,2},{6,1},{7,0},{8,15},{9,14},{10,... | collective-permute-start | bytes 405512 | tf_op jit(solution)/shard_map/ppermute | solution.py:388
  14.0 17.3 %collective-permute-start.2 = (bf16[528,128]{1,0:T(8,128)(2,1)S(1)}, bf16[528,128]{1,0:T(8,128)(2,1)S(1)}, u32[]{:S(2)}, u32[]{:S(2)}) collective-permute-start(bf16[528,128]{1,0:T(8,128)(2,1)S(1)} %get-tuple-element.16), channel_id=1, source_target_pairs={{0,6},{1,7},{2,4},{3,5},{4,2},{5,3},{6,0},{7,1},{8,14},{9,15},{10,... | collective-permute-start | bytes 405512 | tf_op jit(solution)/shard_map/ppermute | solution.py:388
  16.4 19.5 %collective-permute-start.3 = (bf16[528,128]{1,0:T(8,128)(2,1)S(1)}, bf16[528,128]{1,0:T(8,128)(2,1)S(1)}, u32[]{:S(2)}, u32[]{:S(2)}) collective-permute-start(bf16[528,128]{1,0:T(8,128)(2,1)S(1)} %get-tuple-element.18), channel_id=1, source_target_pairs={{0,5},{1,4},{2,7},{3,6},{4,1},{5,0},{6,3},{7,2},{8,13},{9,12},{10,... | collective-permute-start | bytes 405512 | tf_op jit(solution)/shard_map/ppermute | solution.py:388
  20.5 17.6 %collective-permute-start.4 = (bf16[528,128]{1,0:T(8,128)(2,1)S(1)}, bf16[528,128]{1,0:T(8,128)(2,1)S(1)}, u32[]{:S(2)}, u32[]{:S(2)}) collective-permute-start(bf16[528,128]{1,0:T(8,128)(2,1)S(1)} %get-tuple-element.19), channel_id=1, source_target_pairs={{0,4},{1,5},{2,6},{3,7},{4,0},{5,1},{6,2},{7,3},{8,12},{9,13},{10,... | collective-permute-start | bytes 405512 | tf_op jit(solution)/shard_map/ppermute | solution.py:388
  27.5 13.7 %collective-permute-start.5 = (bf16[528,128]{1,0:T(8,128)(2,1)S(1)}, bf16[528,128]{1,0:T(8,128)(2,1)S(1)}, u32[]{:S(2)}, u32[]{:S(2)}) collective-permute-start(bf16[528,128]{1,0:T(8,128)(2,1)S(1)} %get-tuple-element.21), channel_id=1, source_target_pairs={{0,3},{1,2},{2,1},{3,0},{4,7},{5,6},{6,5},{7,4},{8,11},{9,10},{10,... | collective-permute-start | bytes 405512 | tf_op jit(solution)/shard_map/ppermute | solution.py:388
  30.9 12.5 %collective-permute-start.6 = (bf16[528,128]{1,0:T(8,128)(2,1)S(1)}, bf16[528,128]{1,0:T(8,128)(2,1)S(1)}, u32[]{:S(2)}, u32[]{:S(2)}) collective-permute-start(bf16[528,128]{1,0:T(8,128)(2,1)S(1)} %get-tuple-element.22), channel_id=1, source_target_pairs={{0,2},{1,3},{2,0},{3,1},{4,6},{5,7},{6,4},{7,5},{8,10},{9,11},{10,... | collective-permute-start | bytes 405512 | tf_op jit(solution)/shard_map/ppermute | solution.py:388
  31.3 12.1 %collective-permute-start.7 = (bf16[528,128]{1,0:T(8,128)(2,1)S(1)}, bf16[528,128]{1,0:T(8,128)(2,1)S(1)}, u32[]{:S(2)}, u32[]{:S(2)}) collective-permute-start(bf16[528,128]{1,0:T(8,128)(2,1)S(1)} %get-tuple-element.23), channel_id=1, source_target_pairs={{0,1},{1,0},{2,3},{3,2},{4,5},{5,4},{6,7},{7,6},{8,9},{9,8},{10,11... | collective-permute-start | bytes 405512 | tf_op jit(solution)/shard_map/ppermute | solution.py:388
  44.7 2.7 %collective-permute-start.8 = (f32[2048,128]{1,0:T(8,128)S(1)}, f32[2048,128]{1,0:T(8,128)S(1)}, u32[]{:S(2)}, u32[]{:S(2)}) collective-permute-start(f32[2048,128]{1,0:T(8,128)S(1)} %sum_slots.1), channel_id=1, source_target_pairs={{0,8},{8,0},{1,9},{9,1},{2,10},{10,2},{3,11},{11,3},{4,12},{12,4},... | collective-permute-start | bytes 3145736 | tf_op jit(solution)/shard_map/ppermute | solution.py:397
